TPU v7x, 256 devices: a whole 4x4x8 slice. The times are simulated.
256 devices in a mesh: group: 8 (over z), dom: 32 (over y, x, core).
Axes of the slice: x: 4, y: 4, z: 8, core: 2. Of those that a mesh axis runs over, the one named last changes fastest.
Arguments:
- pressure_old: float32 [1048576], P(('group', 'dom')), may hold values from -6 to 6
- source_term: float32 [1048576], P(('group', 'dom')), may hold values from -36 to 36
- diagonal: float32 [1048576], P(('group', 'dom')), may hold values from 6.5 to 7.5
- face_coeffs: float32 [6, 1048576], P(None, ('group', 'dom')), may hold values from 0.1 to 0.9
- neighbours: int32 [6, 1048576], P(None, ('group', 'dom')), may hold values from 0 to 8191
- export_cells: int32 [4, 262144], P(None, ('group', 'dom')), may hold values from 0 to 4095
- fluid_velocity: float32 [3, 1048576], P(None, ('group', 'dom')), may hold values from -6 to 6
- parcel_velocity: float32 [3, 262144], P(None, ('group', 'dom')), may hold values from -6 to 6
- drag_rate: float32 [262144], P(('group', 'dom')), may hold values from 0.05 to 1
- parcel_owner: int32 [262144], P(('group', 'dom')), may hold values from 0 to 31, as said below
- parcel_cells: int32 [8, 262144], P(None, ('group', 'dom')), may hold values from 0 to 4095
- interp_weights: float32 [8, 262144], P(None, ('group', 'dom')), may hold values from 0 to 0.25
- grad_weights: float32 [3, 8, 262144], P(None, None, ('group', 'dom')), may hold values from -3 to 3
Outputs:
- pressure: float32 [1048576], P(('group', 'dom'))
- parcel_new: float32 [3, 262144], P(None, ('group', 'dom'))
- momentum_source: float32 [3, 1048576], P(None, ('group', 'dom'))
Inputs may be any that keep to these rules, and one draw needn't show every extreme that they name: `parcel_owner`: A parcel's cells lie in its own group; in every group one partition is named exactly 128 times by the parcels of each device of the group, and no partition is named more than 128 times by the parcels of one device. `neighbours`: values under 4096 are the device's own cells; 4096 + d * 1024 + f is entry f of the cells exported by the neighbour in direction d. `export_cells`: local cell indices; repeats may occur.
All inputs are finite; a program needn't handle non-finite values.
Results may differ from a plain program's by a relative error of at most 0.00002.
Values sent between devices are 32-bit elements; how exact they have to be, the bound alone decides.
No kernel may reach another device: no remote copies, remote signals or barrier semaphores. Data moves between devices by JAX's collectives and lax.ppermute only.
A program may use at most 192 MiB of HBM per device.

v0:
```python
import jax
import jax.numpy as jnp
from jax import lax
from jax.sharding import PartitionSpec as P

ITERS = 2


CENTRE = 7.0
HALF_WIDTH = 4.0
LOADING = 8.0


def with_halo(block, sides, width, periodic):
    for axis, dim in sides:
        count = lax.axis_size(axis)
        forward = [(i, i + 1) for i in range(count - 1)]
        if periodic:
            forward.append((count - 1, 0))
        backward = [(target, source) for source, target in forward]
        low = lax.ppermute(
            lax.slice_in_dim(block, block.shape[dim] - width, None, axis=dim), axis, forward
        )
        high = lax.ppermute(lax.slice_in_dim(block, 0, width, axis=dim), axis, backward)
        block = jnp.concatenate([low, block, high], axis=dim)
    return block


def apply_matrix(vector, diagonal, face_coeffs, neighbours, export_cells):
    exported = vector[export_cells]
    along_dom = with_halo(jnp.stack([exported[1], exported[0]]), (("dom", 0),), 1, True)
    along_group = with_halo(jnp.stack([exported[3], exported[2]]), (("group", 0),), 1, False)
    received = jnp.concatenate([along_dom[0], along_dom[3], along_group[0], along_group[3]])
    extended = jnp.concatenate([vector, received])
    linked = extended[neighbours]
    result = diagonal * vector
    for column in range(face_coeffs.shape[0]):
        result = result - face_coeffs[column] * linked[column]
    return result


def slot_places(parcel_owner, owners, capacity):
    onehot = (parcel_owner[:, None] == jnp.arange(owners, dtype=jnp.int32)[None, :]).astype(
        jnp.int32
    )
    slot_rank = jnp.sum(onehot * (jnp.cumsum(onehot, axis=0) - 1), axis=1)
    return parcel_owner * capacity + slot_rank


def drag_update(fluid_cells, weights, velocity, rates):
    fluid_at = jnp.sum(weights[None] * fluid_cells, axis=1)
    moved = velocity + rates[None] * (fluid_at - velocity)
    reaction = LOADING * weights[None] * (rates[None] * (velocity - fluid_at))[:, None, :]
    return (moved, reaction)


def per_device(
    pressure_old,
    source_term,
    diagonal,
    face_coeffs,
    neighbours,
    export_cells,
    fluid_velocity,
    parcel_velocity,
    drag_rate,
    parcel_owner,
    parcel_cells,
    interp_weights,
    grad_weights,
):
    cells_here = pressure_old.shape[0]
    points = parcel_cells.shape[0]
    parcels_here = parcel_owner.shape[0]

    def operate(vector):
        return apply_matrix(vector, diagonal, face_coeffs, neighbours, export_cells)

    sigma = CENTRE / HALF_WIDTH
    rho_now = 1.0 / sigma
    iterate = pressure_old
    residual = source_term - operate(pressure_old)
    direction = residual / CENTRE
    for iteration in range(ITERS):
        iterate = iterate + direction
        if iteration + 1 < ITERS:
            residual = residual - operate(direction)
            rho_next = 1.0 / (2.0 * sigma - rho_now)
            direction = rho_next * rho_now * direction + 2.0 * rho_next / HALF_WIDTH * residual
            rho_now = rho_next
    owners = lax.axis_size("dom")
    capacity = 4 * parcels_here // owners
    slot_index = slot_places(parcel_owner, owners, capacity)
    packed = jnp.concatenate(
        [
            interp_weights,
            grad_weights.reshape(3 * points, parcels_here),
            parcel_velocity,
            drag_rate[None],
        ],
        axis=0,
    )
    fields_count = packed.shape[0]
    float_slots = (
        jnp.zeros((fields_count, owners * capacity), jnp.float32).at[:, slot_index].set(packed)
    )
    index_slots = (
        jnp.zeros((points, owners * capacity), jnp.int32).at[:, slot_index].set(parcel_cells)
    )
    got_floats, got_cells = (
        lax.all_to_all(
            float_slots.reshape(fields_count, owners, capacity),
            "dom",
            split_axis=1,
            concat_axis=1,
            tiled=True,
        ),
        lax.all_to_all(
            index_slots.reshape(points, owners, capacity),
            "dom",
            split_axis=1,
            concat_axis=1,
            tiled=True,
        ),
    )
    got_floats = got_floats.reshape(fields_count, -1)
    got_cells = got_cells.reshape(points, -1)
    weights = got_floats[:points]
    gradients = got_floats[points : 4 * points].reshape(3, points, -1)
    velocity = got_floats[4 * points : 4 * points + 3]
    rates = got_floats[4 * points + 3]
    table = jnp.concatenate([fluid_velocity, iterate[None]], axis=0)
    looked = table[:, got_cells]
    moved, reaction = drag_update(looked[:3], weights, velocity, rates)
    updated = moved - jnp.sum(gradients * looked[3][None], axis=1)
    momentum_source = jnp.zeros((3, cells_here), jnp.float32).at[:, got_cells].add(reaction)
    returned = lax.all_to_all(
        updated.reshape(3, owners, capacity), "dom", split_axis=1, concat_axis=1, tiled=True
    ).reshape(3, -1)
    parcel_new = returned[:, slot_index]
    return (iterate, parcel_new, momentum_source)


def solution(mesh):
    return jax.shard_map(
        per_device,
        mesh=mesh,
        in_specs=(
            P(("group", "dom")),
            P(("group", "dom")),
            P(("group", "dom")),
            P(None, ("group", "dom")),
            P(None, ("group", "dom")),
            P(None, ("group", "dom")),
            P(None, ("group", "dom")),
            P(None, ("group", "dom")),
            P(("group", "dom")),
            P(("group", "dom")),
            P(None, ("group", "dom")),
            P(None, ("group", "dom")),
            P(None, None, ("group", "dom")),
        ),
        out_specs=(P(("group", "dom")), P(None, ("group", "dom")), P(None, ("group", "dom"))),
        check_vma=False,
    )
```

profile of v0, /device:TPU:1, one launch (start us, length us, event | category | flops | bytes accessed | tf_op | source)
XLA Modules:
  0.0 724.4 jit_solution(1465310412388931592)
XLA Ops:
  0.6 0.7 fusion.14
  1.4 0.0 copy-start.7
  1.4 0.0 copy-start.8
  1.4 23.0 %gather_fusion = f32[4096]{0:T(1024)S(1)} fusion(f32[4096]{0:T(1024)S(1)} %copy-done, s32[4096]{0:T(1024)S(1)} %bitcast_clamp_fusion), kind=kCustom, calls=%fused_computation | custom fusion | bytes 49152 | tf_op jit(solution)/shard_map/gather | solution.py:30
  24.5 2.7 collective-permute-start
  27.1 0.7 collective-permute-start.1
  27.9 2.8 collective-permute-start.2
  30.7 1.3 collective-permute-start.3
  32.0 9.0 %reduce-window.6 = s32[32,8,128]{2,1,0:T(8,128)S(1)} reduce-window(s32[32,8,128]{2,1,0:T(8,128)S(1)} %fusion.10, s32[]{:T(128)} %constant.10.clone.1), window={size=1x1x128 pad=0_0x0_0x127_0}, to_apply=%region_0.0 | reduce-window | flops 4161536 | bytes 262148 | tf_op jit(solution)/shard_map/reduce-window
  41.0 0.1 slice.201
  41.1 0.1 copy.55
  41.3 0.1 copy.56
  41.4 0.1 add_add_fusion
  41.6 0.2 copy.61
  41.8 0.0 copy-start.2
  41.8 3.6 scatter_custom_fusion.1
  45.4 0.0 copy-start.3
  45.4 0.0 copy-start.9
  45.4 0.0 copy-start.10
  45.4 0.0 copy-start.12
  45.4 1.2 copy.62
  46.6 8.0 %all-to-all-start.1 = ((s32[8,32,128]{2,0,1:T(8,128)}), s32[8,32,128]{2,0,1:T(8,128)S(1)}, u32[]{:S(2)}, u32[]{:S(2)}) async-start(s32[8,32,128]{2,0,1:T(8,128)} %copy.62), calls=%async_computation.1 | async-start | bytes 262144 | tf_op jit(solution)/shard_map/all_to_all | solution.py:118
  54.7 0.1 reshape.144
  54.9 0.2 copy.57
  55.1 3.6 scatter_custom_fusion
  58.7 1.5 copy.58
  60.2 0.0 collective-permute-done
  60.2 0.0 collective-permute-done.1
  60.2 0.0 collective-permute-done.2
  60.2 0.0 copy-start.1
  60.2 0.0 copy-start.6
  60.2 0.0 copy-start.11
  60.3 135.5 %gather_fusion.1 = f32[24576]{0:T(1024)S(1)} fusion(f32[8192]{0:T(1024)S(1)} %constant_dynamic-update-slice_fusion, s32[24576]{0:T(1024)S(1)} %broadcast_clamp_fusion.1), kind=kCustom, calls=%fused_computation.1 | custom fusion | bytes 294912 | tf_op jit(solution)/shard_map/gather | solution.py:35
  195.8 0.1 slice_multiply_fusion.12
  196.0 23.0 %gather_fusion.2 = f32[4096]{0:T(1024)S(1)} fusion(f32[4096]{0:T(1024)S(1)} %get-tuple-element.17, s32[4096]{0:T(1024)S(1)} %bitcast_clamp_fusion), kind=kCustom, calls=%fused_computation.2 | custom fusion | bytes 49152 | tf_op jit(solution)/shard_map/gather | solution.py:30
  219.0 1.7 collective-permute-start.4
  220.8 4.3 collective-permute-start.6
  225.0 1.3 collective-permute-start.7
  226.3 0.0 collective-permute-done.4
  226.3 0.0 collective-permute-done.5
  226.4 0.0 collective-permute-done.6
  226.4 3.2 collective-permute-done.7
  229.6 135.5 %gather_fusion.3 = f32[24576]{0:T(1024)S(1)} fusion(f32[8192]{0:T(1024)S(1)} %constant_dynamic-update-slice_fusion.1, s32[24576]{0:T(1024)S(1)} %broadcast_clamp_fusion.1), kind=kCustom, calls=%fused_computation.3 | custom fusion | bytes 294912 | tf_op jit(solution)/shard_map/gather | solution.py:35
  365.1 0.1 slice_multiply_fusion.11
  365.3 0.0 copy-start.4
  365.3 0.6 copy.63
  366.0 0.0 all-to-all-done.1
  366.0 8.7 %all-to-all-start = ((f32[36,32,128]{2,0,1:T(8,128)}), f32[36,32,128]{2,0,1:T(8,128)S(1)}, u32[]{:S(2)}, u32[]{:S(2)}) async-start(f32[36,32,128]{2,0,1:T(8,128)} %copy.58), calls=%async_computation | async-start | bytes 1310720 | tf_op jit(solution)/shard_map/all_to_all | solution.py:111
  374.9 108.4 %gather_fusion.4 = f32[32768,4]{1,0:T(8,128)} fusion(f32[4,4096]{0,1:T(8,128)S(1)} %copy.63, s32[32768]{0:T(1024)S(1)} %broadcast_clamp_fusion), kind=kCustom, calls=%fused_computation.4 | custom fusion | bytes 1179648 | tf_op jit(solution)/shard_map/gather | solution.py:133
  483.3 9.8 %copy.64 = f32[8,4096,4]{1,0,2:T(8,128)S(1)} copy(f32[8,4096,4]{2,1,0:T(8,128)} %bitcast.107) | data formatting | bytes 1048576 | tf_op jit(solution)/shard_map/gather | solution.py:133
  493.1 0.1 copy.65
  493.2 0.1 reshape.132
  493.3 0.1 fusion.6
  493.4 0.1 multiply_reduce_fusion
  493.6 0.7 copy.66
  494.3 7.4 %all-to-all-start.2 = ((f32[3,32,128]{2,0,1:T(4,128)}), f32[3,32,128]{2,0,1:T(4,128)S(1)}, u32[]{:S(2)}, u32[]{:S(2)}) async-start(f32[3,32,128]{2,0,1:T(4,128)} %copy.66), calls=%async_computation.2 | async-start | bytes 131072 | tf_op jit(solution)/shard_map/all_to_all | solution.py:137
  501.7 0.6 copy.68
  502.4 6.3 broadcast_multiply_fusion
  508.7 210.2 %scatter_custom_fusion.2 = f32[3,4096]{0,1:T(8,128)S(1)} fusion(s32[32768]{0:T(1024)S(1)} %bitcast.117, f32[32768,3]{1,0:T(8,128)} %bitcast.108, f32[]{:T(128)} %constant.16.clone.1), kind=kCustom, calls=%fused_computation.10 | custom fusion | flops 98304 | bytes 49664 | tf_op jit(solution)/shard_map/scatter-add | solution.py:136
  718.9 1.2 copy.70
  720.2 0.0 all-to-all-done.2
  720.2 0.6 copy.67
  720.8 2.8 gather_fusion.5
  723.6 0.8 copy.69
  (55 shorter events, 0.5 us)
Async XLA Ops:
  0.6 0.7 copy-start
  1.4 30.6 %copy-start.7 = (s32[1024]{0:T(1024)S(1)}, s32[1024]{0:T(1024)}, u32[]{:S(2)}) copy-start(s32[1024]{0:T(1024)} %param.22) | copy-start | bytes 12292
  1.4 40.1 %copy-start.8 = (s32[8,1024]{1,0:T(8,128)S(1)}, s32[8,1024]{1,0:T(8,128)}, u32[]{:S(2)}) copy-start(s32[8,1024]{1,0:T(8,128)} %param.23) | copy-start | bytes 98308
  24.5 35.7 %collective-permute-start = (f32[1,1024]{1,0:T(1,128)S(1)}, f32[1,1024]{1,0:T(1,128)S(1)}, u32[]{:S(2)}, u32[]{:S(2)}) collective-permute-start(f32[1,1024]{1,0:T(1,128)S(1)} %bitcast.163), channel_id=1, source_target_pairs={{0,1},{1,2},{2,3},{3,4},{4,5},{5,6},{6,7},{7,8},{8,9},{9,10},{10,1... | collective-permute-start | bytes 12296 | tf_op jit(solution)/shard_map/ppermute | solution.py:21
  27.1 33.0 %collective-permute-start.1 = (f32[1,1024]{1,0:T(1,128)S(1)}, f32[1,1024]{1,0:T(1,128)S(1)}, u32[]{:S(2)}, u32[]{:S(2)}) collective-permute-start(f32[1,1024]{1,0:T(1,128)S(1)} %bitcast.162), channel_id=1, source_target_pairs={{1,0},{2,1},{3,2},{4,3},{5,4},{6,5},{7,6},{8,7},{9,8},{10,9},{11,1... | collective-permute-start | bytes 12296 | tf_op jit(solution)/shard_map/ppermute | solution.py:24
  27.9 32.3 %collective-permute-start.2 = (f32[1,1024]{1,0:T(1,128)S(1)}, f32[1,1024]{1,0:T(1,128)S(1)}, u32[]{:S(2)}, u32[]{:S(2)}) collective-permute-start(f32[1,1024]{1,0:T(1,128)S(1)} %bitcast.161), channel_id=1, source_target_pairs={{0,32},{32,64},{64,96},{96,128},{128,160},{160,192},{192,224},{1,3... | collective-permute-start | bytes 12296 | tf_op jit(solution)/shard_map/ppermute | solution.py:21
  30.7 29.5 %collective-permute-start.3 = (f32[1,1024]{1,0:T(1,128)S(1)}, f32[1,1024]{1,0:T(1,128)S(1)}, u32[]{:S(2)}, u32[]{:S(2)}) collective-permute-start(f32[1,1024]{1,0:T(1,128)S(1)} %bitcast.160), channel_id=1, source_target_pairs={{32,0},{64,32},{96,64},{128,96},{160,128},{192,160},{224,192},{33,... | collective-permute-start | bytes 12296 | tf_op jit(solution)/shard_map/ppermute | solution.py:24
  41.8 12.9 %copy-start.2 = (s32[6,4096]{1,0:T(8,128)S(1)}, s32[6,4096]{1,0:T(8,128)}, u32[]{:S(2)}) copy-start(s32[6,4096]{1,0:T(8,128)} %param.17) | copy-start | bytes 294916
  45.4 9.4 %copy-start.3 = (f32[3,8,1024]{2,1,0:T(8,128)S(1)}, f32[3,8,1024]{2,1,0:T(8,128)}, u32[]{:S(2)}) copy-start(f32[3,8,1024]{2,1,0:T(8,128)} %param.25) | copy-start | bytes 294916
  45.4 9.4 %copy-start.9 = (f32[8,1024]{1,0:T(8,128)S(1)}, f32[8,1024]{1,0:T(8,128)}, u32[]{:S(2)}) copy-start(f32[8,1024]{1,0:T(8,128)} %param.24) | copy-start | bytes 98308
  45.4 9.4 %copy-start.10 = (f32[3,1024]{1,0:T(4,128)S(1)}, f32[3,1024]{1,0:T(4,128)}, u32[]{:S(2)}) copy-start(f32[3,1024]{1,0:T(4,128)} %param.20) | copy-start | bytes 36868
  45.4 9.4 %copy-start.12 = (f32[1024]{0:T(1024)S(1)}, f32[1024]{0:T(1024)}, u32[]{:S(2)}) copy-start(f32[1024]{0:T(1024)} %param.21) | copy-start | bytes 12292
  46.6 319.3 %all-to-all-start.1 = ((s32[8,32,128]{2,0,1:T(8,128)}), s32[8,32,128]{2,0,1:T(8,128)S(1)}, u32[]{:S(2)}, u32[]{:S(2)}) async-start(s32[8,32,128]{2,0,1:T(8,128)} %copy.62), calls=%async_computation.1 | async-start | bytes 262144 | tf_op jit(solution)/shard_map/all_to_all | solution.py:118
  60.2 135.6 %copy-start.1 = (f32[6,4096]{1,0:T(8,128)S(1)}, f32[6,4096]{1,0:T(8,128)}, u32[]{:S(2)}) copy-start(f32[6,4096]{1,0:T(8,128)} %param.16) | copy-start | bytes 294916
  60.2 135.7 %copy-start.6 = (f32[4096]{0:T(1024)S(1)}, f32[4096]{0:T(1024)}, u32[]{:S(2)}) copy-start(f32[4096]{0:T(1024)} %param.15) | copy-start | bytes 49156
  60.2 135.7 %copy-start.11 = (f32[4096]{0:T(1024)S(1)}, f32[4096]{0:T(1024)}, u32[]{:S(2)}) copy-start(f32[4096]{0:T(1024)} %param.14) | copy-start | bytes 49156
  219.0 7.3 %collective-permute-start.4 = (f32[1,1024]{1,0:T(1,128)S(1)}, f32[1,1024]{1,0:T(1,128)S(1)}, u32[]{:S(2)}, u32[]{:S(2)}) collective-permute-start(f32[1,1024]{1,0:T(1,128)S(1)} %bitcast.167), channel_id=1, source_target_pairs={{0,1},{1,2},{2,3},{3,4},{4,5},{5,6},{6,7},{7,8},{8,9},{9,10},{10,1... | collective-permute-start | bytes 12296 | tf_op jit(solution)/shard_map/ppermute | solution.py:21
  220.8 5.6 collective-permute-start.5
  220.8 5.6 collective-permute-start.6
  225.0 4.5 collective-permute-start.7
  229.6 135.7 %copy-start.5 = (f32[3,4096]{1,0:T(4,128)S(1)}, f32[3,4096]{1,0:T(4,128)}, u32[]{:S(2)}) copy-start(f32[3,4096]{1,0:T(4,128)} %param.19) | copy-start | bytes 147460
  365.3 9.6 %copy-start.4 = (f32[4096]{0:T(1024)}, f32[4096]{0:T(1024)S(1)}, u32[]{:S(2)}) copy-start(f32[4096]{0:T(1024)S(1)} %add_add_fusion.1) | copy-start | bytes 49156
  366.0 127.1 %all-to-all-start = ((f32[36,32,128]{2,0,1:T(8,128)}), f32[36,32,128]{2,0,1:T(8,128)S(1)}, u32[]{:S(2)}, u32[]{:S(2)}) async-start(f32[36,32,128]{2,0,1:T(8,128)} %copy.58), calls=%async_computation | async-start | bytes 1310720 | tf_op jit(solution)/shard_map/all_to_all | solution.py:111
  494.3 225.9 %all-to-all-start.2 = ((f32[3,32,128]{2,0,1:T(4,128)}), f32[3,32,128]{2,0,1:T(4,128)S(1)}, u32[]{:S(2)}, u32[]{:S(2)}) async-start(f32[3,32,128]{2,0,1:T(4,128)} %copy.66), calls=%async_computation.2 | async-start | bytes 131072 | tf_op jit(solution)/shard_map/all_to_all | solution.py:137
where the time goes:
time: 728 us; the launch traced here: 724 us
  local copies, waits for them, and re-layouts  454 us (62%)
  other arithmetic  227 us (31%)
  starting transfers between devices  38.9 us (5%)
    gather x2, local copies, waits for them, and re-layouts, apply_matrix(): linked = extended[neighbours]  271 us
    scatter-add x1, other arithmetic, per_device(): jnp.zeros((3, cells_here), jnp.float32).at[:, got_cells].add(reaction)  210 us
    gather x2, local copies, waits for them, and re-layouts, per_device(): looked = table[:, got_cells]  118 us
    gather x2, local copies, waits for them, and re-layouts, apply_matrix(): exported = vector[export_cells]  46.1 us
  transfers between devices with their start and end apart: 11, of which 1 were waited for; matrix products, arithmetic and copies ran while one was open for 90% of the time, Pallas kernels for 0%

commit v1 on v0

v1 whole, which is shorter than its diff:
```python
import jax
import jax.numpy as jnp
from jax import lax
from jax.experimental import pallas as pl
from jax.experimental.pallas import tpu as pltpu
from jax.sharding import PartitionSpec as P

CENTRE = 7.0
HALF_WIDTH = 4.0
LOADING = 8.0
SIGMA = CENTRE / HALF_WIDTH
RHO_FIRST = 1.0 / SIGMA
RHO_NEXT = 1.0 / (2.0 * SIGMA - RHO_FIRST)

CELLS = 4096
LANES = 128
ROWS = CELLS // LANES
FACE = 1024
FACE_ROWS = FACE // LANES
NBR = 6
K = 8
PARCELS = 1024
CHUNKS = PARCELS // LANES
OWNERS = 32
CAP = 128
SENT = 48

F32 = jnp.float32
BF16 = jnp.bfloat16
I32 = jnp.int32


def pick(row, lanes):
    return jnp.take_along_axis(row, lanes, axis=1, mode="promise_in_bounds")


def wide(row, height):
    return jnp.broadcast_to(row, (height, LANES))


def look_up(tables, index):
    height = index.shape[0]
    high = lax.shift_right_logical(index, 7)
    low = lax.bitwise_and(index, 127)
    found = [jnp.zeros((height, LANES), F32) for _ in tables]
    for r in range(len(tables[0])):
        here = high == r
        for c, table in enumerate(tables):
            found[c] = jnp.where(here, pick(wide(table[r](), height), low), found[c])
    return found


def rows_of(ref, count):
    return [lambda r=r: ref[r : r + 1, :] for r in range(count)]


def write_exports(field_ref, export_ref, outs):
    for t in range(FACE_ROWS):
        index = export_ref[:, t * LANES : (t + 1) * LANES]
        (found,) = look_up([rows_of(field_ref, ROWS)], index)
        for d in range(4):
            outs[d][t : t + 1, :] = found[d : d + 1, :]


def export_kernel(field_ref, export_ref, *outs):
    write_exports(field_ref, export_ref, outs)


def multiply(vector_ref, got_refs, diagonal_ref, coeff_ref, neighbour_ref, halo_ref, out_ref):
    group = lax.axis_index("group")
    last = lax.axis_size("group") - 1
    for d in range(4):
        value = got_refs[d][...]
        if d == 2:
            value = jnp.where(group > 0, value, 0.0)
        if d == 3:
            value = jnp.where(group < last, value, 0.0)
        halo_ref[d * FACE_ROWS : (d + 1) * FACE_ROWS, :] = value
    table = rows_of(vector_ref, ROWS) + rows_of(halo_ref, 4 * FACE_ROWS)
    for t in range(ROWS):
        cut = slice(t * LANES, (t + 1) * LANES)
        (found,) = look_up([table], neighbour_ref[:, cut])
        linked = jnp.sum(coeff_ref[:, cut] * found, axis=0, keepdims=True)
        out_ref[t : t + 1, :] = diagonal_ref[t : t + 1, :] * vector_ref[t : t + 1, :] - linked


def first_kernel(
    pressure_ref, got0, got1, got2, got3, source_ref, diagonal_ref, coeff_ref, neighbour_ref,
    export_ref, residual_ref, direction_ref, out0, out1, out2, out3, halo_ref, product_ref,
):
    multiply(
        pressure_ref, (got0, got1, got2, got3), diagonal_ref, coeff_ref, neighbour_ref,
        halo_ref, product_ref,
    )
    residual = source_ref[...] - product_ref[...]
    residual_ref[...] = residual
    direction_ref[...] = residual / CENTRE
    write_exports(direction_ref, export_ref, (out0, out1, out2, out3))


def second_kernel(
    direction_ref, got0, got1, got2, got3, pressure_ref, residual_ref, diagonal_ref, coeff_ref,
    neighbour_ref, parcel_ref, moved_ref, out_ref, updated_ref, halo_ref, product_ref,
):
    multiply(
        direction_ref, (got0, got1, got2, got3), diagonal_ref, coeff_ref, neighbour_ref,
        halo_ref, product_ref,
    )
    direction = direction_ref[...]
    residual = residual_ref[...] - product_ref[...]
    iterate = pressure_ref[...] + direction
    direction = RHO_NEXT * RHO_FIRST * direction + (2.0 * RHO_NEXT / HALF_WIDTH) * residual
    out_ref[...] = iterate + direction
    table = rows_of(out_ref, ROWS)
    for s in range(OWNERS):
        (found,) = look_up([table], parcel_ref[s, 8:16, :].astype(I32))
        for c in range(3):
            weights = parcel_ref[s, 16 + 8 * c : 24 + 8 * c, :]
            gradient = jnp.sum(weights * found, axis=0, keepdims=True)
            updated_ref[s, c : c + 1, :] = moved_ref[s, c : c + 1, :] - gradient
        updated_ref[s, 3:4, :] = jnp.zeros((1, LANES), F32)


def slot_kernel(owner_ref, cells_ref, weight_ref, grad_ref, velocity_ref, rate_ref, place_ref, sent_ref):
    owners = lax.broadcasted_iota(I32, (OWNERS, LANES), 0)
    lanes = lax.broadcasted_iota(I32, (OWNERS, LANES), 1)
    chosen = [owners == wide(owner_ref[j : j + 1, :], OWNERS) for j in range(CHUNKS)]
    stacked = jnp.concatenate([c.astype(F32).astype(BF16) for c in chosen], axis=0)
    row = lax.broadcasted_iota(I32, (LANES, 2 * LANES), 0)
    column = lax.broadcasted_iota(I32, (LANES, 2 * LANES), 1)
    before = ((row < column) | (column >= LANES)).astype(F32).astype(BF16)
    counts = jnp.dot(stacked, before, preferred_element_type=F32)
    carried = jnp.zeros((OWNERS, LANES), F32)
    ranks = []
    for j in range(CHUNKS):
        part = counts[j * OWNERS : (j + 1) * OWNERS]
        rank = jnp.where(chosen[j], part[:, :LANES] + carried, 0.0)
        ranks.append(jnp.sum(rank, axis=0, keepdims=True))
        carried = carried + part[:, LANES:]
        place_ref[j : j + 1, :] = owner_ref[j : j + 1, :] * CAP + ranks[j].astype(I32)
    slots = lax.broadcasted_iota(I32, (CAP, LANES), 0).astype(F32)
    at_rank = jnp.concatenate(
        [(slots == wide(ranks[j], CAP)).astype(F32).astype(BF16) for j in range(CHUNKS)], axis=1
    )
    lane_of = jnp.concatenate(
        [jnp.where(c, lanes.astype(F32), 0.0).astype(BF16) for c in chosen], axis=1
    )
    chunk_of = jnp.concatenate(
        [jnp.where(c, F32(j + 1), 0.0).astype(BF16) for j, c in enumerate(chosen)], axis=1
    )
    found = lax.dot_general(
        jnp.concatenate([lane_of, chunk_of], axis=0), at_rank, (((1,), (1,)), ((), ())),
        preferred_element_type=F32,
    ).astype(I32)
    for o in range(OWNERS):
        low = wide(found[o : o + 1], 8)
        high = wide(found[OWNERS + o : OWNERS + o + 1], 8)
        here = [high == j + 1 for j in range(CHUNKS)]

        def place(group, ref, height=8):
            value = jnp.zeros((height, LANES), F32)
            for j in range(CHUNKS):
                cut = slice(j * LANES, (j + 1) * LANES)
                part = ref[:, cut] if group is None else ref[group, :, cut]
                value = jnp.where(here[j][:height], pick(part.astype(F32), low[:height]), value)
            return value

        sent_ref[o, 0:8, :] = place(None, weight_ref)
        sent_ref[o, 8:16, :] = place(None, cells_ref)
        for c in range(3):
            sent_ref[o, 16 + 8 * c : 24 + 8 * c, :] = place(c, grad_ref)
        sent_ref[o, 40:43, :] = place(None, velocity_ref, 3)
        value = jnp.zeros((8, LANES), F32)
        for j in range(CHUNKS):
            value = jnp.where(here[j], pick(wide(rate_ref[j : j + 1, :], 8), low), value)
        sent_ref[o, 43:44, :] = value[:1]
        sent_ref[o, 44:48, :] = jnp.zeros((4, LANES), F32)


def fluid_kernel(fluid_ref, parcel_ref, moved_ref, force_ref):
    tables = [
        [lambda c=c, r=r: fluid_ref[c : c + 1, r * LANES : (r + 1) * LANES] for r in range(ROWS)]
        for c in range(3)
    ]
    for s in range(OWNERS):
        found = look_up(tables, parcel_ref[s, 8:16, :].astype(I32))
        weights = parcel_ref[s, 0:8, :]
        rate = parcel_ref[s, 43:44, :]
        for c in range(3):
            velocity = parcel_ref[s, 40 + c : 41 + c, :]
            fluid_at = jnp.sum(weights * found[c], axis=0, keepdims=True)
            moved_ref[s, c : c + 1, :] = velocity + rate * (fluid_at - velocity)
            force_ref[s, c : c + 1, :] = rate * (velocity - fluid_at)
        moved_ref[s, 3:4, :] = jnp.zeros((1, LANES), F32)
        force_ref[s, 3:4, :] = jnp.zeros((1, LANES), F32)


def scatter_kernel(parcel_ref, force_ref, out_ref, total_ref):
    rows = lax.broadcasted_iota(I32, (ROWS, LANES), 0)
    columns = lax.broadcasted_iota(I32, (LANES, LANES), 0)
    total_ref[...] = jnp.zeros_like(total_ref)

    def step(s, carry):
        cells = parcel_ref[s, 8:16, :].astype(I32)
        high = lax.shift_right_logical(cells, 7)
        low = lax.bitwise_and(cells, 127)
        weights = LOADING * parcel_ref[s, 0:8, :]
        parts = []
        for c in range(3):
            value = weights * force_ref[s, c : c + 1, :]
            top = value.astype(BF16)
            parts.append(top.astype(F32))
            parts.append((value - top.astype(F32)).astype(BF16).astype(F32))
        left, right = [], []
        for k in range(K):
            here = rows == wide(high[k : k + 1], ROWS)
            left.append(
                jnp.concatenate(
                    [jnp.where(here, wide(p[k : k + 1], ROWS), 0.0).astype(BF16) for p in parts],
                    axis=0,
                )
            )
            right.append((columns == wide(low[k : k + 1], LANES)).astype(F32).astype(BF16))
        total_ref[...] += lax.dot_general(
            jnp.concatenate(left, axis=1), jnp.concatenate(right, axis=1),
            (((1,), (1,)), ((), ())), preferred_element_type=F32,
        )
        return carry

    lax.fori_loop(0, OWNERS, step, 0)
    for c in range(3):
        both = (
            total_ref[2 * c * ROWS : (2 * c + 1) * ROWS, :]
            + total_ref[(2 * c + 1) * ROWS : (2 * c + 2) * ROWS, :]
        )
        for r in range(ROWS):
            out_ref[c : c + 1, r * LANES : (r + 1) * LANES] = both[r : r + 1]


def return_kernel(place_ref, updated_ref, out_ref):
    tables = [[lambda c=c, o=o: updated_ref[o, c : c + 1, :] for o in range(OWNERS)] for c in range(3)]
    found = look_up(tables, place_ref[...])
    for c in range(3):
        for j in range(CHUNKS):
            out_ref[c : c + 1, j * LANES : (j + 1) * LANES] = found[c][j : j + 1]


def shape(*dims, dtype=F32):
    return jax.ShapeDtypeStruct(dims, dtype)


def exchange(faces):
    count, groups = lax.axis_size("dom"), lax.axis_size("group")
    up = [(i, (i + 1) % count) for i in range(count)]
    over = [(i, (i + 1) % groups) for i in range(groups)]
    down = [(b, a) for a, b in up]
    under = [(b, a) for a, b in over]
    return (
        lax.ppermute(faces[0], "dom", up),
        lax.ppermute(faces[1], "dom", down),
        lax.ppermute(faces[2], "group", over),
        lax.ppermute(faces[3], "group", under),
    )


def call(kernel, outs, flops, scratch=()):
    return pl.pallas_call(
        kernel,
        out_shape=outs,
        scratch_shapes=list(scratch),
        compiler_params=pltpu.CompilerParams(vmem_limit_bytes=32 * 1024 * 1024),
        cost_estimate=pl.CostEstimate(flops=flops, bytes_accessed=400000, transcendentals=0),
    )


def per_device(
    pressure_old, source_term, diagonal, face_coeffs, neighbours, export_cells, fluid_velocity,
    parcel_velocity, drag_rate, parcel_owner, parcel_cells, interp_weights, grad_weights,
):
    pressure_old = pressure_old.reshape(ROWS, LANES)
    source_term = source_term.reshape(ROWS, LANES)
    diagonal = diagonal.reshape(ROWS, LANES)
    face = shape(FACE_ROWS, LANES)
    field = shape(ROWS, LANES)
    halo = (pltpu.VMEM((4 * FACE_ROWS, LANES), F32), pltpu.VMEM((ROWS, LANES), F32))

    faces = call(export_kernel, (face,) * 4, 10**6)(pressure_old, export_cells)
    place, sent = call(
        slot_kernel, (shape(CHUNKS, LANES, dtype=I32), shape(OWNERS, SENT, CAP)), 10**8
    )(
        parcel_owner.reshape(CHUNKS, LANES), parcel_cells, interp_weights, grad_weights,
        parcel_velocity, drag_rate.reshape(CHUNKS, LANES),
    )
    parcels = lax.all_to_all(sent, "dom", split_axis=0, concat_axis=0, tiled=True)
    got = exchange(faces)
    residual, direction, *faces = call(first_kernel, (field, field) + (face,) * 4, 10**8, halo)(
        pressure_old, *got, source_term, diagonal, face_coeffs, neighbours, export_cells
    )
    got = exchange(faces)
    moved, force = call(fluid_kernel, (shape(OWNERS, 4, CAP),) * 2, 10**9)(fluid_velocity, parcels)
    iterate, updated = call(second_kernel, (field, shape(OWNERS, 4, CAP)), 10**8, halo)(
        direction, *got, pressure_old, residual, diagonal, face_coeffs, neighbours, parcels, moved
    )
    returned = lax.all_to_all(updated, "dom", split_axis=0, concat_axis=0, tiled=True)
    momentum_source = call(
        scatter_kernel, shape(3, CELLS), 2 * 10**9, (pltpu.VMEM((6 * ROWS, LANES), F32),)
    )(parcels, force)
    parcel_new = call(return_kernel, shape(3, PARCELS), 10**6)(place, returned)
    return (iterate.reshape(CELLS), parcel_new, momentum_source)


def solution(mesh):
    whole = ("group", "dom")
    flat, rows = P(whole), P(None, whole)
    return jax.shard_map(
        per_device,
        mesh=mesh,
        in_specs=(
            flat, flat, flat, rows, rows, rows, rows, rows, flat, flat, rows, rows,
            P(None, None, whole),
        ),
        out_specs=(flat, rows, rows),
        check_vma=False,
    )
```

time: 728 us -> 67.2 us (0.09)
  local copies, waits for them, and re-layouts: 454 us -> 4.52 us
  other arithmetic: 227 us -> 0 us
  Pallas kernels: 0 us -> 24.3 us
    gather x7 -> x0, local copies, waits for them, and re-layouts: 438 us -> none  [the longest x2 271 us: apply_matrix(): linked = extended[neighbours]]
    scatter-add x1 -> x0, other arithmetic: 210 us -> none  [per_device(): jnp.zeros((3, cells_here), jnp.float32).at[:, got_cells].add(reaction)]
    pallas_call x0 -> x7, Pallas kernels: none -> 24.3 us  [the longest x1 9.47 us: per_device(): call(scatter_kernel, shape(3, CELLS), 2 * 10 ** 9, (pltpu.VMEM((6 * ROWS,...]
    another operation x2 -> x0, other arithmetic: 9.04 us -> none
    all_to_all x3 -> x2, starting transfers between devices: 24.1 us -> 17.5 us  [the longest x1 8.74 us: per_device(): lax.all_to_all(updated, 'dom', split_axis=0, concat_axis=0, tiled=True)]
  transfers between devices with their start and end apart: 11 -> 10, of which waited for: 1 -> 2; matrix products, arithmetic and copies ran while one was open for 90% -> 0% of each run, Pallas kernels for 0% -> 24%
where the time goes in v1:
time: 67.2 us; the launch traced here: 66.7 us
  starting transfers between devices  33.5 us (50%)
  Pallas kernels  24.3 us (36%)
  local copies, waits for them, and re-layouts  4.52 us (7%)
  waiting for transfers between devices  3.51 us (5%)
  between operations  0.8 us (1%)
    pallas_call x1, Pallas kernels, per_device(): call(scatter_kernel, shape(3, CELLS), 2 * 10 ** 9, (pltpu.VMEM((6 * ROWS,...  9.47 us
    all_to_all x1, starting transfers between devices, per_device(): lax.all_to_all(updated, 'dom', split_axis=0, concat_axis=0, tiled=True)  8.74 us
    all_to_all x1, starting transfers between devices, per_device(): lax.all_to_all(sent, 'dom', split_axis=0, concat_axis=0, tiled=True)  8.73 us
    ppermute x2, starting transfers between devices, exchange(): lax.ppermute(faces[3], 'group', under)  7.88 us
    unnamed x26, local copies, waits for them, and re-layouts  4.52 us
    pallas_call x1, Pallas kernels, per_device(): call(second_kernel, (field, shape(OWNERS, 4, CAP)), 10 ** 8, halo)  4.2 us
    pallas_call x1, Pallas kernels, per_device(): call(fluid_kernel, (shape(OWNERS, 4, CAP),) * 2, 10 ** 9)  3.48 us
    pallas_call x1, Pallas kernels, per_device(): call(slot_kernel, (shape(CHUNKS, LANES, dtype=I32), shape(OWNERS, SENT, C...  3.34 us
  transfers between devices with their start and end apart: 10, of which 2 were waited for; matrix products, arithmetic and copies ran while one was open for 0% of the time, Pallas kernels for 24%

profile of v1, /device:TPU:1, one launch (start us, length us, event | category | flops | bytes accessed | tf_op | source)
XLA Modules:
  0.0 66.7 jit_solution(11119735772896012663)
XLA Ops:
  0.6 0.0 copy-start.5
  0.6 0.9 %copy-done.5 = f32[3,8,1024]{2,1,0:T(8,128)S(1)} copy-done((f32[3,8,1024]{2,1,0:T(8,128)S(1)}, f32[3,8,1024]{2,1,0:T(8,128)}, u32[]{:S(2)}) %copy-start.5) | copy-done | bytes 98328
  1.5 0.0 copy-start.7
  1.5 0.8 %copy-done.7 = s32[8,1024]{1,0:T(8,128)S(1)} copy-done((s32[8,1024]{1,0:T(8,128)S(1)}, s32[8,1024]{1,0:T(8,128)}, u32[]{:S(2)}) %copy-start.7) | copy-done | bytes 32792
  2.3 0.0 copy-start.8
  2.3 0.8 %copy-done.8 = f32[8,1024]{1,0:T(8,128)S(1)} copy-done((f32[8,1024]{1,0:T(8,128)S(1)}, f32[8,1024]{1,0:T(8,128)}, u32[]{:S(2)}) %copy-start.8) | copy-done | bytes 32792
  3.0 0.0 copy-start.9
  3.0 0.7 %copy-done.9 = f32[3,1024]{1,0:T(4,128)S(1)} copy-done((f32[3,1024]{1,0:T(4,128)S(1)}, f32[3,1024]{1,0:T(4,128)}, u32[]{:S(2)}) %copy-start.9) | copy-done | bytes 12312
  3.8 0.0 copy-start.11
  3.8 0.7 %copy-done.11 = s32[1024]{0:T(1024)S(1)} copy-done((s32[1024]{0:T(1024)S(1)}, s32[1024]{0:T(1024)}, u32[]{:S(2)}) %copy-start.11) | copy-done | bytes 4120
  4.4 0.0 copy-start.12
  4.5 0.7 %copy-done.12 = f32[1024]{0:T(1024)S(1)} copy-done((f32[1024]{0:T(1024)S(1)}, f32[1024]{0:T(1024)}, u32[]{:S(2)}) %copy-start.12) | copy-done | bytes 4120
  5.1 3.3 %shard_map.150 = (s32[8,128]{1,0:T(8,128)S(1)}, f32[32,48,128]{2,1,0:T(8,128)}) custom-call(s32[8,128]{1,0:T(8,128)S(1)} %bitcast.12, s32[8,1024]{1,0:T(8,128)S(1)} %copy-done.7, f32[8,1024]{1,0:T(8,128)S(1)} %copy-done.8, f32[3,8,1024]{2,1,0:T(8,128)S(1)} %copy-done.5, f32[3,1024]{1,0:T(4,128)S(1)} %copy-done.9, f32[8,128]{1,0:T(8,128)S(1)} %bitcast.13), custom_call_target="tpu_custom_call" | custom-call | flops 100000000 | bytes 400000 | tf_op jit(solution)/shard_map/pallas_call | solution.py:288
  8.5 0.0 copy-start.2
  8.5 0.0 copy-start.4
  8.5 0.0 copy-start
  8.5 0.0 copy-start.1
  8.5 8.7 %all-to-all-start = ((f32[32,48,128]{2,1,0:T(8,128)}), f32[32,48,128]{2,1,0:T(8,128)S(1)}, u32[]{:S(2)}, u32[]{:S(2)}) async-start(f32[32,48,128]{2,1,0:T(8,128)} %get-tuple-element.29), calls=%async_computation | async-start | bytes 1572864 | tf_op jit(solution)/shard_map/all_to_all | solution.py:294
  17.2 0.0 copy-done.2
  17.2 0.0 copy-done.4
  17.3 0.0 copy-start.3
  17.3 0.0 copy-start.10
  17.3 0.4 shard_map.148
  17.6 1.7 %collective-permute-start = (f32[8,128]{1,0:T(8,128)S(1)}, f32[8,128]{1,0:T(8,128)S(1)}, u32[]{:S(2)}, u32[]{:S(2)}) collective-permute-start(f32[8,128]{1,0:T(8,128)S(1)} %get-tuple-element.19), channel_id=1, source_target_pairs={{0,1},{1,2},{2,3},{3,4},{4,5},{5,6},{6,7},{7,8},{8,9},{9,10},{10,1... | collective-permute-start | bytes 12296 | tf_op jit(solution)/shard_map/ppermute | solution.py:259
  19.4 0.0 collective-permute-start.1
  19.4 1.6 %collective-permute-start.2 = (f32[8,128]{1,0:T(8,128)S(1)}, f32[8,128]{1,0:T(8,128)S(1)}, u32[]{:S(2)}, u32[]{:S(2)}) collective-permute-start(f32[8,128]{1,0:T(8,128)S(1)} %get-tuple-element.21), channel_id=1, source_target_pairs={{0,32},{32,64},{64,96},{96,128},{128,160},{160,192},{192,224},{224... | collective-permute-start | bytes 12296 | tf_op jit(solution)/shard_map/ppermute | solution.py:261
  21.0 3.9 %collective-permute-start.3 = (f32[8,128]{1,0:T(8,128)S(1)}, f32[8,128]{1,0:T(8,128)S(1)}, u32[]{:S(2)}, u32[]{:S(2)}) collective-permute-start(f32[8,128]{1,0:T(8,128)S(1)} %get-tuple-element.22), channel_id=1, source_target_pairs={{32,0},{64,32},{96,64},{128,96},{160,128},{192,160},{224,192},{0,2... | collective-permute-start | bytes 12296 | tf_op jit(solution)/shard_map/ppermute | solution.py:262
  24.9 1.1 %collective-permute-done.got0 = f32[8,128]{1,0:T(8,128)S(1)} collective-permute-done((f32[8,128]{1,0:T(8,128)S(1)}, f32[8,128]{1,0:T(8,128)S(1)}, u32[]{:S(2)}, u32[]{:S(2)}) %collective-permute-start) | collective-permute-done | bytes 4128 | tf_op jit(solution)/shard_map/ppermute | solution.py:259
  26.1 2.4 %collective-permute-done.1.got1 = f32[8,128]{1,0:T(8,128)S(1)} collective-permute-done((f32[8,128]{1,0:T(8,128)S(1)}, f32[8,128]{1,0:T(8,128)S(1)}, u32[]{:S(2)}, u32[]{:S(2)}) %collective-permute-start.1) | collective-permute-done | bytes 4128 | tf_op jit(solution)/shard_map/ppermute | solution.py:260
  28.4 0.0 collective-permute-done.2.got2
  28.4 0.0 collective-permute-done.3.got3
  28.4 0.0 copy-done
  28.4 0.0 copy-done.1
  28.4 0.0 copy-done.3
  28.5 0.0 copy-done.10
  28.5 0.0 copy-start.6
  28.5 2.7 %shard_map.149 = (f32[32,128]{1,0:T(8,128)S(1)}, f32[32,128]{1,0:T(8,128)S(1)}, f32[8,128]{1,0:T(8,128)S(1)}, f32[8,128]{1,0:T(8,128)S(1)}, f32[8,128]{1,0:T(8,128)S(1)}, /*index=5*/f32[8,128]{1,0:T(8,128)S(1)}) custom-call(f32[32,128]{1,0:T(8,128)S(1)} %bitcast.7, f32[8,128]{1,0:T(8,128)S(1)} %collective-permute-done.got0, ...), custom_call_target="tpu_custom_call" | custom-call | flops 100000000 | bytes 400000 | tf_op jit(solution)/shard_map/pallas_call | solution.py:296
  31.2 0.2 collective-permute-start.4
  31.4 3.0 %collective-permute-start.5 = (f32[8,128]{1,0:T(8,128)S(1)}, f32[8,128]{1,0:T(8,128)S(1)}, u32[]{:S(2)}, u32[]{:S(2)}) collective-permute-start(f32[8,128]{1,0:T(8,128)S(1)} %get-tuple-element.25), channel_id=1, source_target_pairs={{1,0},{2,1},{3,2},{4,3},{5,4},{6,5},{7,6},{8,7},{9,8},{10,9},{11,1... | collective-permute-start | bytes 12296 | tf_op jit(solution)/shard_map/ppermute | solution.py:260
  34.4 1.6 %collective-permute-start.6 = (f32[8,128]{1,0:T(8,128)S(1)}, f32[8,128]{1,0:T(8,128)S(1)}, u32[]{:S(2)}, u32[]{:S(2)}) collective-permute-start(f32[8,128]{1,0:T(8,128)S(1)} %get-tuple-element.26), channel_id=1, source_target_pairs={{0,32},{32,64},{64,96},{96,128},{128,160},{160,192},{192,224},{224... | collective-permute-start | bytes 12296 | tf_op jit(solution)/shard_map/ppermute | solution.py:261
  36.0 3.9 %collective-permute-start.7 = (f32[8,128]{1,0:T(8,128)S(1)}, f32[8,128]{1,0:T(8,128)S(1)}, u32[]{:S(2)}, u32[]{:S(2)}) collective-permute-start(f32[8,128]{1,0:T(8,128)S(1)} %get-tuple-element.27), channel_id=1, source_target_pairs={{32,0},{64,32},{96,64},{128,96},{160,128},{192,160},{224,192},{0,2... | collective-permute-start | bytes 12296 | tf_op jit(solution)/shard_map/ppermute | solution.py:262
  39.9 0.0 all-to-all-done.parcel_ref
  39.9 0.0 copy-done.6
  40.0 3.5 %shard_map.151 = (f32[32,4,128]{2,1,0:T(4,128)S(1)}, f32[32,4,128]{2,1,0:T(4,128)S(1)}) custom-call(f32[3,4096]{1,0:T(4,128)S(1)} %copy-done.6, f32[32,48,128]{2,1,0:T(8,128)S(1)} %all-to-all-done.parcel_ref), custom_call_target="tpu_custom_call" | custom-call | flops 1000000000 | bytes 400000 | tf_op jit(solution)/shard_map/pallas_call | solution.py:300
  43.4 0.0 collective-permute-done.4.got0
  43.5 0.0 collective-permute-done.5.got1
  43.5 0.0 collective-permute-done.6.got2
  43.5 0.0 collective-permute-done.7.got3
  43.5 4.2 %shard_map.152 = (f32[32,128]{1,0:T(8,128)}, f32[32,4,128]{2,1,0:T(4,128)}) custom-call(f32[32,128]{1,0:T(8,128)S(1)} %get-tuple-element.23.direction_ref, f32[8,128]{1,0:T(8,128)S(1)} %collective-permute-done.4.got0, f32[8,128]{1,0:T(8,128)S(1)} %collective-permute-done.5.got1, f32[8,128]{1,0:T(8,128)S(1)} %collective-permute-done.6.got2, ...), custom_call_target="tpu_custom_call" | custom-call | flops 100000000 | bytes 400000 | tf_op jit(solution)/shard_map/pallas_call | solution.py:301
  47.7 8.7 %all-to-all-start.1 = ((f32[32,4,128]{2,1,0:T(4,128)}), f32[32,4,128]{2,1,0:T(4,128)S(1)}, u32[]{:S(2)}, u32[]{:S(2)}) async-start(f32[32,4,128]{2,1,0:T(4,128)} %get-tuple-element.33), calls=%async_computation.1 | async-start | bytes 131072 | tf_op jit(solution)/shard_map/all_to_all | solution.py:304
  56.4 9.5 %shard_map.154 = f32[3,4096]{1,0:T(4,128)} custom-call(f32[32,48,128]{2,1,0:T(8,128)S(1)} %all-to-all-done.parcel_ref, f32[32,4,128]{2,1,0:T(4,128)S(1)} %get-tuple-element.34.force_ref), custom_call_target="tpu_custom_call" | custom-call | flops 2000000000 | bytes 400000 | tf_op jit(solution)/shard_map/pallas_call | solution.py:305
  65.9 0.0 all-to-all-done.1.updated_ref
  65.9 0.8 %shard_map.153 = f32[3,1024]{1,0:T(4,128)} custom-call(s32[8,128]{1,0:T(8,128)S(1)} %get-tuple-element.32.place_ref, f32[32,4,128]{2,1,0:T(4,128)S(1)} %all-to-all-done.1.updated_ref), custom_call_target="tpu_custom_call" | custom-call | flops 1000000 | bytes 400000 | tf_op jit(solution)/shard_map/pallas_call | solution.py:308
Async XLA Ops:
  0.6 0.9 %copy-start.5 = (f32[3,8,1024]{2,1,0:T(8,128)S(1)}, f32[3,8,1024]{2,1,0:T(8,128)}, u32[]{:S(2)}) copy-start(f32[3,8,1024]{2,1,0:T(8,128)} %grad_ref.1) | copy-start | bytes 294916
  1.5 0.8 %copy-start.7 = (s32[8,1024]{1,0:T(8,128)S(1)}, s32[8,1024]{1,0:T(8,128)}, u32[]{:S(2)}) copy-start(s32[8,1024]{1,0:T(8,128)} %cells_ref.1) | copy-start | bytes 98308
  2.3 0.8 %copy-start.8 = (f32[8,1024]{1,0:T(8,128)S(1)}, f32[8,1024]{1,0:T(8,128)}, u32[]{:S(2)}) copy-start(f32[8,1024]{1,0:T(8,128)} %weight_ref.1) | copy-start | bytes 98308
  3.0 0.7 %copy-start.9 = (f32[3,1024]{1,0:T(4,128)S(1)}, f32[3,1024]{1,0:T(4,128)}, u32[]{:S(2)}) copy-start(f32[3,1024]{1,0:T(4,128)} %velocity_ref.1) | copy-start | bytes 36868
  3.8 0.7 %copy-start.11 = (s32[1024]{0:T(1024)S(1)}, s32[1024]{0:T(1024)}, u32[]{:S(2)}) copy-start(s32[1024]{0:T(1024)} %param.22) | copy-start | bytes 12292
  4.4 0.7 %copy-start.12 = (f32[1024]{0:T(1024)S(1)}, f32[1024]{0:T(1024)}, u32[]{:S(2)}) copy-start(f32[1024]{0:T(1024)} %param.21) | copy-start | bytes 12292
  8.5 8.8 %copy-start.2 = (f32[4096]{0:T(1024)S(1)}, f32[4096]{0:T(1024)}, u32[]{:S(2)}) copy-start(f32[4096]{0:T(1024)} %param.13) | copy-start | bytes 49156
  8.5 8.8 %copy-start.4 = (s32[4,1024]{1,0:T(4,128)S(1)}, s32[4,1024]{1,0:T(4,128)}, u32[]{:S(2)}) copy-start(s32[4,1024]{1,0:T(4,128)} %export_ref.3) | copy-start | bytes 49156
  8.5 20.0 %copy-start = (f32[6,4096]{1,0:T(8,128)S(1)}, f32[6,4096]{1,0:T(8,128)}, u32[]{:S(2)}) copy-start(f32[6,4096]{1,0:T(8,128)} %coeff_ref.3) | copy-start | bytes 294916
  8.5 20.0 %copy-start.1 = (s32[6,4096]{1,0:T(8,128)S(1)}, s32[6,4096]{1,0:T(8,128)}, u32[]{:S(2)}) copy-start(s32[6,4096]{1,0:T(8,128)} %neighbour_ref.3) | copy-start | bytes 294916
  8.5 31.5 %all-to-all-start = ((f32[32,48,128]{2,1,0:T(8,128)}), f32[32,48,128]{2,1,0:T(8,128)S(1)}, u32[]{:S(2)}, u32[]{:S(2)}) async-start(f32[32,48,128]{2,1,0:T(8,128)} %get-tuple-element.29), calls=%async_computation | async-start | bytes 1572864 | tf_op jit(solution)/shard_map/all_to_all | solution.py:294
  17.3 11.2 %copy-start.3 = (f32[4096]{0:T(1024)S(1)}, f32[4096]{0:T(1024)}, u32[]{:S(2)}) copy-start(f32[4096]{0:T(1024)} %param.15) | copy-start | bytes 49156
  17.3 11.2 %copy-start.10 = (f32[4096]{0:T(1024)S(1)}, f32[4096]{0:T(1024)}, u32[]{:S(2)}) copy-start(f32[4096]{0:T(1024)} %param.14) | copy-start | bytes 49156
  17.6 8.4 %collective-permute-start = (f32[8,128]{1,0:T(8,128)S(1)}, f32[8,128]{1,0:T(8,128)S(1)}, u32[]{:S(2)}, u32[]{:S(2)}) collective-permute-start(f32[8,128]{1,0:T(8,128)S(1)} %get-tuple-element.19), channel_id=1, source_target_pairs={{0,1},{1,2},{2,3},{3,4},{4,5},{5,6},{6,7},{7,8},{8,9},{9,10},{10,1... | collective-permute-start | bytes 12296 | tf_op jit(solution)/shard_map/ppermute | solution.py:259
  19.4 9.1 %collective-permute-start.1 = (f32[8,128]{1,0:T(8,128)S(1)}, f32[8,128]{1,0:T(8,128)S(1)}, u32[]{:S(2)}, u32[]{:S(2)}) collective-permute-start(f32[8,128]{1,0:T(8,128)S(1)} %get-tuple-element.20), channel_id=1, source_target_pairs={{1,0},{2,1},{3,2},{4,3},{5,4},{6,5},{7,6},{8,7},{9,8},{10,9},{11,1... | collective-permute-start | bytes 12296 | tf_op jit(solution)/shard_map/ppermute | solution.py:260
  19.4 9.1 %collective-permute-start.2 = (f32[8,128]{1,0:T(8,128)S(1)}, f32[8,128]{1,0:T(8,128)S(1)}, u32[]{:S(2)}, u32[]{:S(2)}) collective-permute-start(f32[8,128]{1,0:T(8,128)S(1)} %get-tuple-element.21), channel_id=1, source_target_pairs={{0,32},{32,64},{64,96},{96,128},{128,160},{160,192},{192,224},{224... | collective-permute-start | bytes 12296 | tf_op jit(solution)/shard_map/ppermute | solution.py:261
  21.0 7.4 %collective-permute-start.3 = (f32[8,128]{1,0:T(8,128)S(1)}, f32[8,128]{1,0:T(8,128)S(1)}, u32[]{:S(2)}, u32[]{:S(2)}) collective-permute-start(f32[8,128]{1,0:T(8,128)S(1)} %get-tuple-element.22), channel_id=1, source_target_pairs={{32,0},{64,32},{96,64},{128,96},{160,128},{192,160},{224,192},{0,2... | collective-permute-start | bytes 12296 | tf_op jit(solution)/shard_map/ppermute | solution.py:262
  28.5 11.5 %copy-start.6 = (f32[3,4096]{1,0:T(4,128)S(1)}, f32[3,4096]{1,0:T(4,128)}, u32[]{:S(2)}) copy-start(f32[3,4096]{1,0:T(4,128)} %fluid_ref.1) | copy-start | bytes 147460
  31.2 12.3 %collective-permute-start.4 = (f32[8,128]{1,0:T(8,128)S(1)}, f32[8,128]{1,0:T(8,128)S(1)}, u32[]{:S(2)}, u32[]{:S(2)}) collective-permute-start(f32[8,128]{1,0:T(8,128)S(1)} %get-tuple-element.24), channel_id=1, source_target_pairs={{0,1},{1,2},{2,3},{3,4},{4,5},{5,6},{6,7},{7,8},{8,9},{9,10},{10,1... | collective-permute-start | bytes 12296 | tf_op jit(solution)/shard_map/ppermute | solution.py:259
  31.4 12.1 %collective-permute-start.5 = (f32[8,128]{1,0:T(8,128)S(1)}, f32[8,128]{1,0:T(8,128)S(1)}, u32[]{:S(2)}, u32[]{:S(2)}) collective-permute-start(f32[8,128]{1,0:T(8,128)S(1)} %get-tuple-element.25), channel_id=1, source_target_pairs={{1,0},{2,1},{3,2},{4,3},{5,4},{6,5},{7,6},{8,7},{9,8},{10,9},{11,1... | collective-permute-start | bytes 12296 | tf_op jit(solution)/shard_map/ppermute | solution.py:260
  34.4 9.1 %collective-permute-start.6 = (f32[8,128]{1,0:T(8,128)S(1)}, f32[8,128]{1,0:T(8,128)S(1)}, u32[]{:S(2)}, u32[]{:S(2)}) collective-permute-start(f32[8,128]{1,0:T(8,128)S(1)} %get-tuple-element.26), channel_id=1, source_target_pairs={{0,32},{32,64},{64,96},{96,128},{128,160},{160,192},{192,224},{224... | collective-permute-start | bytes 12296 | tf_op jit(solution)/shard_map/ppermute | solution.py:261
  36.0 7.5 %collective-permute-start.7 = (f32[8,128]{1,0:T(8,128)S(1)}, f32[8,128]{1,0:T(8,128)S(1)}, u32[]{:S(2)}, u32[]{:S(2)}) collective-permute-start(f32[8,128]{1,0:T(8,128)S(1)} %get-tuple-element.27), channel_id=1, source_target_pairs={{32,0},{64,32},{96,64},{128,96},{160,128},{192,160},{224,192},{0,2... | collective-permute-start | bytes 12296 | tf_op jit(solution)/shard_map/ppermute | solution.py:262
  47.7 18.2 %all-to-all-start.1 = ((f32[32,4,128]{2,1,0:T(4,128)}), f32[32,4,128]{2,1,0:T(4,128)S(1)}, u32[]{:S(2)}, u32[]{:S(2)}) async-start(f32[32,4,128]{2,1,0:T(4,128)} %get-tuple-element.33), calls=%async_computation.1 | async-start | bytes 131072 | tf_op jit(solution)/shard_map/all_to_all | solution.py:304

commit v2 on v1

v2 whole, which is shorter than its diff:
```python
import jax
import jax.numpy as jnp
from jax import lax
from jax.experimental import pallas as pl
from jax.experimental.pallas import tpu as pltpu
from jax.sharding import PartitionSpec as P

CENTRE = 7.0
HALF_WIDTH = 4.0
LOADING = 8.0
SIGMA = CENTRE / HALF_WIDTH
RHO_FIRST = 1.0 / SIGMA
RHO_NEXT = 1.0 / (2.0 * SIGMA - RHO_FIRST)

CELLS = 4096
LANES = 128
ROWS = CELLS // LANES
FACE = 1024
FACE_ROWS = FACE // LANES
NBR = 6
K = 8
PARCELS = 1024
CHUNKS = PARCELS // LANES
OWNERS = 32
CAP = 128
SENT = 24

F32 = jnp.float32
BF16 = jnp.bfloat16
I32 = jnp.int32


def pick(row, lanes):
    return jnp.take_along_axis(row, lanes, axis=1, mode="promise_in_bounds")


def wide(row, height):
    return jnp.broadcast_to(row, (height, LANES))


def look_up(tables, index):
    height = index.shape[0]
    high = lax.shift_right_logical(index, 7)
    low = lax.bitwise_and(index, 127)
    found = [jnp.zeros((height, LANES), F32) for _ in tables]
    for r in range(len(tables[0])):
        here = high == r
        for c, table in enumerate(tables):
            found[c] = jnp.where(here, pick(wide(table[r](), height), low), found[c])
    return found


def rows_of(ref, count):
    return [lambda r=r: ref[r : r + 1, :] for r in range(count)]


def is_even(axis):
    return lax.rem(lax.axis_index(axis), 2) == 0


def write_exports(field_ref, export_ref, face_ref, outs):
    for t in range(FACE_ROWS):
        index = export_ref[:, t * LANES : (t + 1) * LANES]
        (found,) = look_up([rows_of(field_ref, ROWS)], index)
        for d in range(4):
            face_ref[d, t : t + 1, :] = found[d : d + 1]
    for axis, d in (("dom", 0), ("group", 2)):
        even = is_even(axis)
        outs[d][...] = jnp.where(even, face_ref[d], face_ref[d + 1])
        outs[d + 1][...] = jnp.where(even, face_ref[d + 1], face_ref[d])


def export_kernel(field_ref, export_ref, out0, out1, out2, out3, face_ref):
    write_exports(field_ref, export_ref, face_ref, (out0, out1, out2, out3))


def multiply(vector_ref, got_refs, diagonal_ref, coeff_ref, neighbour_ref, halo_ref, out_ref):
    group = lax.axis_index("group")
    last = lax.axis_size("group") - 1
    for axis, d in (("dom", 0), ("group", 2)):
        even = is_even(axis)
        below = jnp.where(even, got_refs[d + 1][...], got_refs[d][...])
        above = jnp.where(even, got_refs[d][...], got_refs[d + 1][...])
        if axis == "group":
            below = jnp.where(group > 0, below, 0.0)
            above = jnp.where(group < last, above, 0.0)
        halo_ref[d * FACE_ROWS : (d + 1) * FACE_ROWS, :] = below
        halo_ref[(d + 1) * FACE_ROWS : (d + 2) * FACE_ROWS, :] = above
    table = rows_of(vector_ref, ROWS) + rows_of(halo_ref, 4 * FACE_ROWS)
    for t in range(0, ROWS, 4):
        cuts = [slice(u * LANES, (u + 1) * LANES) for u in range(t, t + 4)]
        (found,) = look_up([table], jnp.concatenate([neighbour_ref[:, cut] for cut in cuts], axis=0))
        for u, cut in enumerate(cuts):
            part = coeff_ref[:, cut] * found[NBR * u : NBR * (u + 1)]
            linked = jnp.sum(part, axis=0, keepdims=True)
            row = slice(t + u, t + u + 1)
            out_ref[row, :] = diagonal_ref[row, :] * vector_ref[row, :] - linked


def first_kernel(
    pressure_ref, got0, got1, got2, got3, source_ref, diagonal_ref, coeff_ref, neighbour_ref,
    export_ref, residual_ref, direction_ref, out0, out1, out2, out3, halo_ref, product_ref, face_ref,
):
    multiply(
        pressure_ref, (got0, got1, got2, got3), diagonal_ref, coeff_ref, neighbour_ref,
        halo_ref, product_ref,
    )
    residual = source_ref[...] - product_ref[...]
    residual_ref[...] = residual
    direction_ref[...] = residual / CENTRE
    write_exports(direction_ref, export_ref, face_ref, (out0, out1, out2, out3))


def second_kernel(
    direction_ref, got0, got1, got2, got3, pressure_ref, residual_ref, diagonal_ref, coeff_ref,
    neighbour_ref, parcel_ref, moved_ref, out_ref, answer_ref, halo_ref, product_ref,
):
    multiply(
        direction_ref, (got0, got1, got2, got3), diagonal_ref, coeff_ref, neighbour_ref,
        halo_ref, product_ref,
    )
    direction = direction_ref[...]
    residual = residual_ref[...] - product_ref[...]
    iterate = pressure_ref[...] + direction
    direction = RHO_NEXT * RHO_FIRST * direction + (2.0 * RHO_NEXT / HALF_WIDTH) * residual
    out_ref[...] = iterate + direction
    table = rows_of(out_ref, ROWS)
    for s in range(OWNERS):
        (found,) = look_up([table], parcel_ref[s, 8:16, :].astype(I32))
        answer_ref[s, 0:8, :] = found
        answer_ref[s, 8:16, :] = moved_ref[s]


def slot_kernel(owner_ref, cells_ref, weight_ref, velocity_ref, rate_ref, place_ref, sent_ref):
    owners = lax.broadcasted_iota(I32, (OWNERS, LANES), 0)
    lanes = lax.broadcasted_iota(I32, (OWNERS, LANES), 1)
    chosen = [owners == wide(owner_ref[j : j + 1, :], OWNERS) for j in range(CHUNKS)]
    stacked = jnp.concatenate([c.astype(F32).astype(BF16) for c in chosen], axis=0)
    row = lax.broadcasted_iota(I32, (LANES, 2 * LANES), 0)
    column = lax.broadcasted_iota(I32, (LANES, 2 * LANES), 1)
    before = ((row < column) | (column >= LANES)).astype(F32).astype(BF16)
    counts = jnp.dot(stacked, before, preferred_element_type=F32)
    carried = jnp.zeros((OWNERS, LANES), F32)
    ranks = []
    for j in range(CHUNKS):
        part = counts[j * OWNERS : (j + 1) * OWNERS]
        rank = jnp.where(chosen[j], part[:, :LANES] + carried, 0.0)
        ranks.append(jnp.sum(rank, axis=0, keepdims=True))
        carried = carried + part[:, LANES:]
        place_ref[j : j + 1, :] = owner_ref[j : j + 1, :] * CAP + ranks[j].astype(I32)
    slots = lax.broadcasted_iota(I32, (CAP, LANES), 0).astype(F32)
    at_rank = jnp.concatenate(
        [(slots == wide(ranks[j], CAP)).astype(F32).astype(BF16) for j in range(CHUNKS)], axis=1
    )
    lane_of = jnp.concatenate(
        [jnp.where(c, lanes.astype(F32), 0.0).astype(BF16) for c in chosen], axis=1
    )
    chunk_of = jnp.concatenate(
        [jnp.where(c, F32(j + 1), 0.0).astype(BF16) for j, c in enumerate(chosen)], axis=1
    )
    found = lax.dot_general(
        jnp.concatenate([lane_of, chunk_of], axis=0), at_rank, (((1,), (1,)), ((), ())),
        preferred_element_type=F32,
    ).astype(I32)
    for o in range(OWNERS):
        low = wide(found[o : o + 1], 8)
        high = wide(found[OWNERS + o : OWNERS + o + 1], 8)
        here = [high == j + 1 for j in range(CHUNKS)]

        def place(ref, height=8):
            value = jnp.zeros((height, LANES), F32)
            for j in range(CHUNKS):
                part = ref[:, j * LANES : (j + 1) * LANES].astype(F32)
                value = jnp.where(here[j][:height], pick(part, low[:height]), value)
            return value

        sent_ref[o, 0:8, :] = place(weight_ref)
        sent_ref[o, 8:16, :] = place(cells_ref)
        sent_ref[o, 16:19, :] = place(velocity_ref, 3)
        value = jnp.zeros((8, LANES), F32)
        for j in range(CHUNKS):
            value = jnp.where(here[j], pick(wide(rate_ref[j : j + 1, :], 8), low), value)
        sent_ref[o, 19:24, :] = jnp.concatenate([value[:1], jnp.zeros((4, LANES), F32)], axis=0)


def fluid_kernel(fluid_ref, parcel_ref, moved_ref, force_ref):
    tables = [
        [lambda c=c, r=r: fluid_ref[c : c + 1, r * LANES : (r + 1) * LANES] for r in range(ROWS)]
        for c in range(3)
    ]
    for s in range(OWNERS):
        found = look_up(tables, parcel_ref[s, 8:16, :].astype(I32))
        weights = parcel_ref[s, 0:8, :]
        rate = parcel_ref[s, 19:20, :]
        for c in range(3):
            velocity = parcel_ref[s, 16 + c : 17 + c, :]
            fluid_at = jnp.sum(weights * found[c], axis=0, keepdims=True)
            moved_ref[s, c : c + 1, :] = velocity + rate * (fluid_at - velocity)
            force_ref[s, c : c + 1, :] = rate * (velocity - fluid_at)
        moved_ref[s, 3:8, :] = jnp.zeros((5, LANES), F32)
        force_ref[s, 3:4, :] = jnp.zeros((1, LANES), F32)


def scatter_kernel(parcel_ref, force_ref, out_ref, total_ref):
    rows = lax.broadcasted_iota(I32, (ROWS, LANES), 0)
    columns = lax.broadcasted_iota(I32, (LANES, LANES), 0)
    total_ref[...] = jnp.zeros_like(total_ref)
    for first in range(0, OWNERS, 4):
        left, right = [], []
        for s in range(first, first + 4):
            cells = parcel_ref[s, 8:16, :].astype(I32)
            high = lax.shift_right_logical(cells, 7)
            low = lax.bitwise_and(cells, 127)
            weights = LOADING * parcel_ref[s, 0:8, :]
            parts = []
            for c in range(3):
                value = weights * force_ref[s, c : c + 1, :]
                top = value.astype(BF16).astype(F32)
                parts.append(top)
                parts.append(value - top)
            for k in range(K):
                here = rows == wide(high[k : k + 1], ROWS)
                chosen = [jnp.where(here, wide(p[k : k + 1], ROWS), 0.0).astype(BF16) for p in parts]
                left.append(jnp.concatenate(chosen, axis=0))
                right.append((columns == wide(low[k : k + 1], LANES)).astype(F32).astype(BF16))
        total_ref[...] += lax.dot_general(
            jnp.concatenate(left, axis=1), jnp.concatenate(right, axis=1),
            (((1,), (1,)), ((), ())), preferred_element_type=F32,
        )
    for c in range(3):
        both = (
            total_ref[2 * c * ROWS : (2 * c + 1) * ROWS, :]
            + total_ref[(2 * c + 1) * ROWS : (2 * c + 2) * ROWS, :]
        )
        for r in range(ROWS):
            out_ref[c : c + 1, r * LANES : (r + 1) * LANES] = both[r : r + 1]


def return_kernel(place_ref, answer_ref, grad_ref, out_ref):
    for j in range(CHUNKS):
        cut = slice(j * LANES, (j + 1) * LANES)
        place = wide(place_ref[j : j + 1, :], 8)
        high = lax.shift_right_logical(place, 7)
        low = lax.bitwise_and(place, 127)
        pressure = jnp.zeros((8, LANES), F32)
        moved = jnp.zeros((8, LANES), F32)
        for o in range(OWNERS):
            here = high == o
            pressure = jnp.where(here, pick(answer_ref[o, 0:8, :], low), pressure)
            moved = jnp.where(here, pick(answer_ref[o, 8:16, :], low), moved)
        for c in range(3):
            gradient = jnp.sum(grad_ref[c, :, cut] * pressure, axis=0, keepdims=True)
            out_ref[c : c + 1, cut] = moved[c : c + 1] - gradient


def shape(*dims, dtype=F32):
    return jax.ShapeDtypeStruct(dims, dtype)


def pairs(count):
    first = [(i, i ^ 1) for i in range(count)]
    second = [(i, (i - 1) % count if i % 2 == 0 else (i + 1) % count) for i in range(count)]
    return first, second


def exchange(faces):
    dom_first, dom_second = pairs(lax.axis_size("dom"))
    group_first, group_second = pairs(lax.axis_size("group"))
    far = lax.ppermute(faces[1], "dom", dom_second)
    return (
        lax.ppermute(faces[0], "dom", dom_first),
        far,
        lax.ppermute(faces[2], "group", group_first),
        lax.ppermute(faces[3], "group", group_second),
    )


def call(kernel, outs, flops, scratch=(), grant=32, **kwargs):
    return pl.pallas_call(
        kernel,
        out_shape=outs,
        scratch_shapes=list(scratch),
        compiler_params=pltpu.CompilerParams(vmem_limit_bytes=grant * 1024 * 1024),
        cost_estimate=pl.CostEstimate(flops=flops, bytes_accessed=400000, transcendentals=0),
        **kwargs,
    )


def staged(kernel, operands, outs, flops, scratch=()):
    count = len(operands)

    def run(*refs):
        local, sems = refs[-1 - count : -1], refs[-1]
        copies = [
            pltpu.make_async_copy(refs[i], local[i], sems.at[i]) for i in range(count)
        ]
        for copy in copies:
            copy.start()
        for copy in copies:
            copy.wait()
        kernel(*local, *refs[count : -1 - count])

    scratch = (
        *scratch,
        *(pltpu.VMEM(x.shape, x.dtype) for x in operands),
        pltpu.SemaphoreType.DMA((count,)),
    )
    specs = [pl.BlockSpec(memory_space=pltpu.HBM)] * count
    return call(run, outs, flops, scratch, in_specs=specs)(*operands)


def per_device(
    pressure_old, source_term, diagonal, face_coeffs, neighbours, export_cells, fluid_velocity,
    parcel_velocity, drag_rate, parcel_owner, parcel_cells, interp_weights, grad_weights,
):
    pressure_old = pressure_old.reshape(ROWS, LANES)
    source_term = source_term.reshape(ROWS, LANES)
    diagonal = diagonal.reshape(ROWS, LANES)
    face = shape(FACE_ROWS, LANES)
    field = shape(ROWS, LANES)
    faces_buffer = pltpu.VMEM((4, FACE_ROWS, LANES), F32)
    halo = (pltpu.VMEM((4 * FACE_ROWS, LANES), F32), pltpu.VMEM((ROWS, LANES), F32))

    faces = staged(
        export_kernel, (pressure_old, export_cells), (face,) * 4, 10**6, (faces_buffer,)
    )
    got = exchange(faces)
    place, sent = staged(
        slot_kernel,
        (
            parcel_owner.reshape(CHUNKS, LANES), parcel_cells, interp_weights, parcel_velocity,
            drag_rate.reshape(CHUNKS, LANES),
        ),
        (shape(CHUNKS, LANES, dtype=I32), shape(OWNERS, SENT, CAP)), 10**8,
    )
    got, sent = lax.optimization_barrier((got, sent))
    parcels = lax.all_to_all(sent, "dom", split_axis=0, concat_axis=0, tiled=True)
    residual, direction, *faces = call(
        first_kernel, (field, field) + (face,) * 4, 10**8, halo + (faces_buffer,)
    )(pressure_old, *got, source_term, diagonal, face_coeffs, neighbours, export_cells)
    got = exchange(faces)
    moved, force = call(
        fluid_kernel, (shape(OWNERS, 8, CAP), shape(OWNERS, 4, CAP)), 10**9
    )(fluid_velocity, parcels)
    iterate, answer = call(second_kernel, (field, shape(OWNERS, 16, CAP)), 10**8, halo)(
        direction, *got, pressure_old, residual, diagonal, face_coeffs, neighbours, parcels, moved
    )
    returned = lax.all_to_all(answer, "dom", split_axis=0, concat_axis=0, tiled=True)
    momentum_source = call(
        scatter_kernel, shape(3, CELLS), 2 * 10**9, (pltpu.VMEM((6 * ROWS, LANES), F32),)
    )(parcels, force)
    parcel_new = call(return_kernel, shape(3, PARCELS), 10**6)(place, returned, grad_weights)
    return (iterate.reshape(CELLS), parcel_new, momentum_source)


def solution(mesh):
    whole = ("group", "dom")
    flat, rows = P(whole), P(None, whole)
    return jax.shard_map(
        per_device,
        mesh=mesh,
        in_specs=(
            flat, flat, flat, rows, rows, rows, rows, rows, flat, flat, rows, rows,
            P(None, None, whole),
        ),
        out_specs=(flat, rows, rows),
        check_vma=False,
    )
```

time: 67.2 us -> 60.1 us (0.89)
  starting transfers between devices: 33.5 us -> 26.2 us
  waiting for transfers between devices: 3.51 us -> 7.39 us
  Pallas kernels: 24.3 us -> 22.1 us
  local copies, waits for them, and re-layouts: 4.52 us -> 2.96 us
    pallas_call x1, Pallas kernels: 9.47 us -> 4.18 us  [per_device(): call(scatter_kernel, shape(3, CELLS), 2 * 10 ** 9, (pltpu.VMEM((6 * ROWS,...]
    all_to_all x1, waiting for transfers between devices: 0.01 us -> 4.82 us  [per_device(): lax.all_to_all(answer, 'dom', split_axis=0, concat_axis=0, tiled=True)]
    ppermute x8, starting transfers between devices: 16.1 us -> 12.4 us  [the longest x2 6.12 us: exchange(): lax.ppermute(faces[3], 'group', group_second)]
    ppermute x8, waiting for transfers between devices: 3.51 us -> 0.02 us  [the longest x2 0.01 us: exchange(): far = lax.ppermute(faces[1], 'dom', dom_second)]
    all_to_all x1, starting transfers between devices: 8.74 us -> 5.41 us  [per_device(): lax.all_to_all(answer, 'dom', split_axis=0, concat_axis=0, tiled=True)]
    pallas_call x6, Pallas kernels: 14.9 us -> 17.9 us  [the longest x1 5.92 us: per_device(): call(second_kernel, (field, shape(OWNERS, 16, CAP)), 10 ** 8, halo)]
    all_to_all x1, waiting for transfers between devices: 0.01 us -> 2.55 us  [per_device(): lax.all_to_all(sent, 'dom', split_axis=0, concat_axis=0, tiled=True)]
    unnamed x26 -> x30, local copies, waits for them, and re-layouts: 4.52 us -> 2.96 us
where the time goes in v2:
time: 60.1 us; the launch traced here: 59.5 us
  starting transfers between devices  26.2 us (44%)
  Pallas kernels  22.1 us (37%)
  waiting for transfers between devices  7.39 us (12%)
  local copies, waits for them, and re-layouts  2.96 us (5%)
  between operations  0.87 us (1%)
    all_to_all x1, starting transfers between devices, per_device(): lax.all_to_all(sent, 'dom', split_axis=0, concat_axis=0, tiled=True)  8.34 us
    ppermute x2, starting transfers between devices, exchange(): lax.ppermute(faces[3], 'group', group_second)  6.12 us
    pallas_call x1, Pallas kernels, per_device(): call(second_kernel, (field, shape(OWNERS, 16, CAP)), 10 ** 8, halo)  5.92 us
    all_to_all x1, starting transfers between devices, per_device(): lax.all_to_all(answer, 'dom', split_axis=0, concat_axis=0, tiled=True)  5.41 us
    all_to_all x1, waiting for transfers between devices, per_device(): lax.all_to_all(answer, 'dom', split_axis=0, concat_axis=0, tiled=True)  4.82 us
    pallas_call x1, Pallas kernels, per_device(): call(first_kernel, (field, field) + (face,) * 4, 10 ** 8, halo + (faces_b...  4.33 us
    pallas_call x1, Pallas kernels, per_device(): call(scatter_kernel, shape(3, CELLS), 2 * 10 ** 9, (pltpu.VMEM((6 * ROWS,...  4.18 us
    ppermute x2, starting transfers between devices, exchange(): lax.ppermute(faces[0], 'dom', dom_first)  3.76 us
  transfers between devices with their start and end apart: 10, of which 2 were waited for; matrix products, arithmetic and copies ran while one was open for 0% of the time, Pallas kernels for 24%

profile of v2, /device:TPU:1, one launch (start us, length us, event | category | flops | bytes accessed | tf_op | source)
XLA Modules:
  0.0 59.5 jit_solution(7363014384995458889)
XLA Ops:
  0.6 0.0 copy-start.3
  0.6 0.7 %copy-done.3 = f32[4096]{0:T(1024)S(1)} copy-done((f32[4096]{0:T(1024)S(1)}, f32[4096]{0:T(1024)}, u32[]{:S(2)}) %copy-start.3) | copy-done | bytes 16408
  1.4 0.0 copy-start.6
  1.4 0.7 %copy-done.6 = s32[4,1024]{1,0:T(4,128)S(1)} copy-done((s32[4,1024]{1,0:T(4,128)S(1)}, s32[4,1024]{1,0:T(4,128)}, u32[]{:S(2)}) %copy-start.6) | copy-done | bytes 16408
  2.1 0.0 copy-start.9
  2.1 0.4 shard_map.148
  2.5 3.3 %collective-permute-start = (f32[8,128]{1,0:T(8,128)S(1)}, f32[8,128]{1,0:T(8,128)S(1)}, u32[]{:S(2)}, u32[]{:S(2)}) collective-permute-start(f32[8,128]{1,0:T(8,128)S(1)} %get-tuple-element.24), channel_id=1, source_target_pairs={{0,1},{1,0},{2,3},{3,2},{4,5},{5,4},{6,7},{7,6},{8,9},{9,8},{10,11... | collective-permute-start | bytes 12296 | tf_op jit(solution)/shard_map/ppermute | solution.py:271
  5.8 0.0 copy-start.14
  5.8 0.0 copy-start.13
  5.8 0.0 collective-permute-start.1
  5.8 1.1 %collective-permute-start.2 = (f32[8,128]{1,0:T(8,128)S(1)}, f32[8,128]{1,0:T(8,128)S(1)}, u32[]{:S(2)}, u32[]{:S(2)}) collective-permute-start(f32[8,128]{1,0:T(8,128)S(1)} %get-tuple-element.26), channel_id=1, source_target_pairs={{0,32},{32,0},{64,96},{96,64},{128,160},{160,128},{192,224},{224,1... | collective-permute-start | bytes 12296 | tf_op jit(solution)/shard_map/ppermute | solution.py:273
  6.9 4.7 %collective-permute-start.3 = (f32[8,128]{1,0:T(8,128)S(1)}, f32[8,128]{1,0:T(8,128)S(1)}, u32[]{:S(2)}, u32[]{:S(2)}) collective-permute-start(f32[8,128]{1,0:T(8,128)S(1)} %get-tuple-element.27), channel_id=1, source_target_pairs={{0,224},{32,64},{64,32},{96,128},{128,96},{160,192},{192,160},{224... | collective-permute-start | bytes 12296 | tf_op jit(solution)/shard_map/ppermute | solution.py:274
  11.6 0.0 copy-done.9
  11.6 0.0 copy-done.14
  11.6 0.0 copy-done.13
  11.6 0.0 copy-start.10
  11.6 0.8 %copy-done.10 = f32[8,1024]{1,0:T(8,128)S(1)} copy-done((f32[8,1024]{1,0:T(8,128)S(1)}, f32[8,1024]{1,0:T(8,128)}, u32[]{:S(2)}) %copy-start.10) | copy-done | bytes 32792
  12.4 0.0 copy-start.11
  12.4 0.7 %copy-done.11 = f32[3,1024]{1,0:T(4,128)S(1)} copy-done((f32[3,1024]{1,0:T(4,128)S(1)}, f32[3,1024]{1,0:T(4,128)}, u32[]{:S(2)}) %copy-start.11) | copy-done | bytes 12312
  13.1 2.5 %shard_map.149 = (s32[8,128]{1,0:T(8,128)S(1)}, f32[32,24,128]{2,1,0:T(8,128)}) custom-call(s32[8,128]{1,0:T(8,128)S(1)} %bitcast.12, s32[8,1024]{1,0:T(8,128)S(1)} %copy-done.9, f32[8,1024]{1,0:T(8,128)S(1)} %copy-done.10, f32[3,1024]{1,0:T(4,128)S(1)} %copy-done.11, f32[8,128]{1,0:T(8,128)S(1)} %bitcast.13), custom_call_target="tpu_custom_call" | custom-call | flops 100000000 | bytes 400000 | tf_op jit(solution)/shard_map/pallas_call | solution.py:309
  15.6 0.0 collective-permute-done.got0
  15.6 0.0 collective-permute-done.1.got1
  15.7 0.0 collective-permute-done.2.got2
  15.7 0.0 collective-permute-done.3.got3
  15.7 0.0 copy-start
  15.7 0.0 copy-start.1
  15.7 0.0 copy-start.4
  15.7 0.0 copy-start.5
  15.7 0.0 copy-start.7
  15.7 0.0 copy-start.12
  15.7 8.3 %all-to-all-start = ((f32[32,24,128]{2,1,0:T(8,128)}), f32[32,24,128]{2,1,0:T(8,128)S(1)}, u32[]{:S(2)}, u32[]{:S(2)}) async-start(f32[32,24,128]{2,1,0:T(8,128)} %get-tuple-element.39), calls=%async_computation | async-start | bytes 786432 | tf_op jit(solution)/shard_map/all_to_all | solution.py:337
  24.1 0.0 copy-done
  24.1 0.0 copy-done.1
  24.1 0.0 copy-done.4
  24.1 0.0 copy-done.5
  24.1 0.0 copy-done.7
  24.1 0.0 copy-done.12
  24.2 0.0 copy-start.8
  24.2 4.3 %shard_map.150 = (f32[32,128]{1,0:T(8,128)S(1)}, f32[32,128]{1,0:T(8,128)S(1)}, f32[8,128]{1,0:T(8,128)S(1)}, f32[8,128]{1,0:T(8,128)S(1)}, f32[8,128]{1,0:T(8,128)S(1)}, /*index=5*/f32[8,128]{1,0:T(8,128)S(1)}) custom-call(f32[32,128]{1,0:T(8,128)S(1)} %bitcast.7, f32[8,128]{1,0:T(8,128)S(1)} %collective-permute-done.got0, ...), custom_call_target="tpu_custom_call" | custom-call | flops 100000000 | bytes 400000 | tf_op jit(solution)/shard_map/pallas_call | solution.py:338
  28.5 0.4 collective-permute-start.4
  28.9 1.4 %collective-permute-start.5 = (f32[8,128]{1,0:T(8,128)S(1)}, f32[8,128]{1,0:T(8,128)S(1)}, u32[]{:S(2)}, u32[]{:S(2)}) collective-permute-start(f32[8,128]{1,0:T(8,128)S(1)} %get-tuple-element.35), channel_id=1, source_target_pairs={{0,31},{1,2},{2,1},{3,4},{4,3},{5,6},{6,5},{7,8},{8,7},{9,10},{10,... | collective-permute-start | bytes 12296 | tf_op jit(solution)/shard_map/ppermute | solution.py:269
  30.4 0.0 collective-permute-start.6
  30.4 1.5 %collective-permute-start.7 = (f32[8,128]{1,0:T(8,128)S(1)}, f32[8,128]{1,0:T(8,128)S(1)}, u32[]{:S(2)}, u32[]{:S(2)}) collective-permute-start(f32[8,128]{1,0:T(8,128)S(1)} %get-tuple-element.37), channel_id=1, source_target_pairs={{0,224},{32,64},{64,32},{96,128},{128,96},{160,192},{192,160},{224... | collective-permute-start | bytes 12296 | tf_op jit(solution)/shard_map/ppermute | solution.py:274
  31.8 2.5 %all-to-all-done.parcel_ref = f32[32,24,128]{2,1,0:T(8,128)S(1)} async-done(((f32[32,24,128]{2,1,0:T(8,128)}), f32[32,24,128]{2,1,0:T(8,128)S(1)}, u32[]{:S(2)}, u32[]{:S(2)}) %all-to-all-start) | async-done | bytes 393248 | tf_op jit(solution)/shard_map/all_to_all | solution.py:337
  34.4 0.0 copy-done.8
  34.4 3.5 %shard_map.151 = (f32[32,8,128]{2,1,0:T(8,128)S(1)}, f32[32,4,128]{2,1,0:T(4,128)S(1)}) custom-call(f32[3,4096]{1,0:T(4,128)S(1)} %copy-done.8, f32[32,24,128]{2,1,0:T(8,128)S(1)} %all-to-all-done.parcel_ref), custom_call_target="tpu_custom_call" | custom-call | flops 1000000000 | bytes 400000 | tf_op jit(solution)/shard_map/pallas_call | solution.py:342
  37.9 0.0 collective-permute-done.4.got0
  37.9 0.0 collective-permute-done.5.got1
  37.9 0.0 collective-permute-done.6.got2
  37.9 0.0 collective-permute-done.7.got3
  37.9 5.9 %shard_map.152 = (f32[32,128]{1,0:T(8,128)}, f32[32,16,128]{2,1,0:T(8,128)}) custom-call(f32[32,128]{1,0:T(8,128)S(1)} %get-tuple-element.33.direction_ref, f32[8,128]{1,0:T(8,128)S(1)} %collective-permute-done.4.got0, f32[8,128]{1,0:T(8,128)S(1)} %collective-permute-done.5.got1, f32[8,128]{1,0:T(8,128)S(1)} %collective-permute-done.6.got2, ...), custom_call_target="tpu_custom_call" | custom-call | flops 100000000 | bytes 400000 | tf_op jit(solution)/shard_map/pallas_call | solution.py:345
  43.8 5.4 %all-to-all-start.1 = ((f32[32,16,128]{2,1,0:T(8,128)}), f32[32,16,128]{2,1,0:T(8,128)S(1)}, u32[]{:S(2)}, u32[]{:S(2)}) async-start(f32[32,16,128]{2,1,0:T(8,128)} %get-tuple-element.43), calls=%async_computation.1 | async-start | bytes 524288 | tf_op jit(solution)/shard_map/all_to_all | solution.py:348
  49.2 0.0 copy-start.2
  49.3 4.2 %shard_map.154 = f32[3,4096]{1,0:T(4,128)} custom-call(f32[32,24,128]{2,1,0:T(8,128)S(1)} %all-to-all-done.parcel_ref, f32[32,4,128]{2,1,0:T(4,128)S(1)} %get-tuple-element.44.force_ref), custom_call_target="tpu_custom_call" | custom-call | flops 2000000000 | bytes 400000 | tf_op jit(solution)/shard_map/pallas_call | solution.py:349
  53.4 4.8 %all-to-all-done.1.answer_ref = f32[32,16,128]{2,1,0:T(8,128)S(1)} async-done(((f32[32,16,128]{2,1,0:T(8,128)}), f32[32,16,128]{2,1,0:T(8,128)S(1)}, u32[]{:S(2)}, u32[]{:S(2)}) %all-to-all-start.1) | async-done | bytes 262176 | tf_op jit(solution)/shard_map/all_to_all | solution.py:348
  58.3 0.0 copy-done.2
  58.3 1.2 %shard_map.153 = f32[3,1024]{1,0:T(4,128)} custom-call(s32[8,128]{1,0:T(8,128)S(1)} %get-tuple-element.42.place_ref, f32[32,16,128]{2,1,0:T(8,128)S(1)} %all-to-all-done.1.answer_ref, f32[3,8,1024]{2,1,0:T(8,128)S(1)} %copy-done.2), custom_call_target="tpu_custom_call" | custom-call | flops 1000000 | bytes 400000 | tf_op jit(solution)/shard_map/pallas_call | solution.py:352
Async XLA Ops:
  0.6 0.7 %copy-start.3 = (f32[4096]{0:T(1024)S(1)}, f32[4096]{0:T(1024)}, u32[]{:S(2)}) copy-start(f32[4096]{0:T(1024)} %param.13) | copy-start | bytes 49156
  1.4 0.7 %copy-start.6 = (s32[4,1024]{1,0:T(4,128)S(1)}, s32[4,1024]{1,0:T(4,128)}, u32[]{:S(2)}) copy-start(s32[4,1024]{1,0:T(4,128)} %export_ref.1) | copy-start | bytes 49156
  2.1 9.5 %copy-start.9 = (s32[8,1024]{1,0:T(8,128)S(1)}, s32[8,1024]{1,0:T(8,128)}, u32[]{:S(2)}) copy-start(s32[8,1024]{1,0:T(8,128)} %refs_1_.3) | copy-start | bytes 98308
  2.5 13.1 %collective-permute-start = (f32[8,128]{1,0:T(8,128)S(1)}, f32[8,128]{1,0:T(8,128)S(1)}, u32[]{:S(2)}, u32[]{:S(2)}) collective-permute-start(f32[8,128]{1,0:T(8,128)S(1)} %get-tuple-element.24), channel_id=1, source_target_pairs={{0,1},{1,0},{2,3},{3,2},{4,5},{5,4},{6,7},{7,6},{8,9},{9,8},{10,11... | collective-permute-start | bytes 12296 | tf_op jit(solution)/shard_map/ppermute | solution.py:271
  5.8 5.8 %copy-start.14 = (f32[1024]{0:T(1024)S(1)}, f32[1024]{0:T(1024)}, u32[]{:S(2)}) copy-start(f32[1024]{0:T(1024)} %param.21) | copy-start | bytes 12292
  5.8 5.8 %copy-start.13 = (s32[1024]{0:T(1024)S(1)}, s32[1024]{0:T(1024)}, u32[]{:S(2)}) copy-start(s32[1024]{0:T(1024)} %param.22) | copy-start | bytes 12292
  5.8 9.8 %collective-permute-start.1 = (f32[8,128]{1,0:T(8,128)S(1)}, f32[8,128]{1,0:T(8,128)S(1)}, u32[]{:S(2)}, u32[]{:S(2)}) collective-permute-start(f32[8,128]{1,0:T(8,128)S(1)} %get-tuple-element.25), channel_id=1, source_target_pairs={{0,31},{1,2},{2,1},{3,4},{4,3},{5,6},{6,5},{7,8},{8,7},{9,10},{10,... | collective-permute-start | bytes 12296 | tf_op jit(solution)/shard_map/ppermute | solution.py:269
  5.8 9.8 %collective-permute-start.2 = (f32[8,128]{1,0:T(8,128)S(1)}, f32[8,128]{1,0:T(8,128)S(1)}, u32[]{:S(2)}, u32[]{:S(2)}) collective-permute-start(f32[8,128]{1,0:T(8,128)S(1)} %get-tuple-element.26), channel_id=1, source_target_pairs={{0,32},{32,0},{64,96},{96,64},{128,160},{160,128},{192,224},{224,1... | collective-permute-start | bytes 12296 | tf_op jit(solution)/shard_map/ppermute | solution.py:273
  6.9 8.7 %collective-permute-start.3 = (f32[8,128]{1,0:T(8,128)S(1)}, f32[8,128]{1,0:T(8,128)S(1)}, u32[]{:S(2)}, u32[]{:S(2)}) collective-permute-start(f32[8,128]{1,0:T(8,128)S(1)} %get-tuple-element.27), channel_id=1, source_target_pairs={{0,224},{32,64},{64,32},{96,128},{128,96},{160,192},{192,160},{224... | collective-permute-start | bytes 12296 | tf_op jit(solution)/shard_map/ppermute | solution.py:274
  11.6 0.8 %copy-start.10 = (f32[8,1024]{1,0:T(8,128)S(1)}, f32[8,1024]{1,0:T(8,128)}, u32[]{:S(2)}) copy-start(f32[8,1024]{1,0:T(8,128)} %refs_2_.1) | copy-start | bytes 98308
  12.4 0.7 %copy-start.11 = (f32[3,1024]{1,0:T(4,128)S(1)}, f32[3,1024]{1,0:T(4,128)}, u32[]{:S(2)}) copy-start(f32[3,1024]{1,0:T(4,128)} %refs_3_.1) | copy-start | bytes 36868
  15.7 8.4 %copy-start = (f32[6,4096]{1,0:T(8,128)S(1)}, f32[6,4096]{1,0:T(8,128)}, u32[]{:S(2)}) copy-start(f32[6,4096]{1,0:T(8,128)} %coeff_ref.3) | copy-start | bytes 294916
  15.7 8.4 %copy-start.1 = (s32[6,4096]{1,0:T(8,128)S(1)}, s32[6,4096]{1,0:T(8,128)}, u32[]{:S(2)}) copy-start(s32[6,4096]{1,0:T(8,128)} %neighbour_ref.3) | copy-start | bytes 294916
  15.7 8.4 %copy-start.4 = (f32[4096]{0:T(1024)S(1)}, f32[4096]{0:T(1024)}, u32[]{:S(2)}) copy-start(f32[4096]{0:T(1024)} %param.13) | copy-start | bytes 49156
  15.7 8.4 %copy-start.5 = (f32[4096]{0:T(1024)S(1)}, f32[4096]{0:T(1024)}, u32[]{:S(2)}) copy-start(f32[4096]{0:T(1024)} %param.15) | copy-start | bytes 49156
  15.7 8.4 %copy-start.7 = (s32[4,1024]{1,0:T(4,128)S(1)}, s32[4,1024]{1,0:T(4,128)}, u32[]{:S(2)}) copy-start(s32[4,1024]{1,0:T(4,128)} %export_ref.1) | copy-start | bytes 49156
  15.7 8.4 %copy-start.12 = (f32[4096]{0:T(1024)S(1)}, f32[4096]{0:T(1024)}, u32[]{:S(2)}) copy-start(f32[4096]{0:T(1024)} %param.14) | copy-start | bytes 49156
  15.7 18.6 %all-to-all-start = ((f32[32,24,128]{2,1,0:T(8,128)}), f32[32,24,128]{2,1,0:T(8,128)S(1)}, u32[]{:S(2)}, u32[]{:S(2)}) async-start(f32[32,24,128]{2,1,0:T(8,128)} %get-tuple-element.39), calls=%async_computation | async-start | bytes 786432 | tf_op jit(solution)/shard_map/all_to_all | solution.py:337
  24.2 10.2 %copy-start.8 = (f32[3,4096]{1,0:T(4,128)S(1)}, f32[3,4096]{1,0:T(4,128)}, u32[]{:S(2)}) copy-start(f32[3,4096]{1,0:T(4,128)} %fluid_ref.1) | copy-start | bytes 147460
  28.5 9.4 %collective-permute-start.4 = (f32[8,128]{1,0:T(8,128)S(1)}, f32[8,128]{1,0:T(8,128)S(1)}, u32[]{:S(2)}, u32[]{:S(2)}) collective-permute-start(f32[8,128]{1,0:T(8,128)S(1)} %get-tuple-element.34), channel_id=1, source_target_pairs={{0,1},{1,0},{2,3},{3,2},{4,5},{5,4},{6,7},{7,6},{8,9},{9,8},{10,11... | collective-permute-start | bytes 12296 | tf_op jit(solution)/shard_map/ppermute | solution.py:271
  28.9 8.9 %collective-permute-start.5 = (f32[8,128]{1,0:T(8,128)S(1)}, f32[8,128]{1,0:T(8,128)S(1)}, u32[]{:S(2)}, u32[]{:S(2)}) collective-permute-start(f32[8,128]{1,0:T(8,128)S(1)} %get-tuple-element.35), channel_id=1, source_target_pairs={{0,31},{1,2},{2,1},{3,4},{4,3},{5,6},{6,5},{7,8},{8,7},{9,10},{10,... | collective-permute-start | bytes 12296 | tf_op jit(solution)/shard_map/ppermute | solution.py:269
  30.4 7.5 %collective-permute-start.6 = (f32[8,128]{1,0:T(8,128)S(1)}, f32[8,128]{1,0:T(8,128)S(1)}, u32[]{:S(2)}, u32[]{:S(2)}) collective-permute-start(f32[8,128]{1,0:T(8,128)S(1)} %get-tuple-element.36), channel_id=1, source_target_pairs={{0,32},{32,0},{64,96},{96,64},{128,160},{160,128},{192,224},{224,1... | collective-permute-start | bytes 12296 | tf_op jit(solution)/shard_map/ppermute | solution.py:273
  30.4 7.5 %collective-permute-start.7 = (f32[8,128]{1,0:T(8,128)S(1)}, f32[8,128]{1,0:T(8,128)S(1)}, u32[]{:S(2)}, u32[]{:S(2)}) collective-permute-start(f32[8,128]{1,0:T(8,128)S(1)} %get-tuple-element.37), channel_id=1, source_target_pairs={{0,224},{32,64},{64,32},{96,128},{128,96},{160,192},{192,160},{224... | collective-permute-start | bytes 12296 | tf_op jit(solution)/shard_map/ppermute | solution.py:274
  43.8 14.4 %all-to-all-start.1 = ((f32[32,16,128]{2,1,0:T(8,128)}), f32[32,16,128]{2,1,0:T(8,128)S(1)}, u32[]{:S(2)}, u32[]{:S(2)}) async-start(f32[32,16,128]{2,1,0:T(8,128)} %get-tuple-element.43), calls=%async_computation.1 | async-start | bytes 524288 | tf_op jit(solution)/shard_map/all_to_all | solution.py:348
  49.2 9.0 %copy-start.2 = (f32[3,8,1024]{2,1,0:T(8,128)S(1)}, f32[3,8,1024]{2,1,0:T(8,128)}, u32[]{:S(2)}) copy-start(f32[3,8,1024]{2,1,0:T(8,128)} %grad_ref.1) | copy-start | bytes 294916

commit v3 on v2

--- a/solution.py
+++ b/solution.py
@@ -70,7 +70,9 @@
         outs[d + 1][...] = jnp.where(even, face_ref[d + 1], face_ref[d])
 
 
-def export_kernel(field_ref, export_ref, out0, out1, out2, out3, face_ref):
+def export_kernel(ready, field_ref, export_ref, out0, out1, out2, out3, face_ref):
+    ready(0)
+    ready(1)
     write_exports(field_ref, export_ref, face_ref, (out0, out1, out2, out3))
 
 
@@ -87,14 +89,11 @@
         halo_ref[d * FACE_ROWS : (d + 1) * FACE_ROWS, :] = below
         halo_ref[(d + 1) * FACE_ROWS : (d + 2) * FACE_ROWS, :] = above
     table = rows_of(vector_ref, ROWS) + rows_of(halo_ref, 4 * FACE_ROWS)
-    for t in range(0, ROWS, 4):
-        cuts = [slice(u * LANES, (u + 1) * LANES) for u in range(t, t + 4)]
-        (found,) = look_up([table], jnp.concatenate([neighbour_ref[:, cut] for cut in cuts], axis=0))
-        for u, cut in enumerate(cuts):
-            part = coeff_ref[:, cut] * found[NBR * u : NBR * (u + 1)]
-            linked = jnp.sum(part, axis=0, keepdims=True)
-            row = slice(t + u, t + u + 1)
-            out_ref[row, :] = diagonal_ref[row, :] * vector_ref[row, :] - linked
+    for t in range(ROWS):
+        cut, row = slice(t * LANES, (t + 1) * LANES), slice(t, t + 1)
+        (found,) = look_up([table], neighbour_ref[:, cut])
+        linked = jnp.sum(coeff_ref[:, cut] * found, axis=0, keepdims=True)
+        out_ref[row, :] = diagonal_ref[row, :] * vector_ref[row, :] - linked
 
 
 def first_kernel(
@@ -131,7 +130,10 @@
         answer_ref[s, 8:16, :] = moved_ref[s]
 
 
-def slot_kernel(owner_ref, cells_ref, weight_ref, velocity_ref, rate_ref, place_ref, sent_ref):
+def slot_kernel(
+    ready, owner_ref, cells_ref, weight_ref, velocity_ref, rate_ref, place_ref, sent_ref
+):
+    ready(0)
     owners = lax.broadcasted_iota(I32, (OWNERS, LANES), 0)
     lanes = lax.broadcasted_iota(I32, (OWNERS, LANES), 1)
     chosen = [owners == wide(owner_ref[j : j + 1, :], OWNERS) for j in range(CHUNKS)]
@@ -162,6 +164,8 @@
         jnp.concatenate([lane_of, chunk_of], axis=0), at_rank, (((1,), (1,)), ((), ())),
         preferred_element_type=F32,
     ).astype(I32)
+    for i in range(1, 5):
+        ready(i)
     for o in range(OWNERS):
         low = wide(found[o : o + 1], 8)
         high = wide(found[OWNERS + o : OWNERS + o + 1], 8)
@@ -257,21 +261,22 @@
     return jax.ShapeDtypeStruct(dims, dtype)
 
 
-def pairs(count):
-    first = [(i, i ^ 1) for i in range(count)]
-    second = [(i, (i - 1) % count if i % 2 == 0 else (i + 1) % count) for i in range(count)]
-    return first, second
-
-
 def exchange(faces):
-    dom_first, dom_second = pairs(lax.axis_size("dom"))
-    group_first, group_second = pairs(lax.axis_size("group"))
-    far = lax.ppermute(faces[1], "dom", dom_second)
+    groups, count = lax.axis_size("group"), lax.axis_size("dom")
+    near = [(m, m ^ 1) for m in range(count)]
+    far = [(m, (m - 1 if m % 2 == 0 else m + 1) % count) for m in range(count)]
+    over = [(g, g ^ 1) for g in range(groups)]
+    under = []
+    for g in range(groups):
+        to = g - 1 if g % 2 == 0 else g + 1
+        for m in range(count):
+            inside = 0 <= to < groups
+            under.append((g * count + m, to * count + m if inside else g * count + (m ^ 1)))
     return (
-        lax.ppermute(faces[0], "dom", dom_first),
-        far,
-        lax.ppermute(faces[2], "group", group_first),
-        lax.ppermute(faces[3], "group", group_second),
+        lax.ppermute(faces[0], "dom", near),
+        lax.ppermute(faces[1], "dom", far),
+        lax.ppermute(faces[2], "group", over),
+        lax.ppermute(faces[3], ("group", "dom"), under),
     )
 
 
@@ -296,9 +301,7 @@
         ]
         for copy in copies:
             copy.start()
-        for copy in copies:
-            copy.wait()
-        kernel(*local, *refs[count : -1 - count])
+        kernel(lambda i: copies[i].wait(), *local, *refs[count : -1 - count])
 
     scratch = (
         *scratch,
@@ -306,6 +309,7 @@
         pltpu.SemaphoreType.DMA((count,)),
     )
     specs = [pl.BlockSpec(memory_space=pltpu.HBM)] * count
+    operands = [pltpu.with_memory_space_constraint(x, pltpu.HBM) for x in operands]
     return call(run, outs, flops, scratch, in_specs=specs)(*operands)
 
 

time: 60.1 us -> 53.4 us (0.89)
  the two profiles are of different devices: /device:TPU:1 before, /device:TPU:33 now
where the time goes in v3:
time: 53.4 us; the launch traced here: 52.9 us
  starting transfers between devices  25 us (47%)
  Pallas kernels  20.2 us (38%)
  waiting for transfers between devices  6.89 us (13%)
  between operations  0.85 us (2%)
    all_to_all x1, starting transfers between devices, per_device(): lax.all_to_all(sent, 'dom', split_axis=0, concat_axis=0, tiled=True)  8.36 us
    ppermute x2, starting transfers between devices, exchange(): lax.ppermute(faces[3], ('group', 'dom'), under)  6.49 us
    all_to_all x1, starting transfers between devices, per_device(): lax.all_to_all(answer, 'dom', split_axis=0, concat_axis=0, tiled=True)  5.9 us
    all_to_all x1, waiting for transfers between devices, per_device(): lax.all_to_all(answer, 'dom', split_axis=0, concat_axis=0, tiled=True)  4.82 us
    pallas_call x1, Pallas kernels, per_device(): call(second_kernel, (field, shape(OWNERS, 16, CAP)), 10 ** 8, halo)  4.29 us
    pallas_call x2, Pallas kernels, staged(): return call(run, outs, flops, scratch, in_specs=specs)(*operands)  4.26 us
    pallas_call x1, Pallas kernels, per_device(): call(scatter_kernel, shape(3, CELLS), 2 * 10 ** 9, (pltpu.VMEM((6 * ROWS,...  4.18 us
    pallas_call x1, Pallas kernels, per_device(): call(fluid_kernel, (shape(OWNERS, 8, CAP), shape(OWNERS, 4, CAP)), 10 ** 9)  3.48 us
  transfers between devices with their start and end apart: 10, of which 2 were waited for; matrix products, arithmetic and copies ran while one was open for 0% of the time, Pallas kernels for 26%

profile of v3, /device:TPU:33, one launch (start us, length us, event | category | flops | bytes accessed | tf_op | source)
XLA Modules:
  0.0 52.9 jit_solution(16608599761352804519)
XLA Ops:
  0.6 1.1 %shard_map.148 = (f32[8,128]{1,0:T(8,128)S(1)}, f32[8,128]{1,0:T(8,128)S(1)}, f32[8,128]{1,0:T(8,128)S(1)}, f32[8,128]{1,0:T(8,128)S(1)}) custom-call(f32[32,128]{1,0:T(8,128)} %bitcast.6, s32[4,1024]{1,0:T(4,128)} %export_ref.1), custom_call_target="tpu_custom_call" | custom-call | flops 1000000 | bytes 400000 | tf_op jit(solution)/shard_map/pallas_call | solution.py:313
  1.8 0.8 %collective-permute-start = (f32[8,128]{1,0:T(8,128)S(1)}, f32[8,128]{1,0:T(8,128)S(1)}, u32[]{:S(2)}, u32[]{:S(2)}) collective-permute-start(f32[8,128]{1,0:T(8,128)S(1)} %get-tuple-element.24), channel_id=1, source_target_pairs={{0,1},{1,0},{2,3},{3,2},{4,5},{5,4},{6,7},{7,6},{8,9},{9,8},{10,11... | collective-permute-start | bytes 12296 | tf_op jit(solution)/shard_map/ppermute | solution.py:276
  2.5 1.2 %collective-permute-start.1 = (f32[8,128]{1,0:T(8,128)S(1)}, f32[8,128]{1,0:T(8,128)S(1)}, u32[]{:S(2)}, u32[]{:S(2)}) collective-permute-start(f32[8,128]{1,0:T(8,128)S(1)} %get-tuple-element.25), channel_id=1, source_target_pairs={{0,31},{1,2},{2,1},{3,4},{4,3},{5,6},{6,5},{7,8},{8,7},{9,10},{10,... | collective-permute-start | bytes 12296 | tf_op jit(solution)/shard_map/ppermute | solution.py:277
  3.7 0.4 collective-permute-start.2
  4.1 2.9 %collective-permute-start.3 = (f32[8,128]{1,0:T(8,128)S(1)}, f32[8,128]{1,0:T(8,128)S(1)}, u32[]{:S(2)}, u32[]{:S(2)}) collective-permute-start(f32[8,128]{1,0:T(8,128)S(1)} %get-tuple-element.27), channel_id=1, source_target_pairs={{0,1},{1,0},{2,3},{3,2},{4,5},{5,4},{6,7},{7,6},{8,9},{9,8},{10,11... | collective-permute-start | bytes 12296 | tf_op jit(solution)/shard_map/ppermute | solution.py:279
  7.0 3.1 %shard_map.149 = (s32[8,128]{1,0:T(8,128)S(1)}, f32[32,24,128]{2,1,0:T(8,128)}) custom-call(s32[8,128]{1,0:T(8,128)} %bitcast.13, s32[8,1024]{1,0:T(8,128)} %refs_1_.3, f32[8,1024]{1,0:T(8,128)} %refs_2_.1, f32[3,1024]{1,0:T(4,128)} %refs_3_.1, f32[8,128]{1,0:T(8,128)} %bitcast.14), custom_call_target="tpu_custom_call" | custom-call | flops 100000000 | bytes 400000 | tf_op jit(solution)/shard_map/pallas_call | solution.py:313
  10.1 0.0 collective-permute-done.got0
  10.2 0.0 collective-permute-done.1.got1
  10.2 0.0 collective-permute-done.2.got2
  10.2 0.0 collective-permute-done.3.got3
  10.2 0.0 copy-start
  10.2 0.0 copy-start.1
  10.2 0.0 copy-start.3
  10.2 0.0 copy-start.4
  10.2 0.0 copy-start.5
  10.2 0.0 copy-start.7
  10.3 8.4 %all-to-all-start = ((f32[32,24,128]{2,1,0:T(8,128)}), f32[32,24,128]{2,1,0:T(8,128)S(1)}, u32[]{:S(2)}, u32[]{:S(2)}) async-start(f32[32,24,128]{2,1,0:T(8,128)} %get-tuple-element.39), calls=%async_computation | async-start | bytes 786432 | tf_op jit(solution)/shard_map/all_to_all | solution.py:341
  18.6 0.0 copy-done
  18.6 0.0 copy-done.1
  18.6 0.0 copy-done.3
  18.7 0.0 copy-done.4
  18.7 0.0 copy-done.5
  18.7 0.0 copy-done.7
  18.7 0.0 copy-start.6
  18.7 2.7 %shard_map.150 = (f32[32,128]{1,0:T(8,128)S(1)}, f32[32,128]{1,0:T(8,128)S(1)}, f32[8,128]{1,0:T(8,128)S(1)}, f32[8,128]{1,0:T(8,128)S(1)}, f32[8,128]{1,0:T(8,128)S(1)}, /*index=5*/f32[8,128]{1,0:T(8,128)S(1)}) custom-call(f32[32,128]{1,0:T(8,128)S(1)} %bitcast.7, f32[8,128]{1,0:T(8,128)S(1)} %collective-permute-done.got0, ...), custom_call_target="tpu_custom_call" | custom-call | flops 100000000 | bytes 400000 | tf_op jit(solution)/shard_map/pallas_call | solution.py:342
  21.4 0.4 collective-permute-start.4
  21.8 1.4 %collective-permute-start.5 = (f32[8,128]{1,0:T(8,128)S(1)}, f32[8,128]{1,0:T(8,128)S(1)}, u32[]{:S(2)}, u32[]{:S(2)}) collective-permute-start(f32[8,128]{1,0:T(8,128)S(1)} %get-tuple-element.35), channel_id=1, source_target_pairs={{0,31},{1,2},{2,1},{3,4},{4,3},{5,6},{6,5},{7,8},{8,7},{9,10},{10,... | collective-permute-start | bytes 12296 | tf_op jit(solution)/shard_map/ppermute | solution.py:277
  23.3 0.0 collective-permute-start.6
  23.3 3.6 %collective-permute-start.7 = (f32[8,128]{1,0:T(8,128)S(1)}, f32[8,128]{1,0:T(8,128)S(1)}, u32[]{:S(2)}, u32[]{:S(2)}) collective-permute-start(f32[8,128]{1,0:T(8,128)S(1)} %get-tuple-element.37), channel_id=1, source_target_pairs={{0,1},{1,0},{2,3},{3,2},{4,5},{5,4},{6,7},{7,6},{8,9},{9,8},{10,11... | collective-permute-start | bytes 12296 | tf_op jit(solution)/shard_map/ppermute | solution.py:279
  26.9 2.1 %all-to-all-done.parcel_ref = f32[32,24,128]{2,1,0:T(8,128)S(1)} async-done(((f32[32,24,128]{2,1,0:T(8,128)}), f32[32,24,128]{2,1,0:T(8,128)S(1)}, u32[]{:S(2)}, u32[]{:S(2)}) %all-to-all-start) | async-done | bytes 393248 | tf_op jit(solution)/shard_map/all_to_all | solution.py:341
  28.9 0.0 copy-done.6
  28.9 3.5 %shard_map.151 = (f32[32,8,128]{2,1,0:T(8,128)S(1)}, f32[32,4,128]{2,1,0:T(4,128)S(1)}) custom-call(f32[3,4096]{1,0:T(4,128)S(1)} %copy-done.6, f32[32,24,128]{2,1,0:T(8,128)S(1)} %all-to-all-done.parcel_ref), custom_call_target="tpu_custom_call" | custom-call | flops 1000000000 | bytes 400000 | tf_op jit(solution)/shard_map/pallas_call | solution.py:346
  32.4 0.0 collective-permute-done.4.got0
  32.4 0.0 collective-permute-done.5.got1
  32.4 0.0 collective-permute-done.6.got2
  32.4 0.0 collective-permute-done.7.got3
  32.4 4.3 %shard_map.152 = (f32[32,128]{1,0:T(8,128)}, f32[32,16,128]{2,1,0:T(8,128)}) custom-call(f32[32,128]{1,0:T(8,128)S(1)} %get-tuple-element.33.direction_ref, f32[8,128]{1,0:T(8,128)S(1)} %collective-permute-done.4.got0, f32[8,128]{1,0:T(8,128)S(1)} %collective-permute-done.5.got1, f32[8,128]{1,0:T(8,128)S(1)} %collective-permute-done.6.got2, ...), custom_call_target="tpu_custom_call" | custom-call | flops 100000000 | bytes 400000 | tf_op jit(solution)/shard_map/pallas_call | solution.py:349
  36.7 5.9 %all-to-all-start.1 = ((f32[32,16,128]{2,1,0:T(8,128)}), f32[32,16,128]{2,1,0:T(8,128)S(1)}, u32[]{:S(2)}, u32[]{:S(2)}) async-start(f32[32,16,128]{2,1,0:T(8,128)} %get-tuple-element.43), calls=%async_computation.1 | async-start | bytes 524288 | tf_op jit(solution)/shard_map/all_to_all | solution.py:352
  42.6 0.0 copy-start.2
  42.7 4.2 %shard_map.154 = f32[3,4096]{1,0:T(4,128)} custom-call(f32[32,24,128]{2,1,0:T(8,128)S(1)} %all-to-all-done.parcel_ref, f32[32,4,128]{2,1,0:T(4,128)S(1)} %get-tuple-element.44.force_ref), custom_call_target="tpu_custom_call" | custom-call | flops 2000000000 | bytes 400000 | tf_op jit(solution)/shard_map/pallas_call | solution.py:353
  46.8 4.8 %all-to-all-done.1.answer_ref = f32[32,16,128]{2,1,0:T(8,128)S(1)} async-done(((f32[32,16,128]{2,1,0:T(8,128)}), f32[32,16,128]{2,1,0:T(8,128)S(1)}, u32[]{:S(2)}, u32[]{:S(2)}) %all-to-all-start.1) | async-done | bytes 262176 | tf_op jit(solution)/shard_map/all_to_all | solution.py:352
  51.7 0.0 copy-done.2
  51.7 1.2 %shard_map.153 = f32[3,1024]{1,0:T(4,128)} custom-call(s32[8,128]{1,0:T(8,128)S(1)} %get-tuple-element.42.place_ref, f32[32,16,128]{2,1,0:T(8,128)S(1)} %all-to-all-done.1.answer_ref, f32[3,8,1024]{2,1,0:T(8,128)S(1)} %copy-done.2), custom_call_target="tpu_custom_call" | custom-call | flops 1000000 | bytes 400000 | tf_op jit(solution)/shard_map/pallas_call | solution.py:356
Async XLA Ops:
  1.8 8.4 %collective-permute-start = (f32[8,128]{1,0:T(8,128)S(1)}, f32[8,128]{1,0:T(8,128)S(1)}, u32[]{:S(2)}, u32[]{:S(2)}) collective-permute-start(f32[8,128]{1,0:T(8,128)S(1)} %get-tuple-element.24), channel_id=1, source_target_pairs={{0,1},{1,0},{2,3},{3,2},{4,5},{5,4},{6,7},{7,6},{8,9},{9,8},{10,11... | collective-permute-start | bytes 12296 | tf_op jit(solution)/shard_map/ppermute | solution.py:276
  2.5 7.6 %collective-permute-start.1 = (f32[8,128]{1,0:T(8,128)S(1)}, f32[8,128]{1,0:T(8,128)S(1)}, u32[]{:S(2)}, u32[]{:S(2)}) collective-permute-start(f32[8,128]{1,0:T(8,128)S(1)} %get-tuple-element.25), channel_id=1, source_target_pairs={{0,31},{1,2},{2,1},{3,4},{4,3},{5,6},{6,5},{7,8},{8,7},{9,10},{10,... | collective-permute-start | bytes 12296 | tf_op jit(solution)/shard_map/ppermute | solution.py:277
  3.7 6.4 %collective-permute-start.2 = (f32[8,128]{1,0:T(8,128)S(1)}, f32[8,128]{1,0:T(8,128)S(1)}, u32[]{:S(2)}, u32[]{:S(2)}) collective-permute-start(f32[8,128]{1,0:T(8,128)S(1)} %get-tuple-element.26), channel_id=1, source_target_pairs={{0,32},{32,0},{64,96},{96,64},{128,160},{160,128},{192,224},{224,1... | collective-permute-start | bytes 12296 | tf_op jit(solution)/shard_map/ppermute | solution.py:278
  4.1 6.1 %collective-permute-start.3 = (f32[8,128]{1,0:T(8,128)S(1)}, f32[8,128]{1,0:T(8,128)S(1)}, u32[]{:S(2)}, u32[]{:S(2)}) collective-permute-start(f32[8,128]{1,0:T(8,128)S(1)} %get-tuple-element.27), channel_id=1, source_target_pairs={{0,1},{1,0},{2,3},{3,2},{4,5},{5,4},{6,7},{7,6},{8,9},{9,8},{10,11... | collective-permute-start | bytes 12296 | tf_op jit(solution)/shard_map/ppermute | solution.py:279
  10.2 8.4 %copy-start = (f32[6,4096]{1,0:T(8,128)S(1)}, f32[6,4096]{1,0:T(8,128)}, u32[]{:S(2)}) copy-start(f32[6,4096]{1,0:T(8,128)} %coeff_ref.3) | copy-start | bytes 294916
  10.2 8.4 %copy-start.1 = (s32[6,4096]{1,0:T(8,128)S(1)}, s32[6,4096]{1,0:T(8,128)}, u32[]{:S(2)}) copy-start(s32[6,4096]{1,0:T(8,128)} %neighbour_ref.3) | copy-start | bytes 294916
  10.2 8.4 %copy-start.3 = (f32[4096]{0:T(1024)S(1)}, f32[4096]{0:T(1024)}, u32[]{:S(2)}) copy-start(f32[4096]{0:T(1024)} %param.13) | copy-start | bytes 49156
  10.2 8.4 %copy-start.4 = (f32[4096]{0:T(1024)S(1)}, f32[4096]{0:T(1024)}, u32[]{:S(2)}) copy-start(f32[4096]{0:T(1024)} %param.15) | copy-start | bytes 49156
  10.2 8.4 %copy-start.5 = (s32[4,1024]{1,0:T(4,128)S(1)}, s32[4,1024]{1,0:T(4,128)}, u32[]{:S(2)}) copy-start(s32[4,1024]{1,0:T(4,128)} %export_ref.1) | copy-start | bytes 49156
  10.2 8.4 %copy-start.7 = (f32[4096]{0:T(1024)S(1)}, f32[4096]{0:T(1024)}, u32[]{:S(2)}) copy-start(f32[4096]{0:T(1024)} %param.14) | copy-start | bytes 49156
  10.3 18.7 %all-to-all-start = ((f32[32,24,128]{2,1,0:T(8,128)}), f32[32,24,128]{2,1,0:T(8,128)S(1)}, u32[]{:S(2)}, u32[]{:S(2)}) async-start(f32[32,24,128]{2,1,0:T(8,128)} %get-tuple-element.39), calls=%async_computation | async-start | bytes 786432 | tf_op jit(solution)/shard_map/all_to_all | solution.py:341
  18.7 10.2 %copy-start.6 = (f32[3,4096]{1,0:T(4,128)S(1)}, f32[3,4096]{1,0:T(4,128)}, u32[]{:S(2)}) copy-start(f32[3,4096]{1,0:T(4,128)} %fluid_ref.1) | copy-start | bytes 147460
  21.4 11.0 %collective-permute-start.4 = (f32[8,128]{1,0:T(8,128)S(1)}, f32[8,128]{1,0:T(8,128)S(1)}, u32[]{:S(2)}, u32[]{:S(2)}) collective-permute-start(f32[8,128]{1,0:T(8,128)S(1)} %get-tuple-element.34), channel_id=1, source_target_pairs={{0,1},{1,0},{2,3},{3,2},{4,5},{5,4},{6,7},{7,6},{8,9},{9,8},{10,11... | collective-permute-start | bytes 12296 | tf_op jit(solution)/shard_map/ppermute | solution.py:276
  21.8 10.6 %collective-permute-start.5 = (f32[8,128]{1,0:T(8,128)S(1)}, f32[8,128]{1,0:T(8,128)S(1)}, u32[]{:S(2)}, u32[]{:S(2)}) collective-permute-start(f32[8,128]{1,0:T(8,128)S(1)} %get-tuple-element.35), channel_id=1, source_target_pairs={{0,31},{1,2},{2,1},{3,4},{4,3},{5,6},{6,5},{7,8},{8,7},{9,10},{10,... | collective-permute-start | bytes 12296 | tf_op jit(solution)/shard_map/ppermute | solution.py:277
  23.3 9.2 %collective-permute-start.6 = (f32[8,128]{1,0:T(8,128)S(1)}, f32[8,128]{1,0:T(8,128)S(1)}, u32[]{:S(2)}, u32[]{:S(2)}) collective-permute-start(f32[8,128]{1,0:T(8,128)S(1)} %get-tuple-element.36), channel_id=1, source_target_pairs={{0,32},{32,0},{64,96},{96,64},{128,160},{160,128},{192,224},{224,1... | collective-permute-start | bytes 12296 | tf_op jit(solution)/shard_map/ppermute | solution.py:278
  23.3 9.2 %collective-permute-start.7 = (f32[8,128]{1,0:T(8,128)S(1)}, f32[8,128]{1,0:T(8,128)S(1)}, u32[]{:S(2)}, u32[]{:S(2)}) collective-permute-start(f32[8,128]{1,0:T(8,128)S(1)} %get-tuple-element.37), channel_id=1, source_target_pairs={{0,1},{1,0},{2,3},{3,2},{4,5},{5,4},{6,7},{7,6},{8,9},{9,8},{10,11... | collective-permute-start | bytes 12296 | tf_op jit(solution)/shard_map/ppermute | solution.py:279
  36.7 14.9 %all-to-all-start.1 = ((f32[32,16,128]{2,1,0:T(8,128)}), f32[32,16,128]{2,1,0:T(8,128)S(1)}, u32[]{:S(2)}, u32[]{:S(2)}) async-start(f32[32,16,128]{2,1,0:T(8,128)} %get-tuple-element.43), calls=%async_computation.1 | async-start | bytes 524288 | tf_op jit(solution)/shard_map/all_to_all | solution.py:352
  42.6 9.0 %copy-start.2 = (f32[3,8,1024]{2,1,0:T(8,128)S(1)}, f32[3,8,1024]{2,1,0:T(8,128)}, u32[]{:S(2)}) copy-start(f32[3,8,1024]{2,1,0:T(8,128)} %grad_ref.1) | copy-start | bytes 294916

commit v4 on v3

--- a/solution.py
+++ b/solution.py
@@ -24,6 +24,8 @@
 OWNERS = 32
 CAP = 128
 SENT = 24
+BACK = 16
+PART = 8
 
 F32 = jnp.float32
 BF16 = jnp.bfloat16
@@ -64,25 +66,39 @@
         (found,) = look_up([rows_of(field_ref, ROWS)], index)
         for d in range(4):
             face_ref[d, t : t + 1, :] = found[d : d + 1]
-    for axis, d in (("dom", 0), ("group", 2)):
+    for axis, d, first, second in (("dom", 0, outs[3], outs[0]), ("group", 2, outs[2], outs[1])):
         even = is_even(axis)
-        outs[d][...] = jnp.where(even, face_ref[d], face_ref[d + 1])
-        outs[d + 1][...] = jnp.where(even, face_ref[d + 1], face_ref[d])
-
-
-def export_kernel(ready, field_ref, export_ref, out0, out1, out2, out3, face_ref):
-    ready(0)
-    ready(1)
-    write_exports(field_ref, export_ref, face_ref, (out0, out1, out2, out3))
+        first[...] = jnp.where(even, face_ref[d], face_ref[d + 1])
+        second[...] = jnp.where(even, face_ref[d + 1], face_ref[d])
+
+
+def export_kernel(*refs):
+    (field_hbm, export_hbm), passed = refs[:2], refs[2:7]
+    outs, passed_on = refs[7:11], refs[11:16]
+    face_ref, field_ref, export_ref, sems = refs[16:]
+    sources = (field_hbm, export_hbm) + passed
+    targets = (field_ref, export_ref) + passed_on
+    copies = [
+        pltpu.make_async_copy(source, target, sems.at[i])
+        for i, (source, target) in enumerate(zip(sources, targets))
+    ]
+    for copy in copies:
+        copy.start()
+    copies[0].wait()
+    copies[1].wait()
+    write_exports(field_ref, export_ref, face_ref, outs)
+    for copy in copies[2:]:
+        copy.wait()
 
 
 def multiply(vector_ref, got_refs, diagonal_ref, coeff_ref, neighbour_ref, halo_ref, out_ref):
     group = lax.axis_index("group")
     last = lax.axis_size("group") - 1
-    for axis, d in (("dom", 0), ("group", 2)):
+    far, under, over, near = got_refs
+    for axis, d, first, second in (("dom", 0, near, far), ("group", 2, over, under)):
         even = is_even(axis)
-        below = jnp.where(even, got_refs[d + 1][...], got_refs[d][...])
-        above = jnp.where(even, got_refs[d][...], got_refs[d + 1][...])
+        below = jnp.where(even, second[...], first[...])
+        above = jnp.where(even, first[...], second[...])
         if axis == "group":
             below = jnp.where(group > 0, below, 0.0)
             above = jnp.where(group < last, above, 0.0)
@@ -112,7 +128,7 @@
 
 def second_kernel(
     direction_ref, got0, got1, got2, got3, pressure_ref, residual_ref, diagonal_ref, coeff_ref,
-    neighbour_ref, parcel_ref, moved_ref, out_ref, answer_ref, halo_ref, product_ref,
+    neighbour_ref, out_ref, again_ref, halo_ref, product_ref,
 ):
     multiply(
         direction_ref, (got0, got1, got2, got3), diagonal_ref, coeff_ref, neighbour_ref,
@@ -123,17 +139,18 @@
     iterate = pressure_ref[...] + direction
     direction = RHO_NEXT * RHO_FIRST * direction + (2.0 * RHO_NEXT / HALF_WIDTH) * residual
     out_ref[...] = iterate + direction
-    table = rows_of(out_ref, ROWS)
-    for s in range(OWNERS):
-        (found,) = look_up([table], parcel_ref[s, 8:16, :].astype(I32))
-        answer_ref[s, 0:8, :] = found
-        answer_ref[s, 8:16, :] = moved_ref[s]
+    again_ref[...] = iterate + direction
+
+
+def send_out(local_ref, hbm_ref, sems, part):
+    block = pl.ds(part * PART, PART)
+    return pltpu.make_async_copy(local_ref.at[block], hbm_ref.at[block], sems.at[part])
 
 
 def slot_kernel(
-    ready, owner_ref, cells_ref, weight_ref, velocity_ref, rate_ref, place_ref, sent_ref
-):
-    ready(0)
+    owner_ref, cells_ref, weight_ref, velocity_ref, rate_ref, place_ref, sent_hbm, sent_ref,
+    state_ref, sems,
+):
     owners = lax.broadcasted_iota(I32, (OWNERS, LANES), 0)
     lanes = lax.broadcasted_iota(I32, (OWNERS, LANES), 1)
     chosen = [owners == wide(owner_ref[j : j + 1, :], OWNERS) for j in range(CHUNKS)]
@@ -164,45 +181,55 @@
         jnp.concatenate([lane_of, chunk_of], axis=0), at_rank, (((1,), (1,)), ((), ())),
         preferred_element_type=F32,
     ).astype(I32)
-    for i in range(1, 5):
-        ready(i)
+    state_ref[0:3, :] = velocity_ref[...]
+    for j in range(CHUNKS):
+        state_ref[3:4, j * LANES : (j + 1) * LANES] = rate_ref[j : j + 1, :]
+    state_ref[4:8, :] = jnp.zeros((4, PARCELS), F32)
     for o in range(OWNERS):
         low = wide(found[o : o + 1], 8)
         high = wide(found[OWNERS + o : OWNERS + o + 1], 8)
         here = [high == j + 1 for j in range(CHUNKS)]
 
-        def place(ref, height=8):
-            value = jnp.zeros((height, LANES), F32)
+        def place(ref):
+            value = jnp.zeros((8, LANES), F32)
             for j in range(CHUNKS):
                 part = ref[:, j * LANES : (j + 1) * LANES].astype(F32)
-                value = jnp.where(here[j][:height], pick(part, low[:height]), value)
+                value = jnp.where(here[j], pick(part, low), value)
             return value
 
         sent_ref[o, 0:8, :] = place(weight_ref)
         sent_ref[o, 8:16, :] = place(cells_ref)
-        sent_ref[o, 16:19, :] = place(velocity_ref, 3)
-        value = jnp.zeros((8, LANES), F32)
-        for j in range(CHUNKS):
-            value = jnp.where(here[j], pick(wide(rate_ref[j : j + 1, :], 8), low), value)
-        sent_ref[o, 19:24, :] = jnp.concatenate([value[:1], jnp.zeros((4, LANES), F32)], axis=0)
-
-
-def fluid_kernel(fluid_ref, parcel_ref, moved_ref, force_ref):
+        sent_ref[o, 16:24, :] = place(state_ref)
+        if o % PART == PART - 1:
+            send_out(sent_ref, sent_hbm, sems, o // PART).start()
+    for part in range(OWNERS // PART):
+        send_out(sent_ref, sent_hbm, sems, part).wait()
+
+
+def parcel_kernel(
+    fluid_ref, pressure_ref, parcel_ref, answer_hbm, force_ref, answer_ref, sems
+):
     tables = [
         [lambda c=c, r=r: fluid_ref[c : c + 1, r * LANES : (r + 1) * LANES] for r in range(ROWS)]
         for c in range(3)
     ]
+    tables.append(rows_of(pressure_ref, ROWS))
     for s in range(OWNERS):
-        found = look_up(tables, parcel_ref[s, 8:16, :].astype(I32))
+        *found, pressure = look_up(tables, parcel_ref[s, 8:16, :].astype(I32))
+        answer_ref[s, 0:8, :] = pressure
         weights = parcel_ref[s, 0:8, :]
         rate = parcel_ref[s, 19:20, :]
         for c in range(3):
             velocity = parcel_ref[s, 16 + c : 17 + c, :]
             fluid_at = jnp.sum(weights * found[c], axis=0, keepdims=True)
-            moved_ref[s, c : c + 1, :] = velocity + rate * (fluid_at - velocity)
+            answer_ref[s, 8 + c : 9 + c, :] = velocity + rate * (fluid_at - velocity)
             force_ref[s, c : c + 1, :] = rate * (velocity - fluid_at)
-        moved_ref[s, 3:8, :] = jnp.zeros((5, LANES), F32)
+        answer_ref[s, 11:16, :] = jnp.zeros((5, LANES), F32)
         force_ref[s, 3:4, :] = jnp.zeros((1, LANES), F32)
+        if s % PART == PART - 1:
+            send_out(answer_ref, answer_hbm, sems, s // PART).start()
+    for part in range(OWNERS // PART):
+        send_out(answer_ref, answer_hbm, sems, part).wait()
 
 
 def scatter_kernel(parcel_ref, force_ref, out_ref, total_ref):
@@ -273,10 +300,10 @@
             inside = 0 <= to < groups
             under.append((g * count + m, to * count + m if inside else g * count + (m ^ 1)))
     return (
-        lax.ppermute(faces[0], "dom", near),
-        lax.ppermute(faces[1], "dom", far),
+        lax.ppermute(faces[0], "dom", far),
+        lax.ppermute(faces[1], ("group", "dom"), under),
         lax.ppermute(faces[2], "group", over),
-        lax.ppermute(faces[3], ("group", "dom"), under),
+        lax.ppermute(faces[3], "dom", near),
     )
 
 
@@ -291,28 +318,6 @@
     )
 
 
-def staged(kernel, operands, outs, flops, scratch=()):
-    count = len(operands)
-
-    def run(*refs):
-        local, sems = refs[-1 - count : -1], refs[-1]
-        copies = [
-            pltpu.make_async_copy(refs[i], local[i], sems.at[i]) for i in range(count)
-        ]
-        for copy in copies:
-            copy.start()
-        kernel(lambda i: copies[i].wait(), *local, *refs[count : -1 - count])
-
-    scratch = (
-        *scratch,
-        *(pltpu.VMEM(x.shape, x.dtype) for x in operands),
-        pltpu.SemaphoreType.DMA((count,)),
-    )
-    specs = [pl.BlockSpec(memory_space=pltpu.HBM)] * count
-    operands = [pltpu.with_memory_space_constraint(x, pltpu.HBM) for x in operands]
-    return call(run, outs, flops, scratch, in_specs=specs)(*operands)
-
-
 def per_device(
     pressure_old, source_term, diagonal, face_coeffs, neighbours, export_cells, fluid_velocity,
     parcel_velocity, drag_rate, parcel_owner, parcel_cells, interp_weights, grad_weights,
@@ -325,30 +330,46 @@
     faces_buffer = pltpu.VMEM((4, FACE_ROWS, LANES), F32)
     halo = (pltpu.VMEM((4 * FACE_ROWS, LANES), F32), pltpu.VMEM((ROWS, LANES), F32))
 
-    faces = staged(
-        export_kernel, (pressure_old, export_cells), (face,) * 4, 10**6, (faces_buffer,)
-    )
-    got = exchange(faces)
-    place, sent = staged(
-        slot_kernel,
+    kept = [
+        pltpu.with_memory_space_constraint(x, pltpu.HBM)
+        for x in (
+            pressure_old, export_cells, parcel_owner.reshape(CHUNKS, LANES), parcel_cells,
+            interp_weights, parcel_velocity, drag_rate.reshape(CHUNKS, LANES),
+        )
+    ]
+    outs = call(
+        export_kernel,
+        (face,) * 4 + tuple(shape(*x.shape, dtype=x.dtype) for x in kept[2:]),
+        10**6,
         (
-            parcel_owner.reshape(CHUNKS, LANES), parcel_cells, interp_weights, parcel_velocity,
-            drag_rate.reshape(CHUNKS, LANES),
+            faces_buffer, pltpu.VMEM((ROWS, LANES), F32), pltpu.VMEM((4, FACE), I32),
+            pltpu.SemaphoreType.DMA((len(kept),)),
         ),
-        (shape(CHUNKS, LANES, dtype=I32), shape(OWNERS, SENT, CAP)), 10**8,
-    )
+        in_specs=[pl.BlockSpec(memory_space=pltpu.HBM)] * len(kept),
+    )(*kept)
+    got = exchange(outs[:4])
+    whole = pl.BlockSpec(memory_space=pltpu.VMEM)
+    outside = pl.BlockSpec(memory_space=pl.ANY)
+    parts = pltpu.SemaphoreType.DMA((OWNERS // PART,))
+    place, sent = call(
+        slot_kernel, (shape(CHUNKS, LANES, dtype=I32), shape(OWNERS, SENT, CAP)), 10**8,
+        (pltpu.VMEM((OWNERS, SENT, CAP), F32), pltpu.VMEM((8, PARCELS), F32), parts),
+        out_specs=(whole, outside),
+    )(*outs[4:])
     got, sent = lax.optimization_barrier((got, sent))
     parcels = lax.all_to_all(sent, "dom", split_axis=0, concat_axis=0, tiled=True)
     residual, direction, *faces = call(
         first_kernel, (field, field) + (face,) * 4, 10**8, halo + (faces_buffer,)
     )(pressure_old, *got, source_term, diagonal, face_coeffs, neighbours, export_cells)
     got = exchange(faces)
-    moved, force = call(
-        fluid_kernel, (shape(OWNERS, 8, CAP), shape(OWNERS, 4, CAP)), 10**9
-    )(fluid_velocity, parcels)
-    iterate, answer = call(second_kernel, (field, shape(OWNERS, 16, CAP)), 10**8, halo)(
-        direction, *got, pressure_old, residual, diagonal, face_coeffs, neighbours, parcels, moved
-    )
+    iterate, table = call(second_kernel, (field, field), 10**8, halo)(
+        direction, *got, pressure_old, residual, diagonal, face_coeffs, neighbours
+    )
+    answer, force = call(
+        parcel_kernel, (shape(OWNERS, BACK, CAP), shape(OWNERS, 4, CAP)), 10**9,
+        (pltpu.VMEM((OWNERS, BACK, CAP), F32), parts),
+        out_specs=(outside, whole),
+    )(fluid_velocity, table, parcels)
     returned = lax.all_to_all(answer, "dom", split_axis=0, concat_axis=0, tiled=True)
     momentum_source = call(
         scatter_kernel, shape(3, CELLS), 2 * 10**9, (pltpu.VMEM((6 * ROWS, LANES), F32),)

time: 53.4 us -> 54.8 us (1.026)
  the two profiles are of different devices: /device:TPU:33 before, /device:TPU:1 now
where the time goes in v4:
time: 54.8 us; the launch traced here: 54.5 us
  starting transfers between devices  28.5 us (52%)
  Pallas kernels  19.5 us (36%)
  waiting for transfers between devices  5.65 us (10%)
  between operations  0.82 us (1%)
    ppermute x2, starting transfers between devices, exchange(): lax.ppermute(faces[3], 'dom', near)  8.05 us
    ppermute x2, starting transfers between devices, exchange(): lax.ppermute(faces[1], ('group', 'dom'), under)  7.21 us
    pallas_call x1, Pallas kernels, per_device(): call(parcel_kernel, (shape(OWNERS, BACK, CAP), shape(OWNERS, 4, CAP)), 10...  5.16 us
    all_to_all x1, waiting for transfers between devices, per_device(): lax.all_to_all(answer, 'dom', split_axis=0, concat_axis=0, tiled=True)  4.82 us
    all_to_all x1, starting transfers between devices, per_device(): lax.all_to_all(answer, 'dom', split_axis=0, concat_axis=0, tiled=True)  4.29 us
    ppermute x2, starting transfers between devices, exchange(): lax.ppermute(faces[0], 'dom', far)  4.28 us
    pallas_call x1, Pallas kernels, per_device(): call(scatter_kernel, shape(3, CELLS), 2 * 10 ** 9, (pltpu.VMEM((6 * ROWS,...  4.18 us
    all_to_all x1, starting transfers between devices, per_device(): lax.all_to_all(sent, 'dom', split_axis=0, concat_axis=0, tiled=True)  3.81 us
  transfers between devices with their start and end apart: 10, of which 2 were waited for; matrix products, arithmetic and copies ran while one was open for 0% of the time, Pallas kernels for 22%

profile of v4, /device:TPU:1, one launch (start us, length us, event | category | flops | bytes accessed | tf_op | source)
XLA Modules:
  0.0 54.5 jit_solution(6897020249238181423)
XLA Ops:
  0.6 1.2 %shard_map.148 = (f32[8,128]{1,0:T(8,128)S(1)}, f32[8,128]{1,0:T(8,128)S(1)}, f32[8,128]{1,0:T(8,128)S(1)}, f32[8,128]{1,0:T(8,128)S(1)}, s32[8,128]{1,0:T(8,128...) custom-call(f32[32,128]{1,0:T(8,128)} %bitcast.6, ...), custom_call_target="tpu_custom_call" | custom-call | flops 1000000 | bytes 400000 | tf_op jit(solution)/shard_map/pallas_call | solution.py:340
  1.8 2.7 %collective-permute-start = (f32[8,128]{1,0:T(8,128)S(1)}, f32[8,128]{1,0:T(8,128)S(1)}, u32[]{:S(2)}, u32[]{:S(2)}) collective-permute-start(f32[8,128]{1,0:T(8,128)S(1)} %get-tuple-element.29), channel_id=1, source_target_pairs={{0,31},{1,2},{2,1},{3,4},{4,3},{5,6},{6,5},{7,8},{8,7},{9,10},{10,... | collective-permute-start | bytes 12296 | tf_op jit(solution)/shard_map/ppermute | solution.py:303
  4.5 3.6 %collective-permute-start.1 = (f32[8,128]{1,0:T(8,128)S(1)}, f32[8,128]{1,0:T(8,128)S(1)}, u32[]{:S(2)}, u32[]{:S(2)}) collective-permute-start(f32[8,128]{1,0:T(8,128)S(1)} %get-tuple-element.30), channel_id=1, source_target_pairs={{0,1},{1,0},{2,3},{3,2},{4,5},{5,4},{6,7},{7,6},{8,9},{9,8},{10,11... | collective-permute-start | bytes 12296 | tf_op jit(solution)/shard_map/ppermute | solution.py:304
  8.1 0.0 collective-permute-start.2
  8.1 3.8 %collective-permute-start.3 = (f32[8,128]{1,0:T(8,128)S(1)}, f32[8,128]{1,0:T(8,128)S(1)}, u32[]{:S(2)}, u32[]{:S(2)}) collective-permute-start(f32[8,128]{1,0:T(8,128)S(1)} %get-tuple-element.32), channel_id=1, source_target_pairs={{0,1},{1,0},{2,3},{3,2},{4,5},{5,4},{6,7},{7,6},{8,9},{9,8},{10,11... | collective-permute-start | bytes 12296 | tf_op jit(solution)/shard_map/ppermute | solution.py:306
  11.9 2.1 %shard_map.149 = (s32[8,128]{1,0:T(8,128)S(1)}, f32[32,24,128]{2,1,0:T(8,128)}) custom-call(s32[8,128]{1,0:T(8,128)S(1)} %get-tuple-element.33.owner_ref, s32[8,1024]{1,0:T(8,128)S(1)} %get-tuple-element.34.cells_ref, f32[8,1024]{1,0:T(8,128)S(1)} %get-tuple-element.35.weight_ref, f32[3,1024]{1,0:T(4,128)S(1)} %get-tuple-element.36.velocity_ref, ...), custom_call_target="tpu_custom_call" | custom-call | flops 100000000 | bytes 400000 | tf_op jit(solution)/shard_map/pallas_call | solution.py:354
  14.0 0.0 collective-permute-done.got0
  14.0 0.0 collective-permute-done.1.got1
  14.0 0.0 collective-permute-done.2.got2
  14.0 0.0 collective-permute-done.3.got3
  14.0 0.0 copy-start.1
  14.0 0.0 copy-start.2
  14.0 0.0 copy-start.3
  14.0 0.0 copy-start.4
  14.0 0.0 copy-start.6
  14.1 0.0 copy-start.7
  14.1 3.8 %all-to-all-start = ((f32[32,24,128]{2,1,0:T(8,128)}), f32[32,24,128]{2,1,0:T(8,128)S(1)}, u32[]{:S(2)}, u32[]{:S(2)}) async-start(f32[32,24,128]{2,1,0:T(8,128)} %get-tuple-element.52), calls=%async_computation | async-start | bytes 786432 | tf_op jit(solution)/shard_map/all_to_all | solution.py:360
  17.9 0.0 copy-done.1
  17.9 0.0 copy-done.2
  17.9 0.0 copy-done.3
  17.9 0.0 copy-done.4
  17.9 0.0 copy-done.6
  17.9 0.0 copy-done.7
  17.9 2.7 %shard_map.150 = (f32[32,128]{1,0:T(8,128)S(1)}, f32[32,128]{1,0:T(8,128)S(1)}, f32[8,128]{1,0:T(8,128)S(1)}, f32[8,128]{1,0:T(8,128)S(1)}, f32[8,128]{1,0:T(8,128)S(1)}, /*index=5*/f32[8,128]{1,0:T(8,128)S(1)}) custom-call(f32[32,128]{1,0:T(8,128)S(1)} %bitcast.7, f32[8,128]{1,0:T(8,128)S(1)} %collective-permute-done.got0, ...), custom_call_target="tpu_custom_call" | custom-call | flops 100000000 | bytes 400000 | tf_op jit(solution)/shard_map/pallas_call | solution.py:361
  20.6 1.6 %collective-permute-start.4 = (f32[8,128]{1,0:T(8,128)S(1)}, f32[8,128]{1,0:T(8,128)S(1)}, u32[]{:S(2)}, u32[]{:S(2)}) collective-permute-start(f32[8,128]{1,0:T(8,128)S(1)} %get-tuple-element.44), channel_id=1, source_target_pairs={{0,31},{1,2},{2,1},{3,4},{4,3},{5,6},{6,5},{7,8},{8,7},{9,10},{10,... | collective-permute-start | bytes 12296 | tf_op jit(solution)/shard_map/ppermute | solution.py:303
  22.2 3.7 %collective-permute-start.5 = (f32[8,128]{1,0:T(8,128)S(1)}, f32[8,128]{1,0:T(8,128)S(1)}, u32[]{:S(2)}, u32[]{:S(2)}) collective-permute-start(f32[8,128]{1,0:T(8,128)S(1)} %get-tuple-element.45), channel_id=1, source_target_pairs={{0,1},{1,0},{2,3},{3,2},{4,5},{5,4},{6,7},{7,6},{8,9},{9,8},{10,11... | collective-permute-start | bytes 12296 | tf_op jit(solution)/shard_map/ppermute | solution.py:304
  25.9 0.8 %collective-permute-start.6 = (f32[8,128]{1,0:T(8,128)S(1)}, f32[8,128]{1,0:T(8,128)S(1)}, u32[]{:S(2)}, u32[]{:S(2)}) collective-permute-start(f32[8,128]{1,0:T(8,128)S(1)} %get-tuple-element.46), channel_id=1, source_target_pairs={{0,32},{32,0},{64,96},{96,64},{128,160},{160,128},{192,224},{224,1... | collective-permute-start | bytes 12296 | tf_op jit(solution)/shard_map/ppermute | solution.py:305
  26.7 4.2 %collective-permute-start.7 = (f32[8,128]{1,0:T(8,128)S(1)}, f32[8,128]{1,0:T(8,128)S(1)}, u32[]{:S(2)}, u32[]{:S(2)}) collective-permute-start(f32[8,128]{1,0:T(8,128)S(1)} %get-tuple-element.47), channel_id=1, source_target_pairs={{0,1},{1,0},{2,3},{3,2},{4,5},{5,4},{6,7},{7,6},{8,9},{9,8},{10,11... | collective-permute-start | bytes 12296 | tf_op jit(solution)/shard_map/ppermute | solution.py:306
  30.9 0.0 collective-permute-done.4.got0
  30.9 0.0 collective-permute-done.5.got1
  31.0 0.0 collective-permute-done.6.got2
  31.0 0.8 %collective-permute-done.7.got3 = f32[8,128]{1,0:T(8,128)S(1)} collective-permute-done((f32[8,128]{1,0:T(8,128)S(1)}, f32[8,128]{1,0:T(8,128)S(1)}, u32[]{:S(2)}, u32[]{:S(2)}) %collective-permute-start.7) | collective-permute-done | bytes 4128 | tf_op jit(solution)/shard_map/ppermute | solution.py:306
  31.8 0.0 copy-start.5
  31.8 3.0 %shard_map.151 = (f32[32,128]{1,0:T(8,128)}, f32[32,128]{1,0:T(8,128)S(1)}) custom-call(f32[32,128]{1,0:T(8,128)S(1)} %get-tuple-element.43.direction_ref, f32[8,128]{1,0:T(8,128)S(1)} %collective-permute-done.4.got0, f32[8,128]{1,0:T(8,128)S(1)} %collective-permute-done.5.got1, f32[8,128]{1,0:T(8,128)S(1)} %collective-permute-done.6.got2, ...), custom_call_target="tpu_custom_call" | custom-call | flops 100000000 | bytes 400000 | tf_op jit(solution)/shard_map/pallas_call | solution.py:365
  34.7 0.0 all-to-all-done.parcel_ref
  34.7 0.0 copy-done.5
  34.7 5.2 %shard_map.152 = (f32[32,16,128]{2,1,0:T(8,128)}, f32[32,4,128]{2,1,0:T(4,128)S(1)}) custom-call(f32[3,4096]{1,0:T(4,128)S(1)} %copy-done.5, f32[32,128]{1,0:T(8,128)S(1)} %get-tuple-element.51.pressure_ref, f32[32,24,128]{2,1,0:T(8,128)S(1)} %all-to-all-done.parcel_ref), custom_call_target="tpu_custom_call" | custom-call | flops 1000000000 | bytes 400000 | tf_op jit(solution)/shard_map/pallas_call | solution.py:368
  39.9 4.3 %all-to-all-start.1 = ((f32[32,16,128]{2,1,0:T(8,128)}), f32[32,16,128]{2,1,0:T(8,128)S(1)}, u32[]{:S(2)}, u32[]{:S(2)}) async-start(f32[32,16,128]{2,1,0:T(8,128)} %get-tuple-element.53), calls=%async_computation.1 | async-start | bytes 524288 | tf_op jit(solution)/shard_map/all_to_all | solution.py:373
  44.2 0.0 copy-start
  44.2 4.2 %shard_map.154 = f32[3,4096]{1,0:T(4,128)} custom-call(f32[32,24,128]{2,1,0:T(8,128)S(1)} %all-to-all-done.parcel_ref, f32[32,4,128]{2,1,0:T(4,128)S(1)} %get-tuple-element.54.force_ref), custom_call_target="tpu_custom_call" | custom-call | flops 2000000000 | bytes 400000 | tf_op jit(solution)/shard_map/pallas_call | solution.py:374
  48.4 4.8 %all-to-all-done.1.answer_ref = f32[32,16,128]{2,1,0:T(8,128)S(1)} async-done(((f32[32,16,128]{2,1,0:T(8,128)}), f32[32,16,128]{2,1,0:T(8,128)S(1)}, u32[]{:S(2)}, u32[]{:S(2)}) %all-to-all-start.1) | async-done | bytes 262176 | tf_op jit(solution)/shard_map/all_to_all | solution.py:373
  53.2 0.0 copy-done
  53.2 1.2 %shard_map.153 = f32[3,1024]{1,0:T(4,128)} custom-call(s32[8,128]{1,0:T(8,128)S(1)} %get-tuple-element.50.place_ref, f32[32,16,128]{2,1,0:T(8,128)S(1)} %all-to-all-done.1.answer_ref, f32[3,8,1024]{2,1,0:T(8,128)S(1)} %copy-done), custom_call_target="tpu_custom_call" | custom-call | flops 1000000 | bytes 400000 | tf_op jit(solution)/shard_map/pallas_call | solution.py:377
Async XLA Ops:
  1.8 12.1 %collective-permute-start = (f32[8,128]{1,0:T(8,128)S(1)}, f32[8,128]{1,0:T(8,128)S(1)}, u32[]{:S(2)}, u32[]{:S(2)}) collective-permute-start(f32[8,128]{1,0:T(8,128)S(1)} %get-tuple-element.29), channel_id=1, source_target_pairs={{0,31},{1,2},{2,1},{3,4},{4,3},{5,6},{6,5},{7,8},{8,7},{9,10},{10,... | collective-permute-start | bytes 12296 | tf_op jit(solution)/shard_map/ppermute | solution.py:303
  4.5 9.5 %collective-permute-start.1 = (f32[8,128]{1,0:T(8,128)S(1)}, f32[8,128]{1,0:T(8,128)S(1)}, u32[]{:S(2)}, u32[]{:S(2)}) collective-permute-start(f32[8,128]{1,0:T(8,128)S(1)} %get-tuple-element.30), channel_id=1, source_target_pairs={{0,1},{1,0},{2,3},{3,2},{4,5},{5,4},{6,7},{7,6},{8,9},{9,8},{10,11... | collective-permute-start | bytes 12296 | tf_op jit(solution)/shard_map/ppermute | solution.py:304
  8.1 5.9 %collective-permute-start.2 = (f32[8,128]{1,0:T(8,128)S(1)}, f32[8,128]{1,0:T(8,128)S(1)}, u32[]{:S(2)}, u32[]{:S(2)}) collective-permute-start(f32[8,128]{1,0:T(8,128)S(1)} %get-tuple-element.31), channel_id=1, source_target_pairs={{0,32},{32,0},{64,96},{96,64},{128,160},{160,128},{192,224},{224,1... | collective-permute-start | bytes 12296 | tf_op jit(solution)/shard_map/ppermute | solution.py:305
  8.1 5.9 %collective-permute-start.3 = (f32[8,128]{1,0:T(8,128)S(1)}, f32[8,128]{1,0:T(8,128)S(1)}, u32[]{:S(2)}, u32[]{:S(2)}) collective-permute-start(f32[8,128]{1,0:T(8,128)S(1)} %get-tuple-element.32), channel_id=1, source_target_pairs={{0,1},{1,0},{2,3},{3,2},{4,5},{5,4},{6,7},{7,6},{8,9},{9,8},{10,11... | collective-permute-start | bytes 12296 | tf_op jit(solution)/shard_map/ppermute | solution.py:306
  14.0 3.9 %copy-start.1 = (s32[4,1024]{1,0:T(4,128)S(1)}, s32[4,1024]{1,0:T(4,128)}, u32[]{:S(2)}) copy-start(s32[4,1024]{1,0:T(4,128)} %export_ref.1) | copy-start | bytes 49156
  14.0 3.9 %copy-start.2 = (f32[4096]{0:T(1024)S(1)}, f32[4096]{0:T(1024)}, u32[]{:S(2)}) copy-start(f32[4096]{0:T(1024)} %param.13) | copy-start | bytes 49156
  14.0 3.9 %copy-start.3 = (f32[6,4096]{1,0:T(8,128)S(1)}, f32[6,4096]{1,0:T(8,128)}, u32[]{:S(2)}) copy-start(f32[6,4096]{1,0:T(8,128)} %coeff_ref.3) | copy-start | bytes 294916
  14.0 3.9 %copy-start.4 = (s32[6,4096]{1,0:T(8,128)S(1)}, s32[6,4096]{1,0:T(8,128)}, u32[]{:S(2)}) copy-start(s32[6,4096]{1,0:T(8,128)} %neighbour_ref.3) | copy-start | bytes 294916
  14.0 3.9 %copy-start.6 = (f32[4096]{0:T(1024)S(1)}, f32[4096]{0:T(1024)}, u32[]{:S(2)}) copy-start(f32[4096]{0:T(1024)} %param.14) | copy-start | bytes 49156
  14.1 3.9 %copy-start.7 = (f32[4096]{0:T(1024)S(1)}, f32[4096]{0:T(1024)}, u32[]{:S(2)}) copy-start(f32[4096]{0:T(1024)} %param.15) | copy-start | bytes 49156
  14.1 20.7 %all-to-all-start = ((f32[32,24,128]{2,1,0:T(8,128)}), f32[32,24,128]{2,1,0:T(8,128)S(1)}, u32[]{:S(2)}, u32[]{:S(2)}) async-start(f32[32,24,128]{2,1,0:T(8,128)} %get-tuple-element.52), calls=%async_computation | async-start | bytes 786432 | tf_op jit(solution)/shard_map/all_to_all | solution.py:360
  20.6 10.3 %collective-permute-start.4 = (f32[8,128]{1,0:T(8,128)S(1)}, f32[8,128]{1,0:T(8,128)S(1)}, u32[]{:S(2)}, u32[]{:S(2)}) collective-permute-start(f32[8,128]{1,0:T(8,128)S(1)} %get-tuple-element.44), channel_id=1, source_target_pairs={{0,31},{1,2},{2,1},{3,4},{4,3},{5,6},{6,5},{7,8},{8,7},{9,10},{10,... | collective-permute-start | bytes 12296 | tf_op jit(solution)/shard_map/ppermute | solution.py:303
  22.2 8.7 %collective-permute-start.5 = (f32[8,128]{1,0:T(8,128)S(1)}, f32[8,128]{1,0:T(8,128)S(1)}, u32[]{:S(2)}, u32[]{:S(2)}) collective-permute-start(f32[8,128]{1,0:T(8,128)S(1)} %get-tuple-element.45), channel_id=1, source_target_pairs={{0,1},{1,0},{2,3},{3,2},{4,5},{5,4},{6,7},{7,6},{8,9},{9,8},{10,11... | collective-permute-start | bytes 12296 | tf_op jit(solution)/shard_map/ppermute | solution.py:304
  25.9 5.1 %collective-permute-start.6 = (f32[8,128]{1,0:T(8,128)S(1)}, f32[8,128]{1,0:T(8,128)S(1)}, u32[]{:S(2)}, u32[]{:S(2)}) collective-permute-start(f32[8,128]{1,0:T(8,128)S(1)} %get-tuple-element.46), channel_id=1, source_target_pairs={{0,32},{32,0},{64,96},{96,64},{128,160},{160,128},{192,224},{224,1... | collective-permute-start | bytes 12296 | tf_op jit(solution)/shard_map/ppermute | solution.py:305
  26.7 5.0 %collective-permute-start.7 = (f32[8,128]{1,0:T(8,128)S(1)}, f32[8,128]{1,0:T(8,128)S(1)}, u32[]{:S(2)}, u32[]{:S(2)}) collective-permute-start(f32[8,128]{1,0:T(8,128)S(1)} %get-tuple-element.47), channel_id=1, source_target_pairs={{0,1},{1,0},{2,3},{3,2},{4,5},{5,4},{6,7},{7,6},{8,9},{9,8},{10,11... | collective-permute-start | bytes 12296 | tf_op jit(solution)/shard_map/ppermute | solution.py:306
  31.8 3.0 %copy-start.5 = (f32[3,4096]{1,0:T(4,128)S(1)}, f32[3,4096]{1,0:T(4,128)}, u32[]{:S(2)}) copy-start(f32[3,4096]{1,0:T(4,128)} %fluid_ref.1) | copy-start | bytes 147460
  39.9 13.3 %all-to-all-start.1 = ((f32[32,16,128]{2,1,0:T(8,128)}), f32[32,16,128]{2,1,0:T(8,128)S(1)}, u32[]{:S(2)}, u32[]{:S(2)}) async-start(f32[32,16,128]{2,1,0:T(8,128)} %get-tuple-element.53), calls=%async_computation.1 | async-start | bytes 524288 | tf_op jit(solution)/shard_map/all_to_all | solution.py:373
  44.2 9.0 %copy-start = (f32[3,8,1024]{2,1,0:T(8,128)S(1)}, f32[3,8,1024]{2,1,0:T(8,128)}, u32[]{:S(2)}) copy-start(f32[3,8,1024]{2,1,0:T(8,128)} %grad_ref.1) | copy-start | bytes 294916

commit v5 on v4

--- a/solution.py
+++ b/solution.py
@@ -91,7 +91,16 @@
         copy.wait()
 
 
-def multiply(vector_ref, got_refs, diagonal_ref, coeff_ref, neighbour_ref, halo_ref, out_ref):
+def own_kernel(vector_ref, diagonal_ref, coeff_ref, neighbour_ref, out_ref):
+    table = rows_of(vector_ref, ROWS)
+    for t in range(ROWS):
+        cut, row = slice(t * LANES, (t + 1) * LANES), slice(t, t + 1)
+        (found,) = look_up([table], neighbour_ref[:, cut])
+        linked = jnp.sum(coeff_ref[:, cut] * found, axis=0, keepdims=True)
+        out_ref[row, :] = diagonal_ref[row, :] * vector_ref[row, :] - linked
+
+
+def multiply(own_ref, got_refs, coeff_ref, neighbour_ref, halo_ref, out_ref):
     group = lax.axis_index("group")
     last = lax.axis_size("group") - 1
     far, under, over, near = got_refs
@@ -104,22 +113,21 @@
             above = jnp.where(group < last, above, 0.0)
         halo_ref[d * FACE_ROWS : (d + 1) * FACE_ROWS, :] = below
         halo_ref[(d + 1) * FACE_ROWS : (d + 2) * FACE_ROWS, :] = above
-    table = rows_of(vector_ref, ROWS) + rows_of(halo_ref, 4 * FACE_ROWS)
+    table = rows_of(halo_ref, 4 * FACE_ROWS)
     for t in range(ROWS):
         cut, row = slice(t * LANES, (t + 1) * LANES), slice(t, t + 1)
-        (found,) = look_up([table], neighbour_ref[:, cut])
+        (found,) = look_up([table], neighbour_ref[:, cut] - CELLS)
         linked = jnp.sum(coeff_ref[:, cut] * found, axis=0, keepdims=True)
-        out_ref[row, :] = diagonal_ref[row, :] * vector_ref[row, :] - linked
+        out_ref[row, :] = own_ref[row, :] - linked
 
 
 def first_kernel(
     pressure_ref, got0, got1, got2, got3, source_ref, diagonal_ref, coeff_ref, neighbour_ref,
-    export_ref, residual_ref, direction_ref, out0, out1, out2, out3, halo_ref, product_ref, face_ref,
+    export_ref, residual_ref, direction_ref, out0, out1, out2, out3, halo_ref, product_ref,
+    own_ref, face_ref,
 ):
-    multiply(
-        pressure_ref, (got0, got1, got2, got3), diagonal_ref, coeff_ref, neighbour_ref,
-        halo_ref, product_ref,
-    )
+    own_kernel(pressure_ref, diagonal_ref, coeff_ref, neighbour_ref, own_ref)
+    multiply(own_ref, (got0, got1, got2, got3), coeff_ref, neighbour_ref, halo_ref, product_ref)
     residual = source_ref[...] - product_ref[...]
     residual_ref[...] = residual
     direction_ref[...] = residual / CENTRE
@@ -127,19 +135,25 @@
 
 
 def second_kernel(
-    direction_ref, got0, got1, got2, got3, pressure_ref, residual_ref, diagonal_ref, coeff_ref,
-    neighbour_ref, out_ref, again_ref, halo_ref, product_ref,
+    own_ref, got0, got1, got2, got3, direction_ref, pressure_ref, residual_ref, coeff_ref,
+    neighbour_ref, parcel_ref, moved_ref, out_ref, answer_hbm, halo_ref, product_ref, answer_ref,
+    sems,
 ):
-    multiply(
-        direction_ref, (got0, got1, got2, got3), diagonal_ref, coeff_ref, neighbour_ref,
-        halo_ref, product_ref,
-    )
+    multiply(own_ref, (got0, got1, got2, got3), coeff_ref, neighbour_ref, halo_ref, product_ref)
     direction = direction_ref[...]
     residual = residual_ref[...] - product_ref[...]
     iterate = pressure_ref[...] + direction
     direction = RHO_NEXT * RHO_FIRST * direction + (2.0 * RHO_NEXT / HALF_WIDTH) * residual
     out_ref[...] = iterate + direction
-    again_ref[...] = iterate + direction
+    table = rows_of(out_ref, ROWS)
+    for s in range(OWNERS):
+        (found,) = look_up([table], parcel_ref[s, 8:16, :].astype(I32))
+        answer_ref[s, 0:8, :] = found
+        answer_ref[s, 8:16, :] = moved_ref[s]
+        if s % PART == PART - 1:
+            send_out(answer_ref, answer_hbm, sems, s // PART).start()
+    for part in range(OWNERS // PART):
+        send_out(answer_ref, answer_hbm, sems, part).wait()
 
 
 def send_out(local_ref, hbm_ref, sems, part):
@@ -206,30 +220,22 @@
         send_out(sent_ref, sent_hbm, sems, part).wait()
 
 
-def parcel_kernel(
-    fluid_ref, pressure_ref, parcel_ref, answer_hbm, force_ref, answer_ref, sems
-):
+def fluid_kernel(fluid_ref, parcel_ref, moved_ref, force_ref):
     tables = [
         [lambda c=c, r=r: fluid_ref[c : c + 1, r * LANES : (r + 1) * LANES] for r in range(ROWS)]
         for c in range(3)
     ]
-    tables.append(rows_of(pressure_ref, ROWS))
     for s in range(OWNERS):
-        *found, pressure = look_up(tables, parcel_ref[s, 8:16, :].astype(I32))
-        answer_ref[s, 0:8, :] = pressure
+        found = look_up(tables, parcel_ref[s, 8:16, :].astype(I32))
         weights = parcel_ref[s, 0:8, :]
         rate = parcel_ref[s, 19:20, :]
         for c in range(3):
             velocity = parcel_ref[s, 16 + c : 17 + c, :]
             fluid_at = jnp.sum(weights * found[c], axis=0, keepdims=True)
-            answer_ref[s, 8 + c : 9 + c, :] = velocity + rate * (fluid_at - velocity)
+            moved_ref[s, c : c + 1, :] = velocity + rate * (fluid_at - velocity)
             force_ref[s, c : c + 1, :] = rate * (velocity - fluid_at)
-        answer_ref[s, 11:16, :] = jnp.zeros((5, LANES), F32)
+        moved_ref[s, 3:8, :] = jnp.zeros((5, LANES), F32)
         force_ref[s, 3:4, :] = jnp.zeros((1, LANES), F32)
-        if s % PART == PART - 1:
-            send_out(answer_ref, answer_hbm, sems, s // PART).start()
-    for part in range(OWNERS // PART):
-        send_out(answer_ref, answer_hbm, sems, part).wait()
 
 
 def scatter_kernel(parcel_ref, force_ref, out_ref, total_ref):
@@ -348,28 +354,32 @@
         in_specs=[pl.BlockSpec(memory_space=pltpu.HBM)] * len(kept),
     )(*kept)
     got = exchange(outs[:4])
-    whole = pl.BlockSpec(memory_space=pltpu.VMEM)
+    everything = pl.BlockSpec(memory_space=pltpu.VMEM)
     outside = pl.BlockSpec(memory_space=pl.ANY)
     parts = pltpu.SemaphoreType.DMA((OWNERS // PART,))
     place, sent = call(
         slot_kernel, (shape(CHUNKS, LANES, dtype=I32), shape(OWNERS, SENT, CAP)), 10**8,
         (pltpu.VMEM((OWNERS, SENT, CAP), F32), pltpu.VMEM((8, PARCELS), F32), parts),
-        out_specs=(whole, outside),
+        out_specs=(everything, outside),
     )(*outs[4:])
     got, sent = lax.optimization_barrier((got, sent))
     parcels = lax.all_to_all(sent, "dom", split_axis=0, concat_axis=0, tiled=True)
     residual, direction, *faces = call(
-        first_kernel, (field, field) + (face,) * 4, 10**8, halo + (faces_buffer,)
+        first_kernel, (field, field) + (face,) * 4, 10**8,
+        halo + (pltpu.VMEM((ROWS, LANES), F32), faces_buffer),
     )(pressure_old, *got, source_term, diagonal, face_coeffs, neighbours, export_cells)
     got = exchange(faces)
-    iterate, table = call(second_kernel, (field, field), 10**8, halo)(
-        direction, *got, pressure_old, residual, diagonal, face_coeffs, neighbours
-    )
-    answer, force = call(
-        parcel_kernel, (shape(OWNERS, BACK, CAP), shape(OWNERS, 4, CAP)), 10**9,
-        (pltpu.VMEM((OWNERS, BACK, CAP), F32), parts),
-        out_specs=(outside, whole),
-    )(fluid_velocity, table, parcels)
+    own = call(own_kernel, field, 10**7)(direction, diagonal, face_coeffs, neighbours)
+    moved, force = call(
+        fluid_kernel, (shape(OWNERS, 8, CAP), shape(OWNERS, 4, CAP)), 10**9
+    )(fluid_velocity, parcels)
+    iterate, answer = call(
+        second_kernel, (field, shape(OWNERS, BACK, CAP)), 10**8,
+        halo + (pltpu.VMEM((OWNERS, BACK, CAP), F32), parts),
+        out_specs=(everything, outside),
+    )(
+        own, *got, direction, pressure_old, residual, face_coeffs, neighbours, parcels, moved
+    )
     returned = lax.all_to_all(answer, "dom", split_axis=0, concat_axis=0, tiled=True)
     momentum_source = call(
         scatter_kernel, shape(3, CELLS), 2 * 10**9, (pltpu.VMEM((6 * ROWS, LANES), F32),)

time: 54.8 us -> 53.8 us (0.982)
  waiting for transfers between devices: 5.65 us -> 4.71 us
  starting transfers between devices: 28.5 us -> 27.8 us
    ppermute x2, waiting for transfers between devices: 0.81 us -> 0.01 us  [exchange(): lax.ppermute(faces[3], 'dom', near)]
    all_to_all x1, starting transfers between devices: 4.29 us -> 3.66 us  [per_device(): lax.all_to_all(answer, 'dom', split_axis=0, concat_axis=0, tiled=True)]
    pallas_call x3 -> x4, Pallas kernels: 10.8 us -> 11.3 us  [the longest x1 3.78 us: per_device(): call(second_kernel, (field, shape(OWNERS, BACK, CAP)), 10 ** 8, halo + (p...]
  transfers between devices with their start and end apart: 10 -> 10, of which waited for: 2 -> 1; matrix products, arithmetic and copies ran while one was open for 0% -> 0% of each run, Pallas kernels for 22% -> 26%
where the time goes in v5:
time: 53.8 us; the launch traced here: 53.4 us
  starting transfers between devices  27.8 us (52%)
  Pallas kernels  20 us (37%)
  waiting for transfers between devices  4.71 us (9%)
  between operations  0.87 us (2%)
    ppermute x2, starting transfers between devices, exchange(): lax.ppermute(faces[3], 'dom', near)  8.05 us
    ppermute x2, starting transfers between devices, exchange(): lax.ppermute(faces[1], ('group', 'dom'), under)  7.21 us
    all_to_all x1, waiting for transfers between devices, per_device(): lax.all_to_all(answer, 'dom', split_axis=0, concat_axis=0, tiled=True)  4.69 us
    ppermute x2, starting transfers between devices, exchange(): lax.ppermute(faces[0], 'dom', far)  4.28 us
    pallas_call x1, Pallas kernels, per_device(): call(scatter_kernel, shape(3, CELLS), 2 * 10 ** 9, (pltpu.VMEM((6 * ROWS,...  4.18 us
    all_to_all x1, starting transfers between devices, per_device(): lax.all_to_all(sent, 'dom', split_axis=0, concat_axis=0, tiled=True)  3.81 us
    pallas_call x1, Pallas kernels, per_device(): call(second_kernel, (field, shape(OWNERS, BACK, CAP)), 10 ** 8, halo + (p...  3.78 us
    all_to_all x1, starting transfers between devices, per_device(): lax.all_to_all(answer, 'dom', split_axis=0, concat_axis=0, tiled=True)  3.66 us
  transfers between devices with their start and end apart: 10, of which 1 were waited for; matrix products, arithmetic and copies ran while one was open for 0% of the time, Pallas kernels for 26%

profile of v5, /device:TPU:1, one launch (start us, length us, event | category | flops | bytes accessed | tf_op | source)
XLA Modules:
  0.0 53.4 jit_solution(5038148364197960458)
XLA Ops:
  0.6 1.2 %shard_map.148 = (f32[8,128]{1,0:T(8,128)S(1)}, f32[8,128]{1,0:T(8,128)S(1)}, f32[8,128]{1,0:T(8,128)S(1)}, f32[8,128]{1,0:T(8,128)S(1)}, s32[8,128]{1,0:T(8,128...) custom-call(f32[32,128]{1,0:T(8,128)} %bitcast.6, ...), custom_call_target="tpu_custom_call" | custom-call | flops 1000000 | bytes 400000 | tf_op jit(solution)/shard_map/pallas_call | solution.py:346
  1.8 2.7 %collective-permute-start = (f32[8,128]{1,0:T(8,128)S(1)}, f32[8,128]{1,0:T(8,128)S(1)}, u32[]{:S(2)}, u32[]{:S(2)}) collective-permute-start(f32[8,128]{1,0:T(8,128)S(1)} %get-tuple-element.29), channel_id=1, source_target_pairs={{0,31},{1,2},{2,1},{3,4},{4,3},{5,6},{6,5},{7,8},{8,7},{9,10},{10,... | collective-permute-start | bytes 12296 | tf_op jit(solution)/shard_map/ppermute | solution.py:309
  4.5 3.6 %collective-permute-start.1 = (f32[8,128]{1,0:T(8,128)S(1)}, f32[8,128]{1,0:T(8,128)S(1)}, u32[]{:S(2)}, u32[]{:S(2)}) collective-permute-start(f32[8,128]{1,0:T(8,128)S(1)} %get-tuple-element.30), channel_id=1, source_target_pairs={{0,1},{1,0},{2,3},{3,2},{4,5},{5,4},{6,7},{7,6},{8,9},{9,8},{10,11... | collective-permute-start | bytes 12296 | tf_op jit(solution)/shard_map/ppermute | solution.py:310
  8.1 0.0 collective-permute-start.2
  8.1 3.8 %collective-permute-start.3 = (f32[8,128]{1,0:T(8,128)S(1)}, f32[8,128]{1,0:T(8,128)S(1)}, u32[]{:S(2)}, u32[]{:S(2)}) collective-permute-start(f32[8,128]{1,0:T(8,128)S(1)} %get-tuple-element.32), channel_id=1, source_target_pairs={{0,1},{1,0},{2,3},{3,2},{4,5},{5,4},{6,7},{7,6},{8,9},{9,8},{10,11... | collective-permute-start | bytes 12296 | tf_op jit(solution)/shard_map/ppermute | solution.py:312
  11.9 2.1 %shard_map.149 = (s32[8,128]{1,0:T(8,128)S(1)}, f32[32,24,128]{2,1,0:T(8,128)}) custom-call(s32[8,128]{1,0:T(8,128)S(1)} %get-tuple-element.33.owner_ref, s32[8,1024]{1,0:T(8,128)S(1)} %get-tuple-element.34.cells_ref, f32[8,1024]{1,0:T(8,128)S(1)} %get-tuple-element.35.weight_ref, f32[3,1024]{1,0:T(4,128)S(1)} %get-tuple-element.36.velocity_ref, ...), custom_call_target="tpu_custom_call" | custom-call | flops 100000000 | bytes 400000 | tf_op jit(solution)/shard_map/pallas_call | solution.py:360
  14.0 0.0 collective-permute-done.got0
  14.0 0.0 collective-permute-done.1.got1
  14.0 0.0 collective-permute-done.2.got2
  14.0 0.0 collective-permute-done.3.got3
  14.0 0.0 copy-start
  14.0 0.0 copy-start.1
  14.0 0.0 copy-start.3
  14.0 0.0 copy-start.4
  14.0 0.0 copy-start.5
  14.1 0.0 copy-start.7
  14.1 3.8 %all-to-all-start = ((f32[32,24,128]{2,1,0:T(8,128)}), f32[32,24,128]{2,1,0:T(8,128)S(1)}, u32[]{:S(2)}, u32[]{:S(2)}) async-start(f32[32,24,128]{2,1,0:T(8,128)} %get-tuple-element.49), calls=%async_computation | async-start | bytes 786432 | tf_op jit(solution)/shard_map/all_to_all | solution.py:366
  17.9 0.0 copy-done
  17.9 0.0 copy-done.1
  17.9 0.0 copy-done.3
  17.9 0.0 copy-done.4
  17.9 0.0 copy-done.5
  17.9 0.0 copy-done.7
  17.9 2.8 %shard_map.150 = (f32[32,128]{1,0:T(8,128)S(1)}, f32[32,128]{1,0:T(8,128)S(1)}, f32[8,128]{1,0:T(8,128)S(1)}, f32[8,128]{1,0:T(8,128)S(1)}, f32[8,128]{1,0:T(8,128)S(1)}, /*index=5*/f32[8,128]{1,0:T(8,128)S(1)}) custom-call(f32[32,128]{1,0:T(8,128)S(1)} %bitcast.7, f32[8,128]{1,0:T(8,128)S(1)} %collective-permute-done.got0, ...), custom_call_target="tpu_custom_call" | custom-call | flops 100000000 | bytes 400000 | tf_op jit(solution)/shard_map/pallas_call | solution.py:367
  20.7 1.6 %collective-permute-start.4 = (f32[8,128]{1,0:T(8,128)S(1)}, f32[8,128]{1,0:T(8,128)S(1)}, u32[]{:S(2)}, u32[]{:S(2)}) collective-permute-start(f32[8,128]{1,0:T(8,128)S(1)} %get-tuple-element.44), channel_id=1, source_target_pairs={{0,31},{1,2},{2,1},{3,4},{4,3},{5,6},{6,5},{7,8},{8,7},{9,10},{10,... | collective-permute-start | bytes 12296 | tf_op jit(solution)/shard_map/ppermute | solution.py:309
  22.3 3.7 %collective-permute-start.5 = (f32[8,128]{1,0:T(8,128)S(1)}, f32[8,128]{1,0:T(8,128)S(1)}, u32[]{:S(2)}, u32[]{:S(2)}) collective-permute-start(f32[8,128]{1,0:T(8,128)S(1)} %get-tuple-element.45), channel_id=1, source_target_pairs={{0,1},{1,0},{2,3},{3,2},{4,5},{5,4},{6,7},{7,6},{8,9},{9,8},{10,11... | collective-permute-start | bytes 12296 | tf_op jit(solution)/shard_map/ppermute | solution.py:310
  26.0 0.8 %collective-permute-start.6 = (f32[8,128]{1,0:T(8,128)S(1)}, f32[8,128]{1,0:T(8,128)S(1)}, u32[]{:S(2)}, u32[]{:S(2)}) collective-permute-start(f32[8,128]{1,0:T(8,128)S(1)} %get-tuple-element.46), channel_id=1, source_target_pairs={{0,32},{32,0},{64,96},{96,64},{128,160},{160,128},{192,224},{224,1... | collective-permute-start | bytes 12296 | tf_op jit(solution)/shard_map/ppermute | solution.py:311
  26.8 4.2 %collective-permute-start.7 = (f32[8,128]{1,0:T(8,128)S(1)}, f32[8,128]{1,0:T(8,128)S(1)}, u32[]{:S(2)}, u32[]{:S(2)}) collective-permute-start(f32[8,128]{1,0:T(8,128)S(1)} %get-tuple-element.47), channel_id=1, source_target_pairs={{0,1},{1,0},{2,3},{3,2},{4,5},{5,4},{6,7},{7,6},{8,9},{9,8},{10,11... | collective-permute-start | bytes 12296 | tf_op jit(solution)/shard_map/ppermute | solution.py:312
  31.0 0.0 copy-start.6
  31.0 1.3 %shard_map.151.own_ref = f32[32,128]{1,0:T(8,128)S(1)} custom-call(f32[32,128]{1,0:T(8,128)S(1)} %get-tuple-element.43.vector_ref.direction_ref, f32[32,128]{1,0:T(8,128)S(1)} %bitcast.10, f32[6,4096]{1,0:T(8,128)S(1)} %copy-done, s32[6,4096]{1,0:T(8,128)S(1)} %copy-done.1), custom_call_target="tpu_custom_call" | custom-call | flops 10000000 | bytes 400000 | tf_op jit(solution)/shard_map/pallas_call | solution.py:372
  32.3 0.0 all-to-all-done.parcel_ref
  32.3 0.0 copy-done.6
  32.3 3.5 %shard_map.152 = (f32[32,8,128]{2,1,0:T(8,128)S(1)}, f32[32,4,128]{2,1,0:T(4,128)S(1)}) custom-call(f32[3,4096]{1,0:T(4,128)S(1)} %copy-done.6, f32[32,24,128]{2,1,0:T(8,128)S(1)} %all-to-all-done.parcel_ref), custom_call_target="tpu_custom_call" | custom-call | flops 1000000000 | bytes 400000 | tf_op jit(solution)/shard_map/pallas_call | solution.py:373
  35.8 0.0 collective-permute-done.4.got0
  35.8 0.0 collective-permute-done.5.got1
  35.8 0.0 collective-permute-done.6.got2
  35.8 0.0 collective-permute-done.7.got3
  35.9 3.8 %shard_map.153 = (f32[32,128]{1,0:T(8,128)}, f32[32,16,128]{2,1,0:T(8,128)}) custom-call(f32[32,128]{1,0:T(8,128)S(1)} %shard_map.151.own_ref, f32[8,128]{1,0:T(8,128)S(1)} %collective-permute-done.4.got0, f32[8,128]{1,0:T(8,128)S(1)} %collective-permute-done.5.got1, f32[8,128]{1,0:T(8,128)S(1)} %collective-permute-done.6.got2, ...), custom_call_target="tpu_custom_call" | custom-call | flops 100000000 | bytes 400000 | tf_op jit(solution)/shard_map/pallas_call | solution.py:376
  39.6 3.7 %all-to-all-start.1 = ((f32[32,16,128]{2,1,0:T(8,128)}), f32[32,16,128]{2,1,0:T(8,128)S(1)}, u32[]{:S(2)}, u32[]{:S(2)}) async-start(f32[32,16,128]{2,1,0:T(8,128)} %get-tuple-element.53), calls=%async_computation.1 | async-start | bytes 524288 | tf_op jit(solution)/shard_map/all_to_all | solution.py:383
  43.3 0.0 copy-start.2
  43.3 4.2 %shard_map.155 = f32[3,4096]{1,0:T(4,128)} custom-call(f32[32,24,128]{2,1,0:T(8,128)S(1)} %all-to-all-done.parcel_ref, f32[32,4,128]{2,1,0:T(4,128)S(1)} %get-tuple-element.54.force_ref), custom_call_target="tpu_custom_call" | custom-call | flops 2000000000 | bytes 400000 | tf_op jit(solution)/shard_map/pallas_call | solution.py:384
  47.5 4.7 %all-to-all-done.1.answer_ref = f32[32,16,128]{2,1,0:T(8,128)S(1)} async-done(((f32[32,16,128]{2,1,0:T(8,128)}), f32[32,16,128]{2,1,0:T(8,128)S(1)}, u32[]{:S(2)}, u32[]{:S(2)}) %all-to-all-start.1) | async-done | bytes 262176 | tf_op jit(solution)/shard_map/all_to_all | solution.py:383
  52.2 0.0 copy-done.2
  52.2 1.2 %shard_map.154 = f32[3,1024]{1,0:T(4,128)} custom-call(s32[8,128]{1,0:T(8,128)S(1)} %get-tuple-element.52.place_ref, f32[32,16,128]{2,1,0:T(8,128)S(1)} %all-to-all-done.1.answer_ref, f32[3,8,1024]{2,1,0:T(8,128)S(1)} %copy-done.2), custom_call_target="tpu_custom_call" | custom-call | flops 1000000 | bytes 400000 | tf_op jit(solution)/shard_map/pallas_call | solution.py:387
Async XLA Ops:
  1.8 12.1 %collective-permute-start = (f32[8,128]{1,0:T(8,128)S(1)}, f32[8,128]{1,0:T(8,128)S(1)}, u32[]{:S(2)}, u32[]{:S(2)}) collective-permute-start(f32[8,128]{1,0:T(8,128)S(1)} %get-tuple-element.29), channel_id=1, source_target_pairs={{0,31},{1,2},{2,1},{3,4},{4,3},{5,6},{6,5},{7,8},{8,7},{9,10},{10,... | collective-permute-start | bytes 12296 | tf_op jit(solution)/shard_map/ppermute | solution.py:309
  4.5 9.5 %collective-permute-start.1 = (f32[8,128]{1,0:T(8,128)S(1)}, f32[8,128]{1,0:T(8,128)S(1)}, u32[]{:S(2)}, u32[]{:S(2)}) collective-permute-start(f32[8,128]{1,0:T(8,128)S(1)} %get-tuple-element.30), channel_id=1, source_target_pairs={{0,1},{1,0},{2,3},{3,2},{4,5},{5,4},{6,7},{7,6},{8,9},{9,8},{10,11... | collective-permute-start | bytes 12296 | tf_op jit(solution)/shard_map/ppermute | solution.py:310
  8.1 5.9 %collective-permute-start.2 = (f32[8,128]{1,0:T(8,128)S(1)}, f32[8,128]{1,0:T(8,128)S(1)}, u32[]{:S(2)}, u32[]{:S(2)}) collective-permute-start(f32[8,128]{1,0:T(8,128)S(1)} %get-tuple-element.31), channel_id=1, source_target_pairs={{0,32},{32,0},{64,96},{96,64},{128,160},{160,128},{192,224},{224,1... | collective-permute-start | bytes 12296 | tf_op jit(solution)/shard_map/ppermute | solution.py:311
  8.1 5.9 %collective-permute-start.3 = (f32[8,128]{1,0:T(8,128)S(1)}, f32[8,128]{1,0:T(8,128)S(1)}, u32[]{:S(2)}, u32[]{:S(2)}) collective-permute-start(f32[8,128]{1,0:T(8,128)S(1)} %get-tuple-element.32), channel_id=1, source_target_pairs={{0,1},{1,0},{2,3},{3,2},{4,5},{5,4},{6,7},{7,6},{8,9},{9,8},{10,11... | collective-permute-start | bytes 12296 | tf_op jit(solution)/shard_map/ppermute | solution.py:312
  14.0 3.9 %copy-start = (f32[6,4096]{1,0:T(8,128)S(1)}, f32[6,4096]{1,0:T(8,128)}, u32[]{:S(2)}) copy-start(f32[6,4096]{1,0:T(8,128)} %coeff_ref.5) | copy-start | bytes 294916
  14.0 3.9 %copy-start.1 = (s32[6,4096]{1,0:T(8,128)S(1)}, s32[6,4096]{1,0:T(8,128)}, u32[]{:S(2)}) copy-start(s32[6,4096]{1,0:T(8,128)} %neighbour_ref.5) | copy-start | bytes 294916
  14.0 3.9 %copy-start.3 = (f32[4096]{0:T(1024)S(1)}, f32[4096]{0:T(1024)}, u32[]{:S(2)}) copy-start(f32[4096]{0:T(1024)} %param.13) | copy-start | bytes 49156
  14.0 3.9 %copy-start.4 = (s32[4,1024]{1,0:T(4,128)S(1)}, s32[4,1024]{1,0:T(4,128)}, u32[]{:S(2)}) copy-start(s32[4,1024]{1,0:T(4,128)} %export_ref.1) | copy-start | bytes 49156
  14.0 3.9 %copy-start.5 = (f32[4096]{0:T(1024)S(1)}, f32[4096]{0:T(1024)}, u32[]{:S(2)}) copy-start(f32[4096]{0:T(1024)} %param.15) | copy-start | bytes 49156
  14.1 3.9 %copy-start.7 = (f32[4096]{0:T(1024)S(1)}, f32[4096]{0:T(1024)}, u32[]{:S(2)}) copy-start(f32[4096]{0:T(1024)} %param.14) | copy-start | bytes 49156
  14.1 18.2 %all-to-all-start = ((f32[32,24,128]{2,1,0:T(8,128)}), f32[32,24,128]{2,1,0:T(8,128)S(1)}, u32[]{:S(2)}, u32[]{:S(2)}) async-start(f32[32,24,128]{2,1,0:T(8,128)} %get-tuple-element.49), calls=%async_computation | async-start | bytes 786432 | tf_op jit(solution)/shard_map/all_to_all | solution.py:366
  20.7 15.1 %collective-permute-start.4 = (f32[8,128]{1,0:T(8,128)S(1)}, f32[8,128]{1,0:T(8,128)S(1)}, u32[]{:S(2)}, u32[]{:S(2)}) collective-permute-start(f32[8,128]{1,0:T(8,128)S(1)} %get-tuple-element.44), channel_id=1, source_target_pairs={{0,31},{1,2},{2,1},{3,4},{4,3},{5,6},{6,5},{7,8},{8,7},{9,10},{10,... | collective-permute-start | bytes 12296 | tf_op jit(solution)/shard_map/ppermute | solution.py:309
  22.3 13.5 %collective-permute-start.5 = (f32[8,128]{1,0:T(8,128)S(1)}, f32[8,128]{1,0:T(8,128)S(1)}, u32[]{:S(2)}, u32[]{:S(2)}) collective-permute-start(f32[8,128]{1,0:T(8,128)S(1)} %get-tuple-element.45), channel_id=1, source_target_pairs={{0,1},{1,0},{2,3},{3,2},{4,5},{5,4},{6,7},{7,6},{8,9},{9,8},{10,11... | collective-permute-start | bytes 12296 | tf_op jit(solution)/shard_map/ppermute | solution.py:310
  26.0 9.8 %collective-permute-start.6 = (f32[8,128]{1,0:T(8,128)S(1)}, f32[8,128]{1,0:T(8,128)S(1)}, u32[]{:S(2)}, u32[]{:S(2)}) collective-permute-start(f32[8,128]{1,0:T(8,128)S(1)} %get-tuple-element.46), channel_id=1, source_target_pairs={{0,32},{32,0},{64,96},{96,64},{128,160},{160,128},{192,224},{224,1... | collective-permute-start | bytes 12296 | tf_op jit(solution)/shard_map/ppermute | solution.py:311
  26.8 9.0 %collective-permute-start.7 = (f32[8,128]{1,0:T(8,128)S(1)}, f32[8,128]{1,0:T(8,128)S(1)}, u32[]{:S(2)}, u32[]{:S(2)}) collective-permute-start(f32[8,128]{1,0:T(8,128)S(1)} %get-tuple-element.47), channel_id=1, source_target_pairs={{0,1},{1,0},{2,3},{3,2},{4,5},{5,4},{6,7},{7,6},{8,9},{9,8},{10,11... | collective-permute-start | bytes 12296 | tf_op jit(solution)/shard_map/ppermute | solution.py:312
  31.0 1.3 %copy-start.6 = (f32[3,4096]{1,0:T(4,128)S(1)}, f32[3,4096]{1,0:T(4,128)}, u32[]{:S(2)}) copy-start(f32[3,4096]{1,0:T(4,128)} %fluid_ref.1) | copy-start | bytes 147460
  39.6 12.6 %all-to-all-start.1 = ((f32[32,16,128]{2,1,0:T(8,128)}), f32[32,16,128]{2,1,0:T(8,128)S(1)}, u32[]{:S(2)}, u32[]{:S(2)}) async-start(f32[32,16,128]{2,1,0:T(8,128)} %get-tuple-element.53), calls=%async_computation.1 | async-start | bytes 524288 | tf_op jit(solution)/shard_map/all_to_all | solution.py:383
  43.3 8.9 %copy-start.2 = (f32[3,8,1024]{2,1,0:T(8,128)S(1)}, f32[3,8,1024]{2,1,0:T(8,128)}, u32[]{:S(2)}) copy-start(f32[3,8,1024]{2,1,0:T(8,128)} %grad_ref.1) | copy-start | bytes 294916

commit v6 on v4

--- a/solution.py
+++ b/solution.py
@@ -66,7 +66,7 @@
         (found,) = look_up([rows_of(field_ref, ROWS)], index)
         for d in range(4):
             face_ref[d, t : t + 1, :] = found[d : d + 1]
-    for axis, d, first, second in (("dom", 0, outs[3], outs[0]), ("group", 2, outs[2], outs[1])):
+    for axis, d, first, second in (("dom", 0, outs[3], outs[0]), ("group", 2, outs[1], outs[2])):
         even = is_even(axis)
         first[...] = jnp.where(even, face_ref[d], face_ref[d + 1])
         second[...] = jnp.where(even, face_ref[d + 1], face_ref[d])
@@ -94,7 +94,7 @@
 def multiply(vector_ref, got_refs, diagonal_ref, coeff_ref, neighbour_ref, halo_ref, out_ref):
     group = lax.axis_index("group")
     last = lax.axis_size("group") - 1
-    far, under, over, near = got_refs
+    far, over, under, near = got_refs
     for axis, d, first, second in (("dom", 0, near, far), ("group", 2, over, under)):
         even = is_even(axis)
         below = jnp.where(even, second[...], first[...])
@@ -128,7 +128,7 @@
 
 def second_kernel(
     direction_ref, got0, got1, got2, got3, pressure_ref, residual_ref, diagonal_ref, coeff_ref,
-    neighbour_ref, out_ref, again_ref, halo_ref, product_ref,
+    neighbour_ref, parcel_ref, moved_ref, out_ref, answer_ref, halo_ref, product_ref,
 ):
     multiply(
         direction_ref, (got0, got1, got2, got3), diagonal_ref, coeff_ref, neighbour_ref,
@@ -139,7 +139,11 @@
     iterate = pressure_ref[...] + direction
     direction = RHO_NEXT * RHO_FIRST * direction + (2.0 * RHO_NEXT / HALF_WIDTH) * residual
     out_ref[...] = iterate + direction
-    again_ref[...] = iterate + direction
+    table = rows_of(out_ref, ROWS)
+    for s in range(OWNERS):
+        (found,) = look_up([table], parcel_ref[s, 8:16, :].astype(I32))
+        answer_ref[s, 0:8, :] = found
+        answer_ref[s, 8:16, :] = moved_ref[s]
 
 
 def send_out(local_ref, hbm_ref, sems, part):
@@ -206,30 +210,22 @@
         send_out(sent_ref, sent_hbm, sems, part).wait()
 
 
-def parcel_kernel(
-    fluid_ref, pressure_ref, parcel_ref, answer_hbm, force_ref, answer_ref, sems
-):
+def fluid_kernel(fluid_ref, parcel_ref, moved_ref, force_ref):
     tables = [
         [lambda c=c, r=r: fluid_ref[c : c + 1, r * LANES : (r + 1) * LANES] for r in range(ROWS)]
         for c in range(3)
     ]
-    tables.append(rows_of(pressure_ref, ROWS))
     for s in range(OWNERS):
-        *found, pressure = look_up(tables, parcel_ref[s, 8:16, :].astype(I32))
-        answer_ref[s, 0:8, :] = pressure
+        found = look_up(tables, parcel_ref[s, 8:16, :].astype(I32))
         weights = parcel_ref[s, 0:8, :]
         rate = parcel_ref[s, 19:20, :]
         for c in range(3):
             velocity = parcel_ref[s, 16 + c : 17 + c, :]
             fluid_at = jnp.sum(weights * found[c], axis=0, keepdims=True)
-            answer_ref[s, 8 + c : 9 + c, :] = velocity + rate * (fluid_at - velocity)
+            moved_ref[s, c : c + 1, :] = velocity + rate * (fluid_at - velocity)
             force_ref[s, c : c + 1, :] = rate * (velocity - fluid_at)
-        answer_ref[s, 11:16, :] = jnp.zeros((5, LANES), F32)
+        moved_ref[s, 3:8, :] = jnp.zeros((5, LANES), F32)
         force_ref[s, 3:4, :] = jnp.zeros((1, LANES), F32)
-        if s % PART == PART - 1:
-            send_out(answer_ref, answer_hbm, sems, s // PART).start()
-    for part in range(OWNERS // PART):
-        send_out(answer_ref, answer_hbm, sems, part).wait()
 
 
 def scatter_kernel(parcel_ref, force_ref, out_ref, total_ref):
@@ -301,8 +297,8 @@
             under.append((g * count + m, to * count + m if inside else g * count + (m ^ 1)))
     return (
         lax.ppermute(faces[0], "dom", far),
-        lax.ppermute(faces[1], ("group", "dom"), under),
-        lax.ppermute(faces[2], "group", over),
+        lax.ppermute(faces[1], "group", over),
+        lax.ppermute(faces[2], ("group", "dom"), under),
         lax.ppermute(faces[3], "dom", near),
     )
 
@@ -348,28 +344,27 @@
         in_specs=[pl.BlockSpec(memory_space=pltpu.HBM)] * len(kept),
     )(*kept)
     got = exchange(outs[:4])
-    whole = pl.BlockSpec(memory_space=pltpu.VMEM)
+    everything = pl.BlockSpec(memory_space=pltpu.VMEM)
     outside = pl.BlockSpec(memory_space=pl.ANY)
     parts = pltpu.SemaphoreType.DMA((OWNERS // PART,))
     place, sent = call(
         slot_kernel, (shape(CHUNKS, LANES, dtype=I32), shape(OWNERS, SENT, CAP)), 10**8,
         (pltpu.VMEM((OWNERS, SENT, CAP), F32), pltpu.VMEM((8, PARCELS), F32), parts),
-        out_specs=(whole, outside),
+        out_specs=(everything, outside),
     )(*outs[4:])
     got, sent = lax.optimization_barrier((got, sent))
     parcels = lax.all_to_all(sent, "dom", split_axis=0, concat_axis=0, tiled=True)
     residual, direction, *faces = call(
-        first_kernel, (field, field) + (face,) * 4, 10**8, halo + (faces_buffer,)
+        first_kernel, (field, field) + (face,) * 4, 10**8,
+        halo + (faces_buffer,),
     )(pressure_old, *got, source_term, diagonal, face_coeffs, neighbours, export_cells)
     got = exchange(faces)
-    iterate, table = call(second_kernel, (field, field), 10**8, halo)(
-        direction, *got, pressure_old, residual, diagonal, face_coeffs, neighbours
-    )
-    answer, force = call(
-        parcel_kernel, (shape(OWNERS, BACK, CAP), shape(OWNERS, 4, CAP)), 10**9,
-        (pltpu.VMEM((OWNERS, BACK, CAP), F32), parts),
-        out_specs=(outside, whole),
-    )(fluid_velocity, table, parcels)
+    moved, force = call(
+        fluid_kernel, (shape(OWNERS, 8, CAP), shape(OWNERS, 4, CAP)), 10**9
+    )(fluid_velocity, parcels)
+    iterate, answer = call(second_kernel, (field, shape(OWNERS, BACK, CAP)), 10**8, halo)(
+        direction, *got, pressure_old, residual, diagonal, face_coeffs, neighbours, parcels, moved
+    )
     returned = lax.all_to_all(answer, "dom", split_axis=0, concat_axis=0, tiled=True)
     momentum_source = call(
         scatter_kernel, shape(3, CELLS), 2 * 10**9, (pltpu.VMEM((6 * ROWS, LANES), F32),)

time: 54.8 us -> 51.2 us (0.934)
  the two profiles are of different devices: /device:TPU:1 before, /device:TPU:33 now
where the time goes in v6:
time: 51.2 us; the launch traced here: 50.8 us
  starting transfers between devices  26.1 us (51%)
  Pallas kernels  19.1 us (37%)
  waiting for transfers between devices  4.71 us (9%)
  between operations  0.86 us (2%)
    ppermute x2, starting transfers between devices, exchange(): lax.ppermute(faces[3], 'dom', near)  8.33 us
    ppermute x2, starting transfers between devices, exchange(): lax.ppermute(faces[2], ('group', 'dom'), under)  6.85 us
    all_to_all x1, waiting for transfers between devices, per_device(): lax.all_to_all(answer, 'dom', split_axis=0, concat_axis=0, tiled=True)  4.69 us
    pallas_call x1, Pallas kernels, per_device(): call(second_kernel, (field, shape(OWNERS, BACK, CAP)), 10 ** 8, halo)  4.29 us
    pallas_call x1, Pallas kernels, per_device(): call(scatter_kernel, shape(3, CELLS), 2 * 10 ** 9, (pltpu.VMEM((6 * ROWS,...  4.18 us
    all_to_all x1, starting transfers between devices, per_device(): lax.all_to_all(sent, 'dom', split_axis=0, concat_axis=0, tiled=True)  3.81 us
    all_to_all x1, starting transfers between devices, per_device(): lax.all_to_all(answer, 'dom', split_axis=0, concat_axis=0, tiled=True)  3.65 us
    pallas_call x1, Pallas kernels, per_device(): call(fluid_kernel, (shape(OWNERS, 8, CAP), shape(OWNERS, 4, CAP)), 10 ** 9)  3.48 us
  transfers between devices with their start and end apart: 10, of which 1 were waited for; matrix products, arithmetic and copies ran while one was open for 0% of the time, Pallas kernels for 24%

profile of v6, /device:TPU:33, one launch (start us, length us, event | category | flops | bytes accessed | tf_op | source)
XLA Modules:
  0.0 50.8 jit_solution(9425520097396873035)
XLA Ops:
  0.6 1.2 %shard_map.148 = (f32[8,128]{1,0:T(8,128)S(1)}, f32[8,128]{1,0:T(8,128)S(1)}, f32[8,128]{1,0:T(8,128)S(1)}, f32[8,128]{1,0:T(8,128)S(1)}, s32[8,128]{1,0:T(8,128...) custom-call(f32[32,128]{1,0:T(8,128)} %bitcast.6, ...), custom_call_target="tpu_custom_call" | custom-call | flops 1000000 | bytes 400000 | tf_op jit(solution)/shard_map/pallas_call | solution.py:336
  1.8 1.9 %collective-permute-start = (f32[8,128]{1,0:T(8,128)S(1)}, f32[8,128]{1,0:T(8,128)S(1)}, u32[]{:S(2)}, u32[]{:S(2)}) collective-permute-start(f32[8,128]{1,0:T(8,128)S(1)} %get-tuple-element.29), channel_id=1, source_target_pairs={{0,31},{1,2},{2,1},{3,4},{4,3},{5,6},{6,5},{7,8},{8,7},{9,10},{10,... | collective-permute-start | bytes 12296 | tf_op jit(solution)/shard_map/ppermute | solution.py:299
  3.7 0.0 collective-permute-start.1
  3.7 3.3 %collective-permute-start.2 = (f32[8,128]{1,0:T(8,128)S(1)}, f32[8,128]{1,0:T(8,128)S(1)}, u32[]{:S(2)}, u32[]{:S(2)}) collective-permute-start(f32[8,128]{1,0:T(8,128)S(1)} %get-tuple-element.31), channel_id=1, source_target_pairs={{0,1},{1,0},{2,3},{3,2},{4,5},{5,4},{6,7},{7,6},{8,9},{9,8},{10,11... | collective-permute-start | bytes 12296 | tf_op jit(solution)/shard_map/ppermute | solution.py:301
  7.0 4.1 %collective-permute-start.3 = (f32[8,128]{1,0:T(8,128)S(1)}, f32[8,128]{1,0:T(8,128)S(1)}, u32[]{:S(2)}, u32[]{:S(2)}) collective-permute-start(f32[8,128]{1,0:T(8,128)S(1)} %get-tuple-element.32), channel_id=1, source_target_pairs={{0,1},{1,0},{2,3},{3,2},{4,5},{5,4},{6,7},{7,6},{8,9},{9,8},{10,11... | collective-permute-start | bytes 12296 | tf_op jit(solution)/shard_map/ppermute | solution.py:302
  11.1 2.1 %shard_map.149 = (s32[8,128]{1,0:T(8,128)S(1)}, f32[32,24,128]{2,1,0:T(8,128)}) custom-call(s32[8,128]{1,0:T(8,128)S(1)} %get-tuple-element.33.owner_ref, s32[8,1024]{1,0:T(8,128)S(1)} %get-tuple-element.34.cells_ref, f32[8,1024]{1,0:T(8,128)S(1)} %get-tuple-element.35.weight_ref, f32[3,1024]{1,0:T(4,128)S(1)} %get-tuple-element.36.velocity_ref, ...), custom_call_target="tpu_custom_call" | custom-call | flops 100000000 | bytes 400000 | tf_op jit(solution)/shard_map/pallas_call | solution.py:350
  13.1 0.0 collective-permute-done.got0
  13.1 0.0 collective-permute-done.1.got1
  13.1 0.0 collective-permute-done.2.got2
  13.2 0.0 collective-permute-done.3.got3
  13.2 0.0 copy-start
  13.2 0.0 copy-start.1
  13.2 0.0 copy-start.3
  13.2 0.0 copy-start.4
  13.2 0.0 copy-start.5
  13.2 0.0 copy-start.7
  13.2 3.8 %all-to-all-start = ((f32[32,24,128]{2,1,0:T(8,128)}), f32[32,24,128]{2,1,0:T(8,128)S(1)}, u32[]{:S(2)}, u32[]{:S(2)}) async-start(f32[32,24,128]{2,1,0:T(8,128)} %get-tuple-element.49), calls=%async_computation | async-start | bytes 786432 | tf_op jit(solution)/shard_map/all_to_all | solution.py:356
  17.1 0.0 copy-done
  17.1 0.0 copy-done.1
  17.1 0.0 copy-done.3
  17.1 0.0 copy-done.4
  17.1 0.0 copy-done.5
  17.1 0.0 copy-done.7
  17.1 0.0 copy-start.6
  17.1 2.7 %shard_map.150 = (f32[32,128]{1,0:T(8,128)S(1)}, f32[32,128]{1,0:T(8,128)S(1)}, f32[8,128]{1,0:T(8,128)S(1)}, f32[8,128]{1,0:T(8,128)S(1)}, f32[8,128]{1,0:T(8,128)S(1)}, /*index=5*/f32[8,128]{1,0:T(8,128)S(1)}) custom-call(f32[32,128]{1,0:T(8,128)S(1)} %bitcast.7, f32[8,128]{1,0:T(8,128)S(1)} %collective-permute-done.got0, ...), custom_call_target="tpu_custom_call" | custom-call | flops 100000000 | bytes 400000 | tf_op jit(solution)/shard_map/pallas_call | solution.py:357
  19.8 1.6 %collective-permute-start.4 = (f32[8,128]{1,0:T(8,128)S(1)}, f32[8,128]{1,0:T(8,128)S(1)}, u32[]{:S(2)}, u32[]{:S(2)}) collective-permute-start(f32[8,128]{1,0:T(8,128)S(1)} %get-tuple-element.44), channel_id=1, source_target_pairs={{0,31},{1,2},{2,1},{3,4},{4,3},{5,6},{6,5},{7,8},{8,7},{9,10},{10,... | collective-permute-start | bytes 12296 | tf_op jit(solution)/shard_map/ppermute | solution.py:299
  21.4 0.0 collective-permute-start.5
  21.4 3.6 %collective-permute-start.6 = (f32[8,128]{1,0:T(8,128)S(1)}, f32[8,128]{1,0:T(8,128)S(1)}, u32[]{:S(2)}, u32[]{:S(2)}) collective-permute-start(f32[8,128]{1,0:T(8,128)S(1)} %get-tuple-element.46), channel_id=1, source_target_pairs={{0,1},{1,0},{2,3},{3,2},{4,5},{5,4},{6,7},{7,6},{8,9},{9,8},{10,11... | collective-permute-start | bytes 12296 | tf_op jit(solution)/shard_map/ppermute | solution.py:301
  25.0 4.2 %collective-permute-start.7 = (f32[8,128]{1,0:T(8,128)S(1)}, f32[8,128]{1,0:T(8,128)S(1)}, u32[]{:S(2)}, u32[]{:S(2)}) collective-permute-start(f32[8,128]{1,0:T(8,128)S(1)} %get-tuple-element.47), channel_id=1, source_target_pairs={{0,1},{1,0},{2,3},{3,2},{4,5},{5,4},{6,7},{7,6},{8,9},{9,8},{10,11... | collective-permute-start | bytes 12296 | tf_op jit(solution)/shard_map/ppermute | solution.py:302
  29.2 0.0 all-to-all-done.parcel_ref
  29.2 0.0 copy-done.6
  29.2 3.5 %shard_map.151 = (f32[32,8,128]{2,1,0:T(8,128)S(1)}, f32[32,4,128]{2,1,0:T(4,128)S(1)}) custom-call(f32[3,4096]{1,0:T(4,128)S(1)} %copy-done.6, f32[32,24,128]{2,1,0:T(8,128)S(1)} %all-to-all-done.parcel_ref), custom_call_target="tpu_custom_call" | custom-call | flops 1000000000 | bytes 400000 | tf_op jit(solution)/shard_map/pallas_call | solution.py:362
  32.7 0.0 collective-permute-done.4.got0
  32.7 0.0 collective-permute-done.5.got1
  32.7 0.0 collective-permute-done.6.got2
  32.8 0.0 collective-permute-done.7.got3
  32.8 4.3 %shard_map.152 = (f32[32,128]{1,0:T(8,128)}, f32[32,16,128]{2,1,0:T(8,128)}) custom-call(f32[32,128]{1,0:T(8,128)S(1)} %get-tuple-element.43.direction_ref, f32[8,128]{1,0:T(8,128)S(1)} %collective-permute-done.4.got0, f32[8,128]{1,0:T(8,128)S(1)} %collective-permute-done.5.got1, f32[8,128]{1,0:T(8,128)S(1)} %collective-permute-done.6.got2, ...), custom_call_target="tpu_custom_call" | custom-call | flops 100000000 | bytes 400000 | tf_op jit(solution)/shard_map/pallas_call | solution.py:365
  37.1 3.7 %all-to-all-start.1 = ((f32[32,16,128]{2,1,0:T(8,128)}), f32[32,16,128]{2,1,0:T(8,128)S(1)}, u32[]{:S(2)}, u32[]{:S(2)}) async-start(f32[32,16,128]{2,1,0:T(8,128)} %get-tuple-element.53), calls=%async_computation.1 | async-start | bytes 524288 | tf_op jit(solution)/shard_map/all_to_all | solution.py:368
  40.7 0.0 copy-start.2
  40.7 4.2 %shard_map.154 = f32[3,4096]{1,0:T(4,128)} custom-call(f32[32,24,128]{2,1,0:T(8,128)S(1)} %all-to-all-done.parcel_ref, f32[32,4,128]{2,1,0:T(4,128)S(1)} %get-tuple-element.54.force_ref), custom_call_target="tpu_custom_call" | custom-call | flops 2000000000 | bytes 400000 | tf_op jit(solution)/shard_map/pallas_call | solution.py:369
  44.9 4.7 %all-to-all-done.1.answer_ref = f32[32,16,128]{2,1,0:T(8,128)S(1)} async-done(((f32[32,16,128]{2,1,0:T(8,128)}), f32[32,16,128]{2,1,0:T(8,128)S(1)}, u32[]{:S(2)}, u32[]{:S(2)}) %all-to-all-start.1) | async-done | bytes 262176 | tf_op jit(solution)/shard_map/all_to_all | solution.py:368
  49.6 0.0 copy-done.2
  49.6 1.2 %shard_map.153 = f32[3,1024]{1,0:T(4,128)} custom-call(s32[8,128]{1,0:T(8,128)S(1)} %get-tuple-element.52.place_ref, f32[32,16,128]{2,1,0:T(8,128)S(1)} %all-to-all-done.1.answer_ref, f32[3,8,1024]{2,1,0:T(8,128)S(1)} %copy-done.2), custom_call_target="tpu_custom_call" | custom-call | flops 1000000 | bytes 400000 | tf_op jit(solution)/shard_map/pallas_call | solution.py:372
Async XLA Ops:
  1.8 11.3 %collective-permute-start = (f32[8,128]{1,0:T(8,128)S(1)}, f32[8,128]{1,0:T(8,128)S(1)}, u32[]{:S(2)}, u32[]{:S(2)}) collective-permute-start(f32[8,128]{1,0:T(8,128)S(1)} %get-tuple-element.29), channel_id=1, source_target_pairs={{0,31},{1,2},{2,1},{3,4},{4,3},{5,6},{6,5},{7,8},{8,7},{9,10},{10,... | collective-permute-start | bytes 12296 | tf_op jit(solution)/shard_map/ppermute | solution.py:299
  3.7 9.5 %collective-permute-start.1 = (f32[8,128]{1,0:T(8,128)S(1)}, f32[8,128]{1,0:T(8,128)S(1)}, u32[]{:S(2)}, u32[]{:S(2)}) collective-permute-start(f32[8,128]{1,0:T(8,128)S(1)} %get-tuple-element.30), channel_id=1, source_target_pairs={{0,32},{32,0},{64,96},{96,64},{128,160},{160,128},{192,224},{224,1... | collective-permute-start | bytes 12296 | tf_op jit(solution)/shard_map/ppermute | solution.py:300
  3.7 9.5 %collective-permute-start.2 = (f32[8,128]{1,0:T(8,128)S(1)}, f32[8,128]{1,0:T(8,128)S(1)}, u32[]{:S(2)}, u32[]{:S(2)}) collective-permute-start(f32[8,128]{1,0:T(8,128)S(1)} %get-tuple-element.31), channel_id=1, source_target_pairs={{0,1},{1,0},{2,3},{3,2},{4,5},{5,4},{6,7},{7,6},{8,9},{9,8},{10,11... | collective-permute-start | bytes 12296 | tf_op jit(solution)/shard_map/ppermute | solution.py:301
  7.0 6.2 %collective-permute-start.3 = (f32[8,128]{1,0:T(8,128)S(1)}, f32[8,128]{1,0:T(8,128)S(1)}, u32[]{:S(2)}, u32[]{:S(2)}) collective-permute-start(f32[8,128]{1,0:T(8,128)S(1)} %get-tuple-element.32), channel_id=1, source_target_pairs={{0,1},{1,0},{2,3},{3,2},{4,5},{5,4},{6,7},{7,6},{8,9},{9,8},{10,11... | collective-permute-start | bytes 12296 | tf_op jit(solution)/shard_map/ppermute | solution.py:302
  13.2 3.9 %copy-start = (f32[6,4096]{1,0:T(8,128)S(1)}, f32[6,4096]{1,0:T(8,128)}, u32[]{:S(2)}) copy-start(f32[6,4096]{1,0:T(8,128)} %coeff_ref.3) | copy-start | bytes 294916
  13.2 3.9 %copy-start.1 = (s32[6,4096]{1,0:T(8,128)S(1)}, s32[6,4096]{1,0:T(8,128)}, u32[]{:S(2)}) copy-start(s32[6,4096]{1,0:T(8,128)} %neighbour_ref.3) | copy-start | bytes 294916
  13.2 3.9 %copy-start.3 = (f32[4096]{0:T(1024)S(1)}, f32[4096]{0:T(1024)}, u32[]{:S(2)}) copy-start(f32[4096]{0:T(1024)} %param.13) | copy-start | bytes 49156
  13.2 3.9 %copy-start.4 = (s32[4,1024]{1,0:T(4,128)S(1)}, s32[4,1024]{1,0:T(4,128)}, u32[]{:S(2)}) copy-start(s32[4,1024]{1,0:T(4,128)} %export_ref.1) | copy-start | bytes 49156
  13.2 3.9 %copy-start.5 = (f32[4096]{0:T(1024)S(1)}, f32[4096]{0:T(1024)}, u32[]{:S(2)}) copy-start(f32[4096]{0:T(1024)} %param.15) | copy-start | bytes 49156
  13.2 3.9 %copy-start.7 = (f32[4096]{0:T(1024)S(1)}, f32[4096]{0:T(1024)}, u32[]{:S(2)}) copy-start(f32[4096]{0:T(1024)} %param.14) | copy-start | bytes 49156
  13.2 16.0 %all-to-all-start = ((f32[32,24,128]{2,1,0:T(8,128)}), f32[32,24,128]{2,1,0:T(8,128)S(1)}, u32[]{:S(2)}, u32[]{:S(2)}) async-start(f32[32,24,128]{2,1,0:T(8,128)} %get-tuple-element.49), calls=%async_computation | async-start | bytes 786432 | tf_op jit(solution)/shard_map/all_to_all | solution.py:356
  17.1 12.1 %copy-start.6 = (f32[3,4096]{1,0:T(4,128)S(1)}, f32[3,4096]{1,0:T(4,128)}, u32[]{:S(2)}) copy-start(f32[3,4096]{1,0:T(4,128)} %fluid_ref.1) | copy-start | bytes 147460
  19.8 12.9 %collective-permute-start.4 = (f32[8,128]{1,0:T(8,128)S(1)}, f32[8,128]{1,0:T(8,128)S(1)}, u32[]{:S(2)}, u32[]{:S(2)}) collective-permute-start(f32[8,128]{1,0:T(8,128)S(1)} %get-tuple-element.44), channel_id=1, source_target_pairs={{0,31},{1,2},{2,1},{3,4},{4,3},{5,6},{6,5},{7,8},{8,7},{9,10},{10,... | collective-permute-start | bytes 12296 | tf_op jit(solution)/shard_map/ppermute | solution.py:299
  21.4 11.3 %collective-permute-start.5 = (f32[8,128]{1,0:T(8,128)S(1)}, f32[8,128]{1,0:T(8,128)S(1)}, u32[]{:S(2)}, u32[]{:S(2)}) collective-permute-start(f32[8,128]{1,0:T(8,128)S(1)} %get-tuple-element.45), channel_id=1, source_target_pairs={{0,32},{32,0},{64,96},{96,64},{128,160},{160,128},{192,224},{224,1... | collective-permute-start | bytes 12296 | tf_op jit(solution)/shard_map/ppermute | solution.py:300
  21.4 11.3 %collective-permute-start.6 = (f32[8,128]{1,0:T(8,128)S(1)}, f32[8,128]{1,0:T(8,128)S(1)}, u32[]{:S(2)}, u32[]{:S(2)}) collective-permute-start(f32[8,128]{1,0:T(8,128)S(1)} %get-tuple-element.46), channel_id=1, source_target_pairs={{0,1},{1,0},{2,3},{3,2},{4,5},{5,4},{6,7},{7,6},{8,9},{9,8},{10,11... | collective-permute-start | bytes 12296 | tf_op jit(solution)/shard_map/ppermute | solution.py:301
  25.0 7.7 %collective-permute-start.7 = (f32[8,128]{1,0:T(8,128)S(1)}, f32[8,128]{1,0:T(8,128)S(1)}, u32[]{:S(2)}, u32[]{:S(2)}) collective-permute-start(f32[8,128]{1,0:T(8,128)S(1)} %get-tuple-element.47), channel_id=1, source_target_pairs={{0,1},{1,0},{2,3},{3,2},{4,5},{5,4},{6,7},{7,6},{8,9},{9,8},{10,11... | collective-permute-start | bytes 12296 | tf_op jit(solution)/shard_map/ppermute | solution.py:302
  37.1 12.5 %all-to-all-start.1 = ((f32[32,16,128]{2,1,0:T(8,128)}), f32[32,16,128]{2,1,0:T(8,128)S(1)}, u32[]{:S(2)}, u32[]{:S(2)}) async-start(f32[32,16,128]{2,1,0:T(8,128)} %get-tuple-element.53), calls=%async_computation.1 | async-start | bytes 524288 | tf_op jit(solution)/shard_map/all_to_all | solution.py:368
  40.7 8.9 %copy-start.2 = (f32[3,8,1024]{2,1,0:T(8,128)S(1)}, f32[3,8,1024]{2,1,0:T(8,128)}, u32[]{:S(2)}) copy-start(f32[3,8,1024]{2,1,0:T(8,128)} %grad_ref.1) | copy-start | bytes 294916

commit v7 on v6

--- a/solution.py
+++ b/solution.py
@@ -25,7 +25,6 @@
 CAP = 128
 SENT = 24
 BACK = 16
-PART = 8
 
 F32 = jnp.float32
 BF16 = jnp.bfloat16
@@ -146,14 +145,9 @@
         answer_ref[s, 8:16, :] = moved_ref[s]
 
 
-def send_out(local_ref, hbm_ref, sems, part):
-    block = pl.ds(part * PART, PART)
-    return pltpu.make_async_copy(local_ref.at[block], hbm_ref.at[block], sems.at[part])
-
-
 def slot_kernel(
-    owner_ref, cells_ref, weight_ref, velocity_ref, rate_ref, place_ref, sent_hbm, sent_ref,
-    state_ref, sems,
+    owner_ref, cells_ref, weight_ref, velocity_ref, rate_ref, place_ref, sent_ref,
+    state_ref,
 ):
     owners = lax.broadcasted_iota(I32, (OWNERS, LANES), 0)
     lanes = lax.broadcasted_iota(I32, (OWNERS, LANES), 1)
@@ -204,10 +198,6 @@
         sent_ref[o, 0:8, :] = place(weight_ref)
         sent_ref[o, 8:16, :] = place(cells_ref)
         sent_ref[o, 16:24, :] = place(state_ref)
-        if o % PART == PART - 1:
-            send_out(sent_ref, sent_hbm, sems, o // PART).start()
-    for part in range(OWNERS // PART):
-        send_out(sent_ref, sent_hbm, sems, part).wait()
 
 
 def fluid_kernel(fluid_ref, parcel_ref, moved_ref, force_ref):
@@ -344,13 +334,9 @@
         in_specs=[pl.BlockSpec(memory_space=pltpu.HBM)] * len(kept),
     )(*kept)
     got = exchange(outs[:4])
-    everything = pl.BlockSpec(memory_space=pltpu.VMEM)
-    outside = pl.BlockSpec(memory_space=pl.ANY)
-    parts = pltpu.SemaphoreType.DMA((OWNERS // PART,))
     place, sent = call(
         slot_kernel, (shape(CHUNKS, LANES, dtype=I32), shape(OWNERS, SENT, CAP)), 10**8,
-        (pltpu.VMEM((OWNERS, SENT, CAP), F32), pltpu.VMEM((8, PARCELS), F32), parts),
-        out_specs=(everything, outside),
+        (pltpu.VMEM((8, PARCELS), F32),),
     )(*outs[4:])
     got, sent = lax.optimization_barrier((got, sent))
     parcels = lax.all_to_all(sent, "dom", split_axis=0, concat_axis=0, tiled=True)

time: 51.2 us -> 51.3 us (level)
  transfers between devices with their start and end apart: 10 -> 10, of which waited for: 1 -> 1; matrix products, arithmetic and copies ran while one was open for 0% -> 0% of each run, Pallas kernels for 24% -> 25%
where the time goes in v7:
time: 51.3 us; the launch traced here: 50.9 us
  starting transfers between devices  26.1 us (51%)
  Pallas kernels  19.2 us (37%)
  waiting for transfers between devices  4.71 us (9%)
  between operations  0.83 us (2%)
    ppermute x2, starting transfers between devices, exchange(): lax.ppermute(faces[3], 'dom', near)  8.33 us
    ppermute x2, starting transfers between devices, exchange(): lax.ppermute(faces[2], ('group', 'dom'), under)  6.85 us
    all_to_all x1, waiting for transfers between devices, per_device(): lax.all_to_all(answer, 'dom', split_axis=0, concat_axis=0, tiled=True)  4.69 us
    pallas_call x1, Pallas kernels, per_device(): call(second_kernel, (field, shape(OWNERS, BACK, CAP)), 10 ** 8, halo)  4.29 us
    pallas_call x1, Pallas kernels, per_device(): call(scatter_kernel, shape(3, CELLS), 2 * 10 ** 9, (pltpu.VMEM((6 * ROWS,...  4.18 us
    all_to_all x1, starting transfers between devices, per_device(): lax.all_to_all(sent, 'dom', split_axis=0, concat_axis=0, tiled=True)  3.81 us
    all_to_all x1, starting transfers between devices, per_device(): lax.all_to_all(answer, 'dom', split_axis=0, concat_axis=0, tiled=True)  3.65 us
    pallas_call x1, Pallas kernels, per_device(): call(fluid_kernel, (shape(OWNERS, 8, CAP), shape(OWNERS, 4, CAP)), 10 ** 9)  3.48 us
  transfers between devices with their start and end apart: 10, of which 1 were waited for; matrix products, arithmetic and copies ran while one was open for 0% of the time, Pallas kernels for 25%

profile of v7, /device:TPU:33, one launch (start us, length us, event | category | flops | bytes accessed | tf_op | source)
XLA Modules:
  0.0 50.9 jit_solution(15973019071476398114)
XLA Ops:
  0.6 1.2 %shard_map.148 = (f32[8,128]{1,0:T(8,128)S(1)}, f32[8,128]{1,0:T(8,128)S(1)}, f32[8,128]{1,0:T(8,128)S(1)}, f32[8,128]{1,0:T(8,128)S(1)}, s32[8,128]{1,0:T(8,128...) custom-call(f32[32,128]{1,0:T(8,128)} %bitcast.6, ...), custom_call_target="tpu_custom_call" | custom-call | flops 1000000 | bytes 400000 | tf_op jit(solution)/shard_map/pallas_call | solution.py:326
  1.8 1.9 %collective-permute-start = (f32[8,128]{1,0:T(8,128)S(1)}, f32[8,128]{1,0:T(8,128)S(1)}, u32[]{:S(2)}, u32[]{:S(2)}) collective-permute-start(f32[8,128]{1,0:T(8,128)S(1)} %get-tuple-element.29), channel_id=1, source_target_pairs={{0,31},{1,2},{2,1},{3,4},{4,3},{5,6},{6,5},{7,8},{8,7},{9,10},{10,... | collective-permute-start | bytes 12296 | tf_op jit(solution)/shard_map/ppermute | solution.py:289
  3.7 0.0 collective-permute-start.1
  3.7 3.3 %collective-permute-start.2 = (f32[8,128]{1,0:T(8,128)S(1)}, f32[8,128]{1,0:T(8,128)S(1)}, u32[]{:S(2)}, u32[]{:S(2)}) collective-permute-start(f32[8,128]{1,0:T(8,128)S(1)} %get-tuple-element.31), channel_id=1, source_target_pairs={{0,1},{1,0},{2,3},{3,2},{4,5},{5,4},{6,7},{7,6},{8,9},{9,8},{10,11... | collective-permute-start | bytes 12296 | tf_op jit(solution)/shard_map/ppermute | solution.py:291
  7.0 4.1 %collective-permute-start.3 = (f32[8,128]{1,0:T(8,128)S(1)}, f32[8,128]{1,0:T(8,128)S(1)}, u32[]{:S(2)}, u32[]{:S(2)}) collective-permute-start(f32[8,128]{1,0:T(8,128)S(1)} %get-tuple-element.32), channel_id=1, source_target_pairs={{0,1},{1,0},{2,3},{3,2},{4,5},{5,4},{6,7},{7,6},{8,9},{9,8},{10,11... | collective-permute-start | bytes 12296 | tf_op jit(solution)/shard_map/ppermute | solution.py:292
  11.1 2.1 %shard_map.149 = (s32[8,128]{1,0:T(8,128)S(1)}, f32[32,24,128]{2,1,0:T(8,128)}) custom-call(s32[8,128]{1,0:T(8,128)S(1)} %get-tuple-element.33.owner_ref, s32[8,1024]{1,0:T(8,128)S(1)} %get-tuple-element.34.cells_ref, f32[8,1024]{1,0:T(8,128)S(1)} %get-tuple-element.35.weight_ref, f32[3,1024]{1,0:T(4,128)S(1)} %get-tuple-element.36.velocity_ref, ...), custom_call_target="tpu_custom_call" | custom-call | flops 100000000 | bytes 400000 | tf_op jit(solution)/shard_map/pallas_call | solution.py:337
  13.2 0.0 collective-permute-done.got0
  13.2 0.0 collective-permute-done.1.got1
  13.2 0.0 collective-permute-done.2.got2
  13.2 0.0 collective-permute-done.3.got3
  13.2 0.0 copy-start
  13.2 0.0 copy-start.1
  13.2 0.0 copy-start.3
  13.3 0.0 copy-start.4
  13.3 0.0 copy-start.5
  13.3 0.0 copy-start.7
  13.3 3.8 %all-to-all-start = ((f32[32,24,128]{2,1,0:T(8,128)}), f32[32,24,128]{2,1,0:T(8,128)S(1)}, u32[]{:S(2)}, u32[]{:S(2)}) async-start(f32[32,24,128]{2,1,0:T(8,128)} %get-tuple-element.49), calls=%async_computation | async-start | bytes 786432 | tf_op jit(solution)/shard_map/all_to_all | solution.py:342
  17.1 0.0 copy-done
  17.1 0.0 copy-done.1
  17.1 0.0 copy-done.3
  17.1 0.0 copy-done.4
  17.1 0.0 copy-done.5
  17.2 0.0 copy-done.7
  17.2 0.0 copy-start.6
  17.2 2.7 %shard_map.150 = (f32[32,128]{1,0:T(8,128)S(1)}, f32[32,128]{1,0:T(8,128)S(1)}, f32[8,128]{1,0:T(8,128)S(1)}, f32[8,128]{1,0:T(8,128)S(1)}, f32[8,128]{1,0:T(8,128)S(1)}, /*index=5*/f32[8,128]{1,0:T(8,128)S(1)}) custom-call(f32[32,128]{1,0:T(8,128)S(1)} %bitcast.7, f32[8,128]{1,0:T(8,128)S(1)} %collective-permute-done.got0, ...), custom_call_target="tpu_custom_call" | custom-call | flops 100000000 | bytes 400000 | tf_op jit(solution)/shard_map/pallas_call | solution.py:343
  19.9 1.6 %collective-permute-start.4 = (f32[8,128]{1,0:T(8,128)S(1)}, f32[8,128]{1,0:T(8,128)S(1)}, u32[]{:S(2)}, u32[]{:S(2)}) collective-permute-start(f32[8,128]{1,0:T(8,128)S(1)} %get-tuple-element.44), channel_id=1, source_target_pairs={{0,31},{1,2},{2,1},{3,4},{4,3},{5,6},{6,5},{7,8},{8,7},{9,10},{10,... | collective-permute-start | bytes 12296 | tf_op jit(solution)/shard_map/ppermute | solution.py:289
  21.5 0.0 collective-permute-start.5
  21.5 3.6 %collective-permute-start.6 = (f32[8,128]{1,0:T(8,128)S(1)}, f32[8,128]{1,0:T(8,128)S(1)}, u32[]{:S(2)}, u32[]{:S(2)}) collective-permute-start(f32[8,128]{1,0:T(8,128)S(1)} %get-tuple-element.46), channel_id=1, source_target_pairs={{0,1},{1,0},{2,3},{3,2},{4,5},{5,4},{6,7},{7,6},{8,9},{9,8},{10,11... | collective-permute-start | bytes 12296 | tf_op jit(solution)/shard_map/ppermute | solution.py:291
  25.1 4.2 %collective-permute-start.7 = (f32[8,128]{1,0:T(8,128)S(1)}, f32[8,128]{1,0:T(8,128)S(1)}, u32[]{:S(2)}, u32[]{:S(2)}) collective-permute-start(f32[8,128]{1,0:T(8,128)S(1)} %get-tuple-element.47), channel_id=1, source_target_pairs={{0,1},{1,0},{2,3},{3,2},{4,5},{5,4},{6,7},{7,6},{8,9},{9,8},{10,11... | collective-permute-start | bytes 12296 | tf_op jit(solution)/shard_map/ppermute | solution.py:292
  29.3 0.0 all-to-all-done.parcel_ref
  29.3 0.0 copy-done.6
  29.3 3.5 %shard_map.151 = (f32[32,8,128]{2,1,0:T(8,128)S(1)}, f32[32,4,128]{2,1,0:T(4,128)S(1)}) custom-call(f32[3,4096]{1,0:T(4,128)S(1)} %copy-done.6, f32[32,24,128]{2,1,0:T(8,128)S(1)} %all-to-all-done.parcel_ref), custom_call_target="tpu_custom_call" | custom-call | flops 1000000000 | bytes 400000 | tf_op jit(solution)/shard_map/pallas_call | solution.py:348
  32.8 0.0 collective-permute-done.4.got0
  32.8 0.0 collective-permute-done.5.got1
  32.8 0.0 collective-permute-done.6.got2
  32.8 0.0 collective-permute-done.7.got3
  32.8 4.3 %shard_map.152 = (f32[32,128]{1,0:T(8,128)}, f32[32,16,128]{2,1,0:T(8,128)}) custom-call(f32[32,128]{1,0:T(8,128)S(1)} %get-tuple-element.43.direction_ref, f32[8,128]{1,0:T(8,128)S(1)} %collective-permute-done.4.got0, f32[8,128]{1,0:T(8,128)S(1)} %collective-permute-done.5.got1, f32[8,128]{1,0:T(8,128)S(1)} %collective-permute-done.6.got2, ...), custom_call_target="tpu_custom_call" | custom-call | flops 100000000 | bytes 400000 | tf_op jit(solution)/shard_map/pallas_call | solution.py:351
  37.1 3.7 %all-to-all-start.1 = ((f32[32,16,128]{2,1,0:T(8,128)}), f32[32,16,128]{2,1,0:T(8,128)S(1)}, u32[]{:S(2)}, u32[]{:S(2)}) async-start(f32[32,16,128]{2,1,0:T(8,128)} %get-tuple-element.53), calls=%async_computation.1 | async-start | bytes 524288 | tf_op jit(solution)/shard_map/all_to_all | solution.py:354
  40.8 0.0 copy-start.2
  40.8 4.2 %shard_map.154 = f32[3,4096]{1,0:T(4,128)} custom-call(f32[32,24,128]{2,1,0:T(8,128)S(1)} %all-to-all-done.parcel_ref, f32[32,4,128]{2,1,0:T(4,128)S(1)} %get-tuple-element.54.force_ref), custom_call_target="tpu_custom_call" | custom-call | flops 2000000000 | bytes 400000 | tf_op jit(solution)/shard_map/pallas_call | solution.py:355
  45.0 4.7 %all-to-all-done.1.answer_ref = f32[32,16,128]{2,1,0:T(8,128)S(1)} async-done(((f32[32,16,128]{2,1,0:T(8,128)}), f32[32,16,128]{2,1,0:T(8,128)S(1)}, u32[]{:S(2)}, u32[]{:S(2)}) %all-to-all-start.1) | async-done | bytes 262176 | tf_op jit(solution)/shard_map/all_to_all | solution.py:354
  49.7 0.0 copy-done.2
  49.7 1.2 %shard_map.153 = f32[3,1024]{1,0:T(4,128)} custom-call(s32[8,128]{1,0:T(8,128)S(1)} %get-tuple-element.52.place_ref, f32[32,16,128]{2,1,0:T(8,128)S(1)} %all-to-all-done.1.answer_ref, f32[3,8,1024]{2,1,0:T(8,128)S(1)} %copy-done.2), custom_call_target="tpu_custom_call" | custom-call | flops 1000000 | bytes 400000 | tf_op jit(solution)/shard_map/pallas_call | solution.py:358
Async XLA Ops:
  1.8 11.4 %collective-permute-start = (f32[8,128]{1,0:T(8,128)S(1)}, f32[8,128]{1,0:T(8,128)S(1)}, u32[]{:S(2)}, u32[]{:S(2)}) collective-permute-start(f32[8,128]{1,0:T(8,128)S(1)} %get-tuple-element.29), channel_id=1, source_target_pairs={{0,31},{1,2},{2,1},{3,4},{4,3},{5,6},{6,5},{7,8},{8,7},{9,10},{10,... | collective-permute-start | bytes 12296 | tf_op jit(solution)/shard_map/ppermute | solution.py:289
  3.7 9.5 %collective-permute-start.1 = (f32[8,128]{1,0:T(8,128)S(1)}, f32[8,128]{1,0:T(8,128)S(1)}, u32[]{:S(2)}, u32[]{:S(2)}) collective-permute-start(f32[8,128]{1,0:T(8,128)S(1)} %get-tuple-element.30), channel_id=1, source_target_pairs={{0,32},{32,0},{64,96},{96,64},{128,160},{160,128},{192,224},{224,1... | collective-permute-start | bytes 12296 | tf_op jit(solution)/shard_map/ppermute | solution.py:290
  3.7 9.5 %collective-permute-start.2 = (f32[8,128]{1,0:T(8,128)S(1)}, f32[8,128]{1,0:T(8,128)S(1)}, u32[]{:S(2)}, u32[]{:S(2)}) collective-permute-start(f32[8,128]{1,0:T(8,128)S(1)} %get-tuple-element.31), channel_id=1, source_target_pairs={{0,1},{1,0},{2,3},{3,2},{4,5},{5,4},{6,7},{7,6},{8,9},{9,8},{10,11... | collective-permute-start | bytes 12296 | tf_op jit(solution)/shard_map/ppermute | solution.py:291
  7.0 6.3 %collective-permute-start.3 = (f32[8,128]{1,0:T(8,128)S(1)}, f32[8,128]{1,0:T(8,128)S(1)}, u32[]{:S(2)}, u32[]{:S(2)}) collective-permute-start(f32[8,128]{1,0:T(8,128)S(1)} %get-tuple-element.32), channel_id=1, source_target_pairs={{0,1},{1,0},{2,3},{3,2},{4,5},{5,4},{6,7},{7,6},{8,9},{9,8},{10,11... | collective-permute-start | bytes 12296 | tf_op jit(solution)/shard_map/ppermute | solution.py:292
  13.2 3.9 %copy-start = (f32[6,4096]{1,0:T(8,128)S(1)}, f32[6,4096]{1,0:T(8,128)}, u32[]{:S(2)}) copy-start(f32[6,4096]{1,0:T(8,128)} %coeff_ref.3) | copy-start | bytes 294916
  13.2 3.9 %copy-start.1 = (s32[6,4096]{1,0:T(8,128)S(1)}, s32[6,4096]{1,0:T(8,128)}, u32[]{:S(2)}) copy-start(s32[6,4096]{1,0:T(8,128)} %neighbour_ref.3) | copy-start | bytes 294916
  13.2 3.9 %copy-start.3 = (f32[4096]{0:T(1024)S(1)}, f32[4096]{0:T(1024)}, u32[]{:S(2)}) copy-start(f32[4096]{0:T(1024)} %param.13) | copy-start | bytes 49156
  13.3 3.9 %copy-start.4 = (s32[4,1024]{1,0:T(4,128)S(1)}, s32[4,1024]{1,0:T(4,128)}, u32[]{:S(2)}) copy-start(s32[4,1024]{1,0:T(4,128)} %export_ref.1) | copy-start | bytes 49156
  13.3 3.9 %copy-start.5 = (f32[4096]{0:T(1024)S(1)}, f32[4096]{0:T(1024)}, u32[]{:S(2)}) copy-start(f32[4096]{0:T(1024)} %param.15) | copy-start | bytes 49156
  13.3 3.9 %copy-start.7 = (f32[4096]{0:T(1024)S(1)}, f32[4096]{0:T(1024)}, u32[]{:S(2)}) copy-start(f32[4096]{0:T(1024)} %param.14) | copy-start | bytes 49156
  13.3 16.0 %all-to-all-start = ((f32[32,24,128]{2,1,0:T(8,128)}), f32[32,24,128]{2,1,0:T(8,128)S(1)}, u32[]{:S(2)}, u32[]{:S(2)}) async-start(f32[32,24,128]{2,1,0:T(8,128)} %get-tuple-element.49), calls=%async_computation | async-start | bytes 786432 | tf_op jit(solution)/shard_map/all_to_all | solution.py:342
  17.2 12.1 %copy-start.6 = (f32[3,4096]{1,0:T(4,128)S(1)}, f32[3,4096]{1,0:T(4,128)}, u32[]{:S(2)}) copy-start(f32[3,4096]{1,0:T(4,128)} %fluid_ref.1) | copy-start | bytes 147460
  19.9 12.9 %collective-permute-start.4 = (f32[8,128]{1,0:T(8,128)S(1)}, f32[8,128]{1,0:T(8,128)S(1)}, u32[]{:S(2)}, u32[]{:S(2)}) collective-permute-start(f32[8,128]{1,0:T(8,128)S(1)} %get-tuple-element.44), channel_id=1, source_target_pairs={{0,31},{1,2},{2,1},{3,4},{4,3},{5,6},{6,5},{7,8},{8,7},{9,10},{10,... | collective-permute-start | bytes 12296 | tf_op jit(solution)/shard_map/ppermute | solution.py:289
  21.5 11.3 %collective-permute-start.5 = (f32[8,128]{1,0:T(8,128)S(1)}, f32[8,128]{1,0:T(8,128)S(1)}, u32[]{:S(2)}, u32[]{:S(2)}) collective-permute-start(f32[8,128]{1,0:T(8,128)S(1)} %get-tuple-element.45), channel_id=1, source_target_pairs={{0,32},{32,0},{64,96},{96,64},{128,160},{160,128},{192,224},{224,1... | collective-permute-start | bytes 12296 | tf_op jit(solution)/shard_map/ppermute | solution.py:290
  21.5 11.3 %collective-permute-start.6 = (f32[8,128]{1,0:T(8,128)S(1)}, f32[8,128]{1,0:T(8,128)S(1)}, u32[]{:S(2)}, u32[]{:S(2)}) collective-permute-start(f32[8,128]{1,0:T(8,128)S(1)} %get-tuple-element.46), channel_id=1, source_target_pairs={{0,1},{1,0},{2,3},{3,2},{4,5},{5,4},{6,7},{7,6},{8,9},{9,8},{10,11... | collective-permute-start | bytes 12296 | tf_op jit(solution)/shard_map/ppermute | solution.py:291
  25.1 7.7 %collective-permute-start.7 = (f32[8,128]{1,0:T(8,128)S(1)}, f32[8,128]{1,0:T(8,128)S(1)}, u32[]{:S(2)}, u32[]{:S(2)}) collective-permute-start(f32[8,128]{1,0:T(8,128)S(1)} %get-tuple-element.47), channel_id=1, source_target_pairs={{0,1},{1,0},{2,3},{3,2},{4,5},{5,4},{6,7},{7,6},{8,9},{9,8},{10,11... | collective-permute-start | bytes 12296 | tf_op jit(solution)/shard_map/ppermute | solution.py:292
  37.1 12.5 %all-to-all-start.1 = ((f32[32,16,128]{2,1,0:T(8,128)}), f32[32,16,128]{2,1,0:T(8,128)S(1)}, u32[]{:S(2)}, u32[]{:S(2)}) async-start(f32[32,16,128]{2,1,0:T(8,128)} %get-tuple-element.53), calls=%async_computation.1 | async-start | bytes 524288 | tf_op jit(solution)/shard_map/all_to_all | solution.py:354
  40.8 8.9 %copy-start.2 = (f32[3,8,1024]{2,1,0:T(8,128)S(1)}, f32[3,8,1024]{2,1,0:T(8,128)}, u32[]{:S(2)}) copy-start(f32[3,8,1024]{2,1,0:T(8,128)} %grad_ref.1) | copy-start | bytes 294916
